TPU v7x, 32 devices: a whole 2x2x4 slice. The times are simulated.
32 devices in a mesh: ctx: 8 (over z, x), req: 4 (over y, core).
Axes of the slice: x: 2, y: 2, z: 4, core: 2. Of those that a mesh axis runs over, the one named last changes fastest.
Arguments:
- latents: bfloat16 [16, 16384, 576], P('req', 'ctx'), may hold values from -6 to 6
- index_keys: bfloat16 [16, 16384, 128], P('req', 'ctx'), may hold values from -6 to 6
- queries: bfloat16 [4, 16, 128, 576], P(None, 'req', 'ctx'), may hold values from -72 to 72
- index_queries: bfloat16 [4, 16, 64, 128], P(None, 'req', 'ctx'), may hold values from -0.5 to 0.5
- index_weights: bfloat16 [4, 16, 64], P(None, 'req', 'ctx'), may hold values from -1.5 to 1.5
- value_up_weight: bfloat16 [128, 512, 128], P('ctx', 'req'), may hold values from -0.75 to 0.75
- selection: int32 [4, 16, 32], P(None, 'req'), may hold values from 0 to 255, as said below
- counts: int32 [4, 16], P(None, 'req'), may hold values from 21 to 32, as said below
- lengths: int32 [16], P('req'), may hold values from 8192 to 16380, as said below
Outputs:
- head_values: bfloat16 [4, 16, 128, 128], P(None, 'req', 'ctx')
- index_scores: float32 [4, 16, 16384], P(None, 'req', 'ctx')
Inputs may be any that keep to these rules, and one draw needn't show every extreme that they name: Context lengths; every step's query position lengths[r] + s lies in the context. `selection`: the first counts[s, r] slots name different blocks, each holding a live position of that step; every list holds the block of the step's own position and at least one block whose positions are all live; later slots hold 0. Of the blocks that one device's context shard holds, at most 8 are named in one list. `counts`: live slots of a list.
All inputs are finite; a program needn't handle non-finite values.
Results may differ from a plain program's by a relative error of at most 0.018.
Values may be sent and summed in bfloat16 or wider, within the bound.
No kernel may reach another device: no remote copies, remote signals or barrier semaphores. Data moves between devices by JAX's collectives and lax.ppermute only.
A program may use at most 128 MiB of HBM per device.

v0:
```python
import jax
import jax.numpy as jnp
from jax import lax
from jax.sharding import PartitionSpec as P

KV = 512
QK_DIM = 192
BLOCK = 64


def compact_slots(owned_slot, local_block, capacity):
    ranking = jnp.cumsum(owned_slot.astype(jnp.int32), axis=-1) - 1
    places = jnp.arange(capacity, dtype=jnp.int32)
    chosen = (owned_slot[..., None, :] & (ranking[..., None, :] == places[:, None])).astype(
        jnp.int32
    )
    block_index = jnp.sum(chosen * local_block[..., None, :], axis=-1)
    filled = jnp.sum(chosen, axis=-1) > 0
    return (block_index, filled)


def per_device(
    latents,
    index_keys,
    queries,
    index_queries,
    index_weights,
    value_up_weight,
    selection,
    counts,
    lengths,
):
    own_shard = lax.axis_index("ctx")
    step_count, request_count, slot_count = selection.shape
    half_axis = lax.axis_size("ctx") // 2
    capacity = max(2, (slot_count - 2) // half_axis + 1)
    context_dev = latents.shape[1]
    row_width = latents.shape[2]
    blocks_dev = context_dev // BLOCK
    score_scale = QK_DIM ** (-0.5)
    all_query, all_index_query, all_index_weight = (
        lax.all_gather(queries, "ctx", axis=2, tiled=True),
        lax.all_gather(index_queries, "ctx", axis=2, tiled=True),
        lax.all_gather(index_weights, "ctx", axis=2, tiled=True),
    )
    step_ids = jnp.arange(step_count, dtype=jnp.int32)
    limits = lengths[None, :] + step_ids[:, None]
    token_pos = own_shard * context_dev + jnp.arange(context_dev, dtype=jnp.int32)
    products = jnp.einsum(
        "srhd,rcd->srhc", all_index_query, index_keys, preferred_element_type=jnp.float32
    )
    weighted = jnp.einsum(
        "srhc,srh->src", jnp.maximum(products, 0.0), all_index_weight.astype(jnp.float32)
    )
    index_scores = jnp.where(token_pos[None, None, :] <= limits[:, :, None], weighted, 0.0)
    local_block = selection - own_shard * blocks_dev
    slot_ids = jnp.arange(slot_count, dtype=jnp.int32)
    owned_slot = (
        (local_block >= 0)
        & (local_block < blocks_dev)
        & (slot_ids[None, None, :] < counts[:, :, None])
    )
    block_index, filled = compact_slots(owned_slot, local_block, capacity)
    block_tiles = latents.reshape(request_count, blocks_dev, BLOCK, row_width)
    request_numbers = jnp.arange(request_count, dtype=jnp.int32)[None, :, None]
    gathered = block_tiles[request_numbers, block_index].reshape(
        step_count, request_count, capacity * BLOCK, row_width
    )
    positions = (block_index + own_shard * blocks_dev)[..., None] * BLOCK + jnp.arange(
        BLOCK, dtype=jnp.int32
    )
    usable = filled[..., None] & (positions <= limits[:, :, None, None])
    usable = usable.reshape(step_count, request_count, 1, capacity * BLOCK)
    scores = (
        jnp.einsum("srhl,srtl->srht", all_query, gathered, preferred_element_type=jnp.float32)
        * score_scale
    )
    scores = jnp.where(usable, scores, -1e30)
    peak_score = jnp.max(scores, axis=-1)
    exp_weights = jnp.where(usable, jnp.exp(scores - peak_score[..., None]), 0.0)
    row_total = jnp.sum(exp_weights, axis=-1)
    mixed_rows = jnp.einsum(
        "srht,srtk->srhk",
        exp_weights.astype(jnp.bfloat16),
        gathered[..., :KV],
        preferred_element_type=jnp.float32,
    )
    global_peak = lax.pmax(peak_score, "ctx")
    shrink = jnp.exp(peak_score - global_peak)
    share_total, mixed_share = (
        lax.psum_scatter(
            (row_total * shrink).astype(jnp.bfloat16), "ctx", scatter_dimension=2, tiled=True
        ).astype(jnp.float32),
        lax.psum_scatter(
            (mixed_rows * shrink[..., None]).astype(jnp.bfloat16),
            "ctx",
            scatter_dimension=2,
            tiled=True,
        ).astype(jnp.float32),
    )
    attended_output = (mixed_share / share_total[..., None]).astype(jnp.bfloat16)
    complete_up_matrix = lax.all_gather(value_up_weight, "req", axis=1, tiled=True)
    lifted_values = jnp.einsum(
        "xefy,fym->xefm", attended_output, complete_up_matrix, preferred_element_type=jnp.float32
    )
    head_values = lifted_values.astype(jnp.bfloat16)
    return (head_values, index_scores)


def solution(mesh):
    placed = (
        P("req", "ctx", None),
        P("req", "ctx", None),
        P(None, "req", "ctx", None),
        P(None, "req", "ctx", None),
        P(None, "req", "ctx"),
        P("ctx", "req", None),
        P(None, "req", None),
        P(None, "req"),
        P("req"),
    )
    return jax.shard_map(
        per_device,
        mesh=mesh,
        in_specs=placed,
        out_specs=(P(None, "req", "ctx", None), P(None, "req", "ctx")),
        check_vma=False,
    )
```

profile of v0, /device:TPU:0, one launch (start us, length us, event | category | flops | bytes accessed | tf_op | source)
XLA Modules:
  0.0 268.9 jit_solution(4355776819441778309)
XLA Ops:
  8.1 0.7 all-gather.3.cloned.1.call-update
  8.8 0.8 fusion.42
  9.6 0.8 reduce_window_sum.11
  10.4 0.6 convert_reduce_fusion
  11.7 14.2 %copy.27 = bf16[4,2048,576]{2,1,0:T(8,128)(2,1)} copy(bf16[4,2048,576]{1,2,0:T(8,128)(2,1)} %param.9) | data formatting | bytes 18874368 | tf_op args[0]
  25.8 12.3 %gather_fusion = bf16[128,64,576]{2,1,0:T(8,128)(2,1)} fusion(bf16[4,32,64,576]{3,2,1,0:T(8,128)(2,1)} %bitcast.52, s32[128]{0:T(128)S(1)} %reshape.104), kind=kCustom, calls=%fused_computation | custom fusion | bytes 18875392 | tf_op jit(solution)/shard_map/gather | solution.py:66
  38.3 30.5 %all-gather.3.cloned.1.call-done = bf16[4,4,128,576]{3,2,1,0:T(8,128)(2,1)} async-done(((bf16[4,4,16,576]{3,2,1,0:T(8,128)(2,1)}), bf16[4,4,128,576]{3,2,1,0:T(8,128)(2,1)}) %all-gather.3.cloned.1.call-update) | async-done | bytes 2359312 | tf_op jit(solution)/shard_map/all_gather | solution.py:42
  68.8 7.6 %bitcast_reduce_fusion = (f32[4,4,128]{2,1,0:T(4,128)S(1)}, f32[4,4,512,128]{3,2,1,0:T(8,128)}) fusion(pred[4,4,512]{2,1,0:T(4,128)(4,1)S(1)} %fusion.33, bf16[4,4,512,576]{3,2,1,0:T(8,128)(2,1)} %bitcast.53, bf16[4,4,128,576]{3,2,1,0:T(8,128)(2,1)} %all-gather.3.cloned.1.call-done), kind=kOutput, calls=%fused_computation.7 | convolution fusion | flops 1211103232 | bytes 16007168 | tf_op jit(solution)/shard_map/srhl,srtl->srht/dot_general | solution.py:75
  76.4 19.2 %pmax.7 = f32[4,4,128]{2,1,0:T(4,128)S(1)} all-reduce(f32[4,4,128]{2,1,0:T(4,128)S(1)} %get-tuple-element.17), channel_id=1, replica_groups=mesh['ctx'=8,'req'=4] {'ctx'}, use_global_device_ids=true, to_apply=%region_4.5 | all-reduce | flops 2048 | bytes 16384 | tf_op jit(solution)/shard_map/pmax | solution.py:88
  95.6 6.1 %fusion.6 = f32[4,4,128]{2,1,0:T(4,128)S(1)} fusion(f32[4,4,512,128]{3,2,1,0:T(8,128)} %get-tuple-element.18, f32[4,4,128]{2,1,0:T(4,128)S(1)} %get-tuple-element.17, pred[4,4,512]{2,1,0:T(4,128)(4,1)S(1)} %fusion.33), kind=kLoop, calls=%fused_computation.12 | loop fusion | flops 5240832 | bytes 4218880 | tf_op jit(solution)/shard_map/reduce_sum | solution.py:81
  101.9 0.7 reshape.115
  102.7 0.5 all-gather.5.cloned.1.call-update
  103.3 7.7 %multiply_convert_fusion = bf16[4,4,128,512]{3,2,1,0:T(8,128)(2,1)S(1)} fusion(f32[4,4,128]{2,1,0:T(4,128)S(1)} %get-tuple-element.13, bf16[4,4,512,576]{3,2,1,0:T(8,128)(2,1)} %bitcast.54, f32[4,4,512,128]{3,2,1,0:T(8,128)} %get-tuple-element.18, f32[4,4,128]{2,1,0:T(4,128)S(1)} %get-tuple-element.17, pred[4,4,512]{2,1,0:T(4,128)(4,1)S(1)} %fusion.33), kind=kOutput, calls=%fused_computation.10 | convolution fusion | flops 1081081856 | bytes 14712832 | tf_op jit(solution)/shard_map/srht,srtk->srhk/dot_general | solution.py:82
  111.0 2.9 %copy.30 = bf16[4,4,128,512]{3,1,0,2:T(4,128)(2,1)} copy(bf16[4,4,128,512]{3,2,1,0:T(8,128)(2,1)S(1)} %multiply_convert_fusion) | data formatting | bytes 4194304 | tf_op jit(solution)/shard_map/convert_element_type | solution.py:95
  114.2 30.5 %all_gather.15 = bf16[4,4,64]{1,0,2:T(4,128)(2,1)S(1)} all-gather(bf16[4,4,8]{1,0,2:T(4,128)(2,1)S(1)} %copy.33), channel_id=1, replica_groups=mesh['ctx'=8,'req'=4] {'ctx'}, dimensions={2}, use_global_device_ids=true | all-gather | bytes 2304 | tf_op jit(solution)/shard_map/all_gather | solution.py:44
  144.8 0.6 dynamic-slice
  146.0 27.5 %all_gather.14 = bf16[4,4,64,128]{3,2,0,1:T(8,128)(2,1)S(1)} all-gather(bf16[4,4,8,128]{3,2,0,1:T(8,128)(2,1)S(1)} %copy.32), channel_id=1, replica_groups=mesh['ctx'=8,'req'=4] {'ctx'}, dimensions={2}, use_global_device_ids=true | all-gather | bytes 294912 | tf_op jit(solution)/shard_map/all_gather | solution.py:43
  173.5 1.3 maximum_bitcast_fusion
  174.8 0.7 fusion.2
  175.4 0.8 bitcast_select_fusion
  176.2 0.8 reshape.116
  177.2 81.6 %all-reduce.3.cloned.1.call-done = bf16[4,4,128,512]{3,1,0,2:T(4,128)(2,1)} async-done(((bf16[4,4,128,512]{3,1,0,2:T(4,128)(2,1)}), bf16[4,4,128,512]{3,1,0,2:T(4,128)(2,1)}) %all-reduce.3.cloned.1.call-update) | async-done | bytes 2097168
  258.9 2.2 fusion.25
  261.1 0.6 copy.34
  (39 shorter events, 1.6 us)
Async XLA Ops:
  8.0 165.5 %copy-start = (bf16[4,2048,128]{2,1,0:T(8,128)(2,1)S(1)}, bf16[4,2048,128]{2,1,0:T(8,128)(2,1)}, u32[]{:S(2)}) copy-start(bf16[4,2048,128]{2,1,0:T(8,128)(2,1)} %param.10) | copy-start | bytes 6291460
  8.0 60.8 %all-gather.3.cloned.1.call-start = ((), (), s32[]{:S(2)}) async-start(), calls=%async_computation.1 | async-start | bytes 2949120 | tf_op jit(solution)/shard_map/all_gather | solution.py:42
  8.7 167.5 %reduce-scatter.4.cloned.1.call-start = ((), (), s32[]{:S(2)}) async-start(), calls=%async_computation.3 | async-start | bytes 36864
  25.8 12.3 %copy-start.3 = (s32[4]{0:T(128)S(1)}, s32[4]{0:T(128)}, u32[]{:S(2)}) copy-start(s32[4]{0:T(128)} %param.17) | copy-start | bytes 52
  102.6 74.6 %all-gather.5.cloned.1.call-start = ((), (), s32[]{:S(2)}) async-start(), calls=%async_computation.2 | async-start | bytes 2621440 | tf_op jit(solution)/shard_map/all_gather | solution.py:102
  103.2 155.6 %all-reduce.3.cloned.1.call-start = ((), (), s32[]{:S(2)}) async-start(), calls=%async_computation.4 | async-start | bytes 4194304
  111.0 3.0 %copy-start.1 = (bf16[4,4,8,128]{3,2,1,0:T(8,128)(2,1)S(1)}, bf16[4,4,8,128]{3,2,1,0:T(8,128)(2,1)}, u32[]{:S(2)}) copy-start(bf16[4,4,8,128]{3,2,1,0:T(8,128)(2,1)} %param.12) | copy-start | bytes 98308
  111.0 3.0 %copy-start.2 = (bf16[4,4,8]{2,1,0:T(4,128)(2,1)S(1)}, bf16[4,4,8]{2,1,0:T(4,128)(2,1)}, u32[]{:S(2)}) copy-start(bf16[4,4,8]{2,1,0:T(4,128)(2,1)} %param.13) | copy-start | bytes 772
  111.0 33.7 %copy-start.4 = (u32[32]{0:T(128)S(1)}, u32[32]{0:T(128)}, u32[]{:S(2)}) copy-start(u32[32]{0:T(128)} %constant.52) | copy-start | bytes 388
Sparse Core Ops, SparseCore 0:
  11.1 57.6 all-gather.2
  102.8 50.7 reduce-scatter.3
  157.2 101.5 all-reduce.2
Sparse Core Ops, SparseCore 1:
  104.7 19.6 all-gather.4
where the time goes:
time: 270 us; the launch traced here: 269 us
  waiting for transfers between devices  113 us (42%)
  blocking collectives  77.2 us (29%)
  local copies, waits for them, and re-layouts  33.4 us (12%)
  matrix products  19.5 us (7%)
  between operations  16 us (6%)
  other arithmetic  9.22 us (3%)
    unnamed x6, waiting for transfers between devices  82.9 us
    all_gather x1, waiting for transfers between devices, per_device(): lax.all_gather(queries, 'ctx', axis=2, tiled=True)  30.5 us
    all_gather x1, blocking collectives, per_device(): lax.all_gather(index_weights, 'ctx', axis=2, tiled=True)  30.5 us
    all_gather x1, blocking collectives, per_device(): lax.all_gather(index_queries, 'ctx', axis=2, tiled=True)  27.5 us
    pmax x1, blocking collectives, per_device(): global_peak = lax.pmax(peak_score, 'ctx')  19.2 us
    unnamed x19, local copies, waits for them, and re-layouts  17.4 us
    gather x1, local copies, waits for them, and re-layouts, per_device(): block_tiles[request_numbers, block_index]  12.3 us
    dot_general x1, matrix products, per_device(): jnp.einsum('srht,srtk->srhk', exp_weights.astype(jnp.bfloat16), gathered[...  7.72 us
  transfers between devices with their start and end apart: 4, of which 2 were waited for; matrix products, arithmetic and copies ran while one was open for 17% of the time, Pallas kernels for 0%

commit v1 on v0

--- a/solution.py
+++ b/solution.py
@@ -1,11 +1,25 @@
+import functools
+
 import jax
 import jax.numpy as jnp
 from jax import lax
+from jax.experimental import pallas as pl
+from jax.experimental.pallas import tpu as pltpu
 from jax.sharding import PartitionSpec as P
 
 KV = 512
 QK_DIM = 192
 BLOCK = 64
+VMEM_LIMIT = 40 * 1024 * 1024
+
+CHUNKS = 2
+PAIRS = 8
+HEADS = 16
+ROWS = PAIRS * HEADS
+EXTRA = 8
+WIDE = 640
+SLOTS = 8
+LANES = 128
 
 
 def compact_slots(owned_slot, local_block, capacity):
@@ -17,6 +31,444 @@
     block_index = jnp.sum(chosen * local_block[..., None, :], axis=-1)
     filled = jnp.sum(chosen, axis=-1) > 0
     return (block_index, filled)
+
+
+def call(body, **kwargs):
+    return pl.pallas_call(
+        body,
+        compiler_params=pltpu.CompilerParams(vmem_limit_bytes=VMEM_LIMIT),
+        **kwargs,
+    )
+
+
+def whole(shape):
+    return pl.BlockSpec(shape, lambda *_: (0,) * len(shape))
+
+
+def pack_kernel(q_ref, iq_ref, iw_ref, out_ref):
+    for step in range(4):
+        for local in range(2):
+            row = (step * 2 + local) * HEADS
+            query = q_ref[step, local]
+            index_query = iq_ref[step, local]
+            halves = jnp.concatenate([index_query[:, :64], index_query[:, 64:]], axis=0)
+            out_ref[row : row + HEADS, :512] = query[:, :512]
+            out_ref[row : row + HEADS, 512:] = jnp.concatenate([query[:, 512:], halves], axis=1)
+    out_ref[ROWS:, :] = jnp.zeros((EXTRA, WIDE), jnp.bfloat16)
+    out_ref[ROWS:, :LANES] = iw_ref[...]
+
+
+def pack(chunk, queries, index_queries, weight_columns):
+    return call(
+        pack_kernel,
+        grid=(1,),
+        in_specs=[
+            pl.BlockSpec((4, 2, HEADS, 576), lambda _: (0, chunk, 0, 0)),
+            pl.BlockSpec((4, 2, 8, 128), lambda _: (0, chunk, 0, 0)),
+            whole((8, LANES)),
+        ],
+        out_specs=whole((ROWS + EXTRA, WIDE)),
+        out_shape=jax.ShapeDtypeStruct((ROWS + EXTRA, WIDE), jnp.bfloat16),
+        name="pack",
+    )(queries, index_queries, weight_columns)
+
+
+def gather_kernel(chunk, block_ref, latent_ref, out_ref):
+    request = chunk * 2 + pl.program_id(0)
+    first_half = lax.broadcasted_iota(jnp.int32, (576, LANES), 1) < 64
+
+    def tile(step, slot, want_odd):
+        block = block_ref[step, request, slot]
+        start = pl.multiple_of((block // 2) * LANES, LANES)
+        here = latent_ref[0, :, pl.ds(start, LANES)]
+        turned = jnp.concatenate([here[:, 64:], here[:, :64]], axis=1)
+        return jnp.where(block % 2 == want_odd, here, turned)
+
+    for step in range(4):
+        for half in range(SLOTS // 2):
+            left = tile(step, 2 * half, 0)
+            right = tile(step, 2 * half + 1, 1)
+            out_ref[step, 0, :576, half * LANES : (half + 1) * LANES] = jnp.where(
+                first_half, left, right
+            )
+        out_ref[step, 0, 576:, :] = jnp.zeros((64, 512), jnp.bfloat16)
+
+
+def gather(chunk, block_index, latents_t):
+    return call(
+        functools.partial(gather_kernel, chunk),
+        grid_spec=pltpu.PrefetchScalarGridSpec(
+            num_scalar_prefetch=1,
+            grid=(2,),
+            in_specs=[pl.BlockSpec((1, 576, 2048), lambda i, _: (chunk * 2 + i, 0, 0))],
+            out_specs=pl.BlockSpec((4, 1, WIDE, 512), lambda i, _: (0, i, 0, 0)),
+        ),
+        out_shape=jax.ShapeDtypeStruct((4, 2, WIDE, 512), jnp.bfloat16),
+        name="gather_blocks",
+    )(block_index, latents_t)
+
+
+def split3(value):
+    high = value.astype(jnp.bfloat16)
+    rest = value - high.astype(jnp.float32)
+    middle = rest.astype(jnp.bfloat16)
+    low = (rest - middle.astype(jnp.float32)).astype(jnp.bfloat16)
+    return high, middle, low
+
+
+def store_stats(out_ref, row, stats):
+    turned = stats.T[:PAIRS]
+    for place, part in enumerate(split3(turned)):
+        out_ref[row : row + PAIRS, place * LANES : (place + 1) * LANES] = part
+    out_ref[row : row + PAIRS, 3 * LANES :] = jnp.zeros((PAIRS, LANES), jnp.bfloat16)
+
+
+def load_stats(in_ref, row):
+    parts = [
+        in_ref[row : row + PAIRS, place * LANES : (place + 1) * LANES].astype(jnp.float32)
+        for place in range(3)
+    ]
+    turned = (parts[0] + parts[1]) + parts[2]
+    return jnp.concatenate([turned, jnp.zeros((LANES - PAIRS, LANES), jnp.float32)], axis=0).T
+
+
+def attend_kernel(*refs):
+    q_refs = refs[:8]
+    block_ref, bias_ref = refs[8:10]
+    own_a, own_b, send_a, send_b, stats_ref = refs[10:]
+    step = pl.program_id(0)
+    lane = lax.broadcasted_iota(jnp.int32, (LANES, LANES), 1)
+
+    @pl.when(step == 0)
+    def _():
+        stats_ref[...] = jnp.zeros((LANES, LANES), jnp.float32)
+
+    stats = stats_ref[...]
+    for local in range(2):
+        query = jnp.concatenate([r[local * HEADS : (local + 1) * HEADS, :] for r in q_refs], axis=0)
+        blocks = block_ref[0, local]
+        scores = jnp.dot(query, blocks, preferred_element_type=jnp.float32) * (QK_DIM**-0.5)
+        scores = scores + bias_ref[0, local]
+        peak = jnp.maximum(jnp.max(scores, axis=1, keepdims=True), -1e29)
+        weights = jnp.exp(scores - peak)
+        total = jnp.maximum(jnp.sum(weights, axis=1, keepdims=True), 1e-30)
+        mixed = lax.dot_general(
+            weights.astype(jnp.bfloat16),
+            blocks[:KV],
+            (((1,), (1,)), ((), ())),
+            preferred_element_type=jnp.float32,
+        )
+        mixed = (mixed * (1.0 / total)).astype(jnp.bfloat16)
+        pair = step * 2 + local
+        stats = jnp.where(lane == pair, peak + jnp.log(total), stats)
+        for across, (out_a, out_b) in enumerate(((own_a, own_b), (send_a, send_b))):
+            for out, members in ((out_a, (3, 2)), (out_b, (1, 0))):
+                for place, member in enumerate(members):
+                    source = (across * 4 + member) * HEADS
+                    row = pl.multiple_of(place * ROWS + pair * HEADS, HEADS)
+                    out[pl.ds(row, HEADS), :] = mixed[source : source + HEADS]
+    stats_ref[...] = stats
+
+    @pl.when(step == 3)
+    def _():
+        store_stats(send_a, 2 * ROWS, stats)
+
+
+def attend(gathered_queries, blocks, bias):
+    bf16 = jnp.bfloat16
+    return call(
+        attend_kernel,
+        grid=(4,),
+        in_specs=[pl.BlockSpec((2 * HEADS, WIDE), lambda i: (i, 0))] * 8
+        + [
+            pl.BlockSpec((1, 2, WIDE, 512), lambda i: (i, 0, 0, 0)),
+            pl.BlockSpec((1, 2, 1, 512), lambda i: (i, 0, 0, 0)),
+        ],
+        out_specs=[
+            whole((2 * ROWS, KV)),
+            whole((2 * ROWS, KV)),
+            whole((2 * ROWS + EXTRA, KV)),
+            whole((2 * ROWS, KV)),
+            whole((LANES, LANES)),
+        ],
+        out_shape=[
+            jax.ShapeDtypeStruct((2 * ROWS, KV), bf16),
+            jax.ShapeDtypeStruct((2 * ROWS, KV), bf16),
+            jax.ShapeDtypeStruct((2 * ROWS + EXTRA, KV), bf16),
+            jax.ShapeDtypeStruct((2 * ROWS, KV), bf16),
+            jax.ShapeDtypeStruct((LANES, LANES), jnp.float32),
+        ],
+        name="attend",
+    )(*gathered_queries, blocks, bias)
+
+
+def joined(own_ref, other_ref, place, weight_own, weight_other):
+    for pair in range(PAIRS):
+        row = place * ROWS + pair * HEADS
+        own = own_ref[row : row + HEADS, :].astype(jnp.float32)
+        other = other_ref[row : row + HEADS, :].astype(jnp.float32)
+        yield pair, (
+            own * weight_own[:, pair : pair + 1] + other * weight_other[:, pair : pair + 1]
+        )
+
+
+def join_a_kernel(own_ref, other_ref, stats_ref, out3_ref, out2_ref, weight_ref, lse_ref):
+    own = stats_ref[:64]
+    other = load_stats(other_ref, 2 * ROWS)[64:]
+    peak = jnp.maximum(own, other)
+    own, other = jnp.exp(own - peak), jnp.exp(other - peak)
+    total = own + other
+    own, other = own / total, other / total
+    lse = jnp.concatenate([peak + jnp.log(total), jnp.zeros((64, LANES), jnp.float32)], axis=0)
+    weight_ref[0] = own
+    weight_ref[1] = other
+    lse_ref[...] = lse
+    for place, (member, out_ref) in enumerate(((3, out3_ref), (2, out2_ref))):
+        part = slice(member * HEADS, (member + 1) * HEADS)
+        for pair, rows in joined(own_ref, other_ref, place, own[part], other[part]):
+            out_ref[pair * HEADS : (pair + 1) * HEADS, :] = rows.astype(jnp.bfloat16)
+        store_stats(out_ref, ROWS, lse)
+
+
+def join_a(own, other, stats):
+    message = jax.ShapeDtypeStruct((ROWS + EXTRA, KV), jnp.bfloat16)
+    return call(
+        join_a_kernel,
+        out_shape=[
+            message,
+            message,
+            jax.ShapeDtypeStruct((2, 64, LANES), jnp.float32),
+            jax.ShapeDtypeStruct((LANES, LANES), jnp.float32),
+        ],
+        name="join_far",
+    )(own, other, stats)
+
+
+def join_b_kernel(own_ref, other_ref, weight_ref, lse_ref, out1_ref, out0_ref):
+    for place, (member, out_ref) in enumerate(((1, out1_ref), (0, out0_ref))):
+        part = slice(member * HEADS, (member + 1) * HEADS)
+        weights = weight_ref[0, part], weight_ref[1, part]
+        for pair, rows in joined(own_ref, other_ref, place, *weights):
+            out_ref[pair * HEADS : (pair + 1) * HEADS, :] = rows.astype(out_ref.dtype)
+    store_stats(out1_ref, ROWS, lse_ref[...])
+
+
+def join_b(own, other, weights, lse):
+    return call(
+        join_b_kernel,
+        out_shape=[
+            jax.ShapeDtypeStruct((ROWS + EXTRA, KV), jnp.bfloat16),
+            jax.ShapeDtypeStruct((ROWS, KV), jnp.float32),
+        ],
+        name="join_near",
+    )(own, other, weights, lse)
+
+
+def finish_kernel(lse_ref, own_ref, r1_ref, r2_ref, r3_ref, up_ref, *rest):
+    out_ref, rows_ref, lifted_ref = rest[-3:]
+    received = (r1_ref, r2_ref, r3_ref)
+    stats = [lse_ref[:HEADS]] + [
+        load_stats(ref, ROWS)[member * HEADS : (member + 1) * HEADS]
+        for member, ref in enumerate(received, 1)
+    ]
+    peak = functools.reduce(jnp.maximum, stats)
+    stats = [jnp.exp(value - peak) for value in stats]
+    total = functools.reduce(jnp.add, stats)
+    stats = [value / total for value in stats]
+    for pair in range(PAIRS):
+        part = slice(pair * HEADS, (pair + 1) * HEADS)
+        rows = own_ref[part, :] * stats[0][:, pair : pair + 1]
+        for value, ref in zip(stats[1:], received):
+            rows = rows + ref[part, :].astype(jnp.float32) * value[:, pair : pair + 1]
+        for tile in range(4):
+            rows_ref[tile, part, :] = rows[:, tile * LANES : (tile + 1) * LANES]
+    for head in range(HEADS):
+        attended = jnp.concatenate(
+            [rows_ref[tile, pl.ds(head, PAIRS, stride=HEADS), :] for tile in range(4)], axis=1
+        ).astype(jnp.bfloat16)
+        lifted_ref[pl.ds(head, PAIRS, stride=HEADS), :] = jnp.dot(
+            attended, up_ref[head], preferred_element_type=jnp.float32
+        )
+    for step in range(4):
+        for local in range(2):
+            row = (step * 2 + local) * HEADS
+            out_ref[step, local] = lifted_ref[row : row + HEADS, :].astype(jnp.bfloat16)
+
+
+def finish(chunk, lse, own, received, up, before):
+    message = whole((ROWS + EXTRA, KV))
+    specs = [whole((LANES, LANES)), whole((ROWS, KV)), message, message, message]
+    specs.append(whole((HEADS, KV, 128)))
+    args = [lse, own, *received, up]
+    aliases = {}
+    if before is not None:
+        specs.append(pl.BlockSpec(memory_space=pl.ANY))
+        args.append(before)
+        aliases = {len(args) - 1: 0}
+    return call(
+        finish_kernel,
+        grid=(1,),
+        in_specs=specs,
+        out_specs=pl.BlockSpec((4, 2, HEADS, 128), lambda _: (0, chunk, 0, 0)),
+        out_shape=jax.ShapeDtypeStruct((4, 4, HEADS, 128), jnp.bfloat16),
+        scratch_shapes=[
+            pltpu.VMEM((4, ROWS, LANES), jnp.float32),
+            pltpu.VMEM((ROWS, 128), jnp.float32),
+        ],
+        input_output_aliases=aliases,
+        name="finish",
+    )(*args)
+
+
+def assemble_kernel(place_ref, *refs):
+    out_ref = refs[-1]
+    for relative, ref in enumerate(refs[:-1]):
+        start = pl.multiple_of((place_ref[0] ^ relative) * 128, 128)
+        out_ref[:, pl.ds(start, 128), :] = ref[...]
+
+
+def assemble(place, pieces):
+    return call(
+        assemble_kernel,
+        in_specs=[pl.BlockSpec(memory_space=pltpu.SMEM)] + [pl.BlockSpec()] * 4,
+        out_shape=jax.ShapeDtypeStruct((HEADS, KV, 128), jnp.bfloat16),
+        name="assemble_up",
+    )(place, *pieces)
+
+
+def index_kernel(scalar_ref, *refs):
+    payloads = refs[:8], refs[8:16]
+    key_ref, out_ref = refs[16:]
+    request = pl.program_id(0)
+    local = request % 2
+    base = scalar_ref[4]
+    limit = scalar_ref[request]
+    for chunk in range(CHUNKS):
+
+        @pl.when(request // 2 == chunk)
+        def _(members=payloads[chunk]):
+            columns = jnp.concatenate([r[ROWS:, :LANES] for r in members], axis=0)
+            columns = columns.astype(jnp.float32)
+            lane = lax.broadcasted_iota(jnp.int32, (64, LANES), 1)
+            query_rows, weight_rows = [], []
+            for step in range(4):
+                pair = step * 2 + local
+                row = pl.multiple_of(pair * HEADS, HEADS)
+                tail = jnp.concatenate(
+                    [r[pl.ds(row, HEADS), 512:] for r in members], axis=0
+                ).astype(jnp.float32)
+                tail = tail.reshape(8, 2, 8, LANES)
+                first = tail[:, 0].reshape(64, LANES)
+                second = tail[:, 1].reshape(64, LANES)
+                query_rows.append(jnp.concatenate([first[:, 64:], second[:, 64:]], axis=1))
+                weight_rows.append(
+                    jnp.sum(jnp.where(lane == pair, columns, 0.0), axis=1, keepdims=True)
+                )
+            queries = jnp.concatenate(query_rows, axis=0).astype(jnp.bfloat16)
+            for part in range(4):
+                at = slice(part * 512, (part + 1) * 512)
+                products = lax.dot_general(
+                    queries,
+                    key_ref[0, at, :],
+                    (((1,), (1,)), ((), ())),
+                    preferred_element_type=jnp.float32,
+                )
+                position = base + part * 512 + lax.broadcasted_iota(jnp.int32, (1, 512), 1)
+                for step in range(4):
+                    mine = jnp.maximum(products[step * 64 : (step + 1) * 64], 0.0)
+                    summed = jnp.sum(mine * weight_rows[step], axis=0, keepdims=True)
+                    out_ref[step, pl.ds(request, 1), at] = jnp.where(
+                        position <= limit + step, summed, 0.0
+                    )
+
+
+def index_rows(scalars, payloads, index_keys):
+    return call(
+        index_kernel,
+        grid_spec=pltpu.PrefetchScalarGridSpec(
+            num_scalar_prefetch=1,
+            grid=(4,),
+            in_specs=[whole((ROWS + EXTRA, WIDE))] * 16
+            + [pl.BlockSpec((1, 2048, 128), lambda i, _: (i, 0, 0))],
+            out_specs=whole((4, 4, 2048)),
+        ),
+        out_shape=jax.ShapeDtypeStruct((4, 4, 2048), jnp.float32),
+        name="index_scores",
+    )(scalars, *payloads[0], *payloads[1], index_keys)
+
+
+def fast(
+    latents,
+    index_keys,
+    queries,
+    index_queries,
+    index_weights,
+    value_up_weight,
+    selection,
+    counts,
+    lengths,
+):
+    own_shard = lax.axis_index("ctx")
+    context_dev = latents.shape[1]
+    blocks_dev = context_dev // BLOCK
+
+    def across_x(value):
+        return lax.ppermute(value, "ctx", [(i, i ^ 1) for i in range(8)])
+
+    def across_z(value, distance):
+        return lax.ppermute(value, "ctx", [(i, i ^ (2 * distance)) for i in range(8)])
+
+    def across_req(value, distance):
+        return lax.ppermute(value, "req", [(i, i ^ distance) for i in range(4)])
+
+    columns = index_weights.reshape(4, 2, 2, 8).transpose(1, 3, 0, 2).reshape(CHUNKS, 8, PAIRS)
+    columns = jnp.pad(columns, ((0, 0), (0, 0), (0, LANES - PAIRS)))
+
+    gathered = []
+    for chunk in range(CHUNKS):
+        own = pack(chunk, queries, index_queries, columns[chunk])
+        z2 = across_z(own, 2)
+        z1 = across_z(own, 1)
+        z3 = across_z(z2, 1)
+        line = [own, z1, z2, z3]
+        gathered.append(line + [across_x(member) for member in line])
+
+    local_block = selection - own_shard * blocks_dev
+    slot_ids = jnp.arange(selection.shape[2], dtype=jnp.int32)
+    owned_slot = (
+        (local_block >= 0)
+        & (local_block < blocks_dev)
+        & (slot_ids[None, None, :] < counts[:, :, None])
+    )
+    block_index, filled = compact_slots(owned_slot, local_block, SLOTS)
+    limits = lengths[None, :] + jnp.arange(4, dtype=jnp.int32)[:, None]
+    positions = (block_index + own_shard * blocks_dev)[..., None] * BLOCK + jnp.arange(
+        BLOCK, dtype=jnp.int32
+    )
+    usable = filled[..., None] & (positions <= limits[:, :, None, None])
+    bias = jnp.where(usable, 0.0, -1e30).astype(jnp.float32).reshape(4, 4, 1, SLOTS * BLOCK)
+
+    latents_t = jnp.transpose(latents, (0, 2, 1))
+    up_core = across_req(value_up_weight, 1)
+    up_y = across_req(value_up_weight, 2)
+    up_both = across_req(up_y, 1)
+    place = lax.axis_index("req").astype(jnp.int32).reshape(1)
+    up = assemble(place, [value_up_weight, up_core, up_y, up_both])
+
+    head_values = None
+    for chunk in range(CHUNKS):
+        blocks = gather(chunk, block_index, latents_t)
+        own_a, own_b, send_a, send_b, stats = attend(
+            gathered[chunk], blocks, bias[:, 2 * chunk : 2 * chunk + 2]
+        )
+        far3, far2, weights, lse = join_a(own_a, across_x(send_a), stats)
+        near, mine = join_b(own_b, across_x(send_b), weights, lse)
+        received = [across_z(near, 1), across_z(far2, 2), across_z(far3, 3)]
+        head_values = finish(chunk, lse, mine, received, up, head_values)
+
+    scalars = jnp.concatenate([lengths, (own_shard * context_dev).astype(jnp.int32).reshape(1)])
+    index_scores = index_rows(scalars, gathered, index_keys)
+    return (head_values, index_scores)
 
 
 def per_device(
@@ -119,8 +571,10 @@
         P(None, "req"),
         P("req"),
     )
+    sizes = dict(mesh.shape)
+    plan = fast if (sizes["ctx"], sizes["req"]) == (8, 4) else per_device
     return jax.shard_map(
-        per_device,
+        plan,
         mesh=mesh,
         in_specs=placed,
         out_specs=(P(None, "req", "ctx", None), P(None, "req", "ctx")),

time: 270 us -> 108 us (0.40)
  waiting for transfers between devices: 113 us -> 18.8 us
  blocking collectives: 77.2 us -> 0 us
  Pallas kernels: 0 us -> 37.5 us
  starting transfers between devices: 0.16 us -> 32.8 us
  matrix products: 19.5 us -> 0 us
  local copies, waits for them, and re-layouts: 33.4 us -> 14.1 us
  between operations: 16 us -> 1.01 us
  other arithmetic: 9.22 us -> 3.12 us
    unnamed x6 -> x0, waiting for transfers between devices: 82.9 us -> none
    all_gather x2 -> x0, blocking collectives: 58 us -> none  [the longest x1 30.5 us: per_device(): lax.all_gather(index_weights, 'ctx', axis=2, tiled=True)]
    pallas_call x0 -> x14, Pallas kernels: none -> 37.5 us  [the longest x2 16.6 us: gather(): call(functools.partial(gather_kernel, chunk), grid_spec=pltpu.PrefetchSca...]
    ppermute x0 -> x27, starting transfers between devices: none -> 32.8 us  [the longest x12 17.6 us: across_x(): return lax.ppermute(value, 'ctx', [(i, i ^ 1) for i in range(8)])]
    all_gather x2 -> x0, waiting for transfers between devices: 30.5 us -> none  [the longest x1 30.5 us: per_device(): lax.all_gather(queries, 'ctx', axis=2, tiled=True)]
    dot_general x5 -> x0, matrix products: 19.5 us -> none  [the longest x1 7.72 us: per_device(): jnp.einsum('srht,srtk->srhk', exp_weights.astype(jnp.bfloat16), gathered[...]
    pmax x1 -> x0, blocking collectives: 19.2 us -> none  [per_device(): global_peak = lax.pmax(peak_score, 'ctx')]
    ppermute x0 -> x27, waiting for transfers between devices: none -> 18.8 us  [the longest x12 14.7 us: across_x(): return lax.ppermute(value, 'ctx', [(i, i ^ 1) for i in range(8)])]
  transfers between devices with their start and end apart: 4 -> 27, of which waited for: 2 -> 9; matrix products, arithmetic and copies ran while one was open for 17% -> 3% of each run, Pallas kernels for 0% -> 33%
where the time goes in v1:
time: 108 us; the launch traced here: 107 us
  Pallas kernels  37.5 us (35%)
  starting transfers between devices  32.8 us (30%)
  waiting for transfers between devices  18.8 us (17%)
  local copies, waits for them, and re-layouts  14.1 us (13%)
  other arithmetic  3.12 us (3%)
    ppermute x12, starting transfers between devices, across_x(): return lax.ppermute(value, 'ctx', [(i, i ^ 1) for i in range(8)])  17.6 us
    pallas_call x2, Pallas kernels, gather(): call(functools.partial(gather_kernel, chunk), grid_spec=pltpu.PrefetchSca...  16.6 us
    ppermute x12, waiting for transfers between devices, across_x(): return lax.ppermute(value, 'ctx', [(i, i ^ 1) for i in range(8)])  14.7 us
    ppermute x12, starting transfers between devices, across_z(): return lax.ppermute(value, 'ctx', [(i, i ^ 2 * distance) for i in range(8)])  13.1 us
    unnamed x72, local copies, waits for them, and re-layouts  12.9 us
    pallas_call x2, Pallas kernels, attend(): call(attend_kernel, grid=(4,), in_specs=[pl.BlockSpec((2 * HEADS, WIDE),...  8.33 us
    pallas_call x2, Pallas kernels, finish(): call(finish_kernel, grid=(1,), in_specs=specs, out_specs=pl.BlockSpec((4,...  4.56 us
    ppermute x12, waiting for transfers between devices, across_z(): return lax.ppermute(value, 'ctx', [(i, i ^ 2 * distance) for i in range(8)])  4.03 us
  transfers between devices with their start and end apart: 27, of which 9 were waited for; matrix products, arithmetic and copies ran while one was open for 3% of the time, Pallas kernels for 33%

profile of v1, /device:TPU:0, one launch (start us, length us, event | category | flops | bytes accessed | tf_op | source)
XLA Modules:
  0.0 107.3 jit_solution(17093626973960271889)
XLA Ops:
  3.3 4.1 %collective-permute-start.16 = (bf16[136,640]{1,0:T(8,128)(2,1)S(1)}, bf16[136,640]{1,0:T(8,128)(2,1)S(1)}, u32[]{:S(2)}, u32[]{:S(2)}) collective-permute-start(bf16[136,640]{1,0:T(8,128)(2,1)S(1)} %pack.3.refs_0_), channel_id=1, source_target_pairs={{0,16},{4,20},{8,24},{12,28},{16,0},{20,4},{24,8},{28,12},{1,17},{... | collective-permute-start | bytes 522248 | tf_op jit(solution)/shard_map/ppermute | solution.py:419
  7.4 1.6 %collective-permute-start.15 = (bf16[136,640]{1,0:T(8,128)(2,1)S(1)}, bf16[136,640]{1,0:T(8,128)(2,1)S(1)}, u32[]{:S(2)}, u32[]{:S(2)}) collective-permute-start(bf16[136,640]{1,0:T(8,128)(2,1)S(1)} %pack.3.refs_0_), channel_id=1, source_target_pairs={{0,8},{4,12},{8,0},{12,4},{16,24},{20,28},{24,16},{28,20},{1,9},{5... | collective-permute-start | bytes 522248 | tf_op jit(solution)/shard_map/ppermute | solution.py:419
  14.8 2.5 %collective-permute-done.16.refs_2_ = bf16[136,640]{1,0:T(8,128)(2,1)S(1)} collective-permute-done((bf16[136,640]{1,0:T(8,128)(2,1)S(1)}, bf16[136,640]{1,0:T(8,128)(2,1)S(1)}, u32[]{:S(2)}, u32[]{:S(2)}) %collective-permute-start.16) | collective-permute-done | bytes 174112 | tf_op jit(solution)/shard_map/ppermute | solution.py:419
  18.4 2.0 %collective-permute-start = (bf16[136,640]{1,0:T(8,128)(2,1)S(1)}, bf16[136,640]{1,0:T(8,128)(2,1)S(1)}, u32[]{:S(2)}, u32[]{:S(2)}) collective-permute-start(bf16[136,640]{1,0:T(8,128)(2,1)S(1)} %pack.2.refs_0_.refs_8_), channel_id=1, source_target_pairs={{0,8},{4,12},{8,0},{12,4},{16,24},{20,28},{24,16},{28,20},{1,9},{5... | collective-permute-start | bytes 522248 | tf_op jit(solution)/shard_map/ppermute | solution.py:419
  20.4 4.7 %collective-permute-start.20 = (bf16[136,640]{1,0:T(8,128)(2,1)S(1)}, bf16[136,640]{1,0:T(8,128)(2,1)S(1)}, u32[]{:S(2)}, u32[]{:S(2)}) collective-permute-start(bf16[136,640]{1,0:T(8,128)(2,1)S(1)} %collective-permute-done.16.refs_2_), channel_id=1, source_target_pairs={{0,4},{4,0},{8,12},{12,8},{16,20},{20,16},{24,28},{28,24},{1,5},{5... | collective-permute-start | bytes 522248 | tf_op jit(solution)/shard_map/ppermute | solution.py:416
  26.5 1.5 %collective-permute-start.21 = (bf16[136,640]{1,0:T(8,128)(2,1)S(1)}, bf16[136,640]{1,0:T(8,128)(2,1)S(1)}, u32[]{:S(2)}, u32[]{:S(2)}) collective-permute-start(bf16[136,640]{1,0:T(8,128)(2,1)S(1)} %collective-permute-done.17.refs_3_), channel_id=1, source_target_pairs={{0,4},{4,0},{8,12},{12,8},{16,20},{20,16},{24,28},{28,24},{1,5},{5... | collective-permute-start | bytes 522248 | tf_op jit(solution)/shard_map/ppermute | solution.py:416
  28.4 1.5 %collective-permute-start.3 = (bf16[136,640]{1,0:T(8,128)(2,1)S(1)}, bf16[136,640]{1,0:T(8,128)(2,1)S(1)}, u32[]{:S(2)}, u32[]{:S(2)}) collective-permute-start(bf16[136,640]{1,0:T(8,128)(2,1)S(1)} %pack.2.refs_0_.refs_8_), channel_id=1, source_target_pairs={{0,4},{4,0},{8,12},{12,8},{16,20},{20,16},{24,28},{28,24},{1,5},{5... | collective-permute-start | bytes 522248 | tf_op jit(solution)/shard_map/ppermute | solution.py:416
  30.6 3.6 %collective-permute-done.19.refs_5_ = bf16[136,640]{1,0:T(8,128)(2,1)S(1)} collective-permute-done((bf16[136,640]{1,0:T(8,128)(2,1)S(1)}, bf16[136,640]{1,0:T(8,128)(2,1)S(1)}, u32[]{:S(2)}, u32[]{:S(2)}) %collective-permute-start.19) | collective-permute-done | bytes 174112 | tf_op jit(solution)/shard_map/ppermute | solution.py:416
  34.2 2.0 %collective-permute-start.5 = (bf16[136,640]{1,0:T(8,128)(2,1)S(1)}, bf16[136,640]{1,0:T(8,128)(2,1)S(1)}, u32[]{:S(2)}, u32[]{:S(2)}) collective-permute-start(bf16[136,640]{1,0:T(8,128)(2,1)S(1)} %collective-permute-done.1.refs_2_.refs_10_), channel_id=1, source_target_pairs={{0,4},{4,0},{8,12},{12,8},{16,20},{20,16},{24,28},{28,24},{1,5},{5... | collective-permute-start | bytes 522248 | tf_op jit(solution)/shard_map/ppermute | solution.py:416
  36.2 1.7 %collective-permute-done.21.refs_7_ = bf16[136,640]{1,0:T(8,128)(2,1)S(1)} collective-permute-done((bf16[136,640]{1,0:T(8,128)(2,1)S(1)}, bf16[136,640]{1,0:T(8,128)(2,1)S(1)}, u32[]{:S(2)}, u32[]{:S(2)}) %collective-permute-start.21) | collective-permute-done | bytes 174112 | tf_op jit(solution)/shard_map/ppermute | solution.py:416
  37.9 2.0 %collective-permute-start.4 = (bf16[136,640]{1,0:T(8,128)(2,1)S(1)}, bf16[136,640]{1,0:T(8,128)(2,1)S(1)}, u32[]{:S(2)}, u32[]{:S(2)}) collective-permute-start(bf16[136,640]{1,0:T(8,128)(2,1)S(1)} %collective-permute-done.refs_1_.refs_9_), channel_id=1, source_target_pairs={{0,4},{4,0},{8,12},{12,8},{16,20},{20,16},{24,28},{28,24},{1,5},{5... | collective-permute-start | bytes 522248 | tf_op jit(solution)/shard_map/ppermute | solution.py:416
  40.0 8.4 %gather_blocks.3.refs_8_ = bf16[4,2,640,512]{3,2,1,0:T(8,128)(2,1)S(1)} custom-call(s32[4,4,8]{2,1,0:T(4,128)S(1)} %get-tuple-element.47.block_ref, bf16[4,576,2048]{2,1,0:T(8,128)(2,1)} %bitcast.15), custom_call_target="tpu_custom_call" | custom-call | tf_op jit(solution)/shard_map/gather_blocks/pallas_call | solution.py:98
  48.4 4.2 %attend.3 = (bf16[256,512]{1,0:T(8,128)(2,1)S(1)}, bf16[256,512]{1,0:T(8,128)(2,1)S(1)}, bf16[264,512]{1,0:T(8,128)(2,1)S(1)}, bf16[256,512]{1,0:T(8,128)(2,1)S(1)}, f32[128,128]{1,0:T(8,128)S(1)}) custom-call(bf16[136,640]{1,0:T(8,128)(2,1)S(1)} %pack.3.refs_0_, bf16[136,640]{1,0:T(8,128)(2,1)S(1)} %collective-permute-done.15.refs_1_, ...), custom_call_target="tpu_custom_call" | custom-call | tf_op jit(solution)/shard_map/attend/pallas_call | solution.py:179
  53.3 2.0 %collective-permute-start.6 = (bf16[136,640]{1,0:T(8,128)(2,1)S(1)}, bf16[136,640]{1,0:T(8,128)(2,1)S(1)}, u32[]{:S(2)}, u32[]{:S(2)}) collective-permute-start(bf16[136,640]{1,0:T(8,128)(2,1)S(1)} %collective-permute-done.2.refs_3_.refs_11_), channel_id=1, source_target_pairs={{0,4},{4,0},{8,12},{12,8},{16,20},{20,16},{24,28},{28,24},{1,5},{5... | collective-permute-start | bytes 522248 | tf_op jit(solution)/shard_map/ppermute | solution.py:416
  55.3 8.2 %gather_blocks.2.refs_8_ = bf16[4,2,640,512]{3,2,1,0:T(8,128)(2,1)S(1)} custom-call(s32[4,4,8]{2,1,0:T(4,128)S(1)} %get-tuple-element.47.block_ref, bf16[4,576,2048]{2,1,0:T(8,128)(2,1)} %bitcast.16), custom_call_target="tpu_custom_call" | custom-call | tf_op jit(solution)/shard_map/gather_blocks/pallas_call | solution.py:98
  63.6 2.0 %collective-permute-done.6.refs_7_.refs_15_ = bf16[136,640]{1,0:T(8,128)(2,1)S(1)} collective-permute-done((bf16[136,640]{1,0:T(8,128)(2,1)S(1)}, bf16[136,640]{1,0:T(8,128)(2,1)S(1)}, u32[]{:S(2)}, u32[]{:S(2)}) %collective-permute-start.6) | collective-permute-done | bytes 174112 | tf_op jit(solution)/shard_map/ppermute | solution.py:416
  65.6 4.2 %attend.2 = (bf16[256,512]{1,0:T(8,128)(2,1)S(1)}, bf16[256,512]{1,0:T(8,128)(2,1)S(1)}, bf16[264,512]{1,0:T(8,128)(2,1)S(1)}, bf16[256,512]{1,0:T(8,128)(2,1)S(1)}, f32[128,128]{1,0:T(8,128)S(1)}) custom-call(bf16[136,640]{1,0:T(8,128)(2,1)S(1)} %pack.2.refs_0_.refs_8_, bf16[136,640]{1,0:T(8,128)(2,1)S(1)} %collective-permute-done.refs_1_.refs_9_, ...), custom_call_target="tpu_custom_call" | custom-call | tf_op jit(solution)/shard_map/attend/pallas_call | solution.py:179
  69.9 2.0 %collective-permute-start.8 = (bf16[256,512]{1,0:T(8,128)(2,1)S(1)}, bf16[256,512]{1,0:T(8,128)(2,1)S(1)}, u32[]{:S(2)}, u32[]{:S(2)}) collective-permute-start(bf16[256,512]{1,0:T(8,128)(2,1)S(1)} %get-tuple-element.29), channel_id=1, source_target_pairs={{0,4},{4,0},{8,12},{12,8},{16,20},{20,16},{24,28},{28,24},{1,5},{5... | collective-permute-start | bytes 786440 | tf_op jit(solution)/shard_map/ppermute | solution.py:416
  73.9 5.1 %collective-permute-done.7.other_ref = bf16[264,512]{1,0:T(8,128)(2,1)S(1)} collective-permute-done((bf16[264,512]{1,0:T(8,128)(2,1)S(1)}, bf16[264,512]{1,0:T(8,128)(2,1)S(1)}, u32[]{:S(2)}, u32[]{:S(2)}) %collective-permute-start.7) | collective-permute-done | bytes 270368 | tf_op jit(solution)/shard_map/ppermute | solution.py:416
  80.0 1.8 %collective-permute-done.8.other_ref = bf16[256,512]{1,0:T(8,128)(2,1)S(1)} collective-permute-done((bf16[256,512]{1,0:T(8,128)(2,1)S(1)}, bf16[256,512]{1,0:T(8,128)(2,1)S(1)}, u32[]{:S(2)}, u32[]{:S(2)}) %collective-permute-start.8) | collective-permute-done | bytes 262176 | tf_op jit(solution)/shard_map/ppermute | solution.py:416
  86.5 2.7 %collective-permute-start.10 = (bf16[136,512]{1,0:T(8,128)(2,1)}, bf16[136,512]{1,0:T(8,128)(2,1)}, u32[]{:S(2)}, u32[]{:S(2)}) collective-permute-start(bf16[136,512]{1,0:T(8,128)(2,1)} %get-tuple-element.33), channel_id=1, source_target_pairs={{0,16},{4,20},{8,24},{12,28},{16,0},{20,4},{24,8},{28,12},{1,17},{... | collective-permute-start | bytes 417800 | tf_op jit(solution)/shard_map/ppermute | solution.py:419
  98.1 3.4 %index_scores.1 = f32[4,4,2048]{2,1,0:T(4,128)} custom-call(s32[5]{0:T(128)S(1)} %pad_add_fusion.scalar_ref, bf16[136,640]{1,0:T(8,128)(2,1)S(1)} %pack.3.refs_0_, bf16[136,640]{1,0:T(8,128)(2,1)S(1)} %collective-permute-done.15.refs_1_, bf16[136,640]{1,0:T(8,128)(2,1)S(1)} %collective-permute-done.16.refs_2_, ...), custom_call_target="tpu_custom_call" | custom-call | tf_op jit(solution)/shard_map/index_scores/pallas_call | solution.py:386
  102.7 2.2 %finish.2.rest_0_ = bf16[4,4,16,128]{3,2,1,0:T(8,128)(2,1)} custom-call(f32[128,128]{1,0:T(8,128)S(1)} %copy-done.27, f32[128,512]{1,0:T(8,128)S(1)} %copy-done.31, bf16[136,512]{1,0:T(8,128)(2,1)S(1)} %copy-done.33, bf16[136,512]{1,0:T(8,128)(2,1)} %collective-permute-done.25.r2_ref, bf16[136,512]{1,0:T(8,128)(2,1)} %collective-permute-done.26.r3_ref, ...), custom_call_target="tpu_custom_call" | custom-call | tf_op jit(solution)/shard_map/finish/pallas_call | solution.py:308
  104.9 2.3 %finish.3 = bf16[4,4,16,128]{3,2,1,0:T(8,128)(2,1)} custom-call(f32[128,128]{1,0:T(8,128)S(1)} %copy-done.29, f32[128,512]{1,0:T(8,128)S(1)} %copy-done.25, bf16[136,512]{1,0:T(8,128)(2,1)} %collective-permute-done.9.r1_ref, bf16[136,512]{1,0:T(8,128)(2,1)} %collective-permute-done.10.r2_ref, ...), custom_call_target="tpu_custom_call", output_to_operand_aliasing={{}: (6, {})} | custom-call | tf_op jit(solution)/shard_map/finish/pallas_call | solution.py:308
  (135 shorter events, 30.6 us)
Async XLA Ops:
  3.3 14.0 %collective-permute-start.16 = (bf16[136,640]{1,0:T(8,128)(2,1)S(1)}, bf16[136,640]{1,0:T(8,128)(2,1)S(1)}, u32[]{:S(2)}, u32[]{:S(2)}) collective-permute-start(bf16[136,640]{1,0:T(8,128)(2,1)S(1)} %pack.3.refs_0_), channel_id=1, source_target_pairs={{0,16},{4,20},{8,24},{12,28},{16,0},{20,4},{24,8},{28,12},{1,17},{... | collective-permute-start | bytes 522248 | tf_op jit(solution)/shard_map/ppermute | solution.py:419
  7.4 11.0 %collective-permute-start.15 = (bf16[136,640]{1,0:T(8,128)(2,1)S(1)}, bf16[136,640]{1,0:T(8,128)(2,1)S(1)}, u32[]{:S(2)}, u32[]{:S(2)}) collective-permute-start(bf16[136,640]{1,0:T(8,128)(2,1)S(1)} %pack.3.refs_0_), channel_id=1, source_target_pairs={{0,8},{4,12},{8,0},{12,4},{16,24},{20,28},{24,16},{28,20},{1,9},{5... | collective-permute-start | bytes 522248 | tf_op jit(solution)/shard_map/ppermute | solution.py:419
  9.0 11.5 %collective-permute-start.18 = (bf16[136,640]{1,0:T(8,128)(2,1)S(1)}, bf16[136,640]{1,0:T(8,128)(2,1)S(1)}, u32[]{:S(2)}, u32[]{:S(2)}) collective-permute-start(bf16[136,640]{1,0:T(8,128)(2,1)S(1)} %pack.3.refs_0_), channel_id=1, source_target_pairs={{0,4},{4,0},{8,12},{12,8},{16,20},{20,16},{24,28},{28,24},{1,5},{5... | collective-permute-start | bytes 522248 | tf_op jit(solution)/shard_map/ppermute | solution.py:416
  10.4 42.3 %collective-permute-start.13 = (bf16[16,128,128]{2,1,0:T(8,128)(2,1)}, bf16[16,128,128]{2,1,0:T(8,128)(2,1)}, u32[]{:S(2)}, u32[]{:S(2)}) collective-permute-start(bf16[16,128,128]{2,1,0:T(8,128)(2,1)} %refs_0_.1), channel_id=1, source_target_pairs={{0,2},{1,3},{2,0},{3,1},{4,6},{5,7},{6,4},{7,5},{8,10},{9,11},{10,... | collective-permute-start | bytes 1572872 | tf_op jit(solution)/shard_map/ppermute | solution.py:422
  12.1 13.0 %collective-permute-start.1 = (bf16[136,640]{1,0:T(8,128)(2,1)S(1)}, bf16[136,640]{1,0:T(8,128)(2,1)S(1)}, u32[]{:S(2)}, u32[]{:S(2)}) collective-permute-start(bf16[136,640]{1,0:T(8,128)(2,1)S(1)} %pack.2.refs_0_.refs_8_), channel_id=1, source_target_pairs={{0,16},{4,20},{8,24},{12,28},{16,0},{20,4},{24,8},{28,12},{1,17},{... | collective-permute-start | bytes 522248 | tf_op jit(solution)/shard_map/ppermute | solution.py:419
  18.4 10.0 %collective-permute-start = (bf16[136,640]{1,0:T(8,128)(2,1)S(1)}, bf16[136,640]{1,0:T(8,128)(2,1)S(1)}, u32[]{:S(2)}, u32[]{:S(2)}) collective-permute-start(bf16[136,640]{1,0:T(8,128)(2,1)S(1)} %pack.2.refs_0_.refs_8_), channel_id=1, source_target_pairs={{0,8},{4,12},{8,0},{12,4},{16,24},{20,28},{24,16},{28,20},{1,9},{5... | collective-permute-start | bytes 522248 | tf_op jit(solution)/shard_map/ppermute | solution.py:419
  20.4 10.0 %collective-permute-start.20 = (bf16[136,640]{1,0:T(8,128)(2,1)S(1)}, bf16[136,640]{1,0:T(8,128)(2,1)S(1)}, u32[]{:S(2)}, u32[]{:S(2)}) collective-permute-start(bf16[136,640]{1,0:T(8,128)(2,1)S(1)} %collective-permute-done.16.refs_2_), channel_id=1, source_target_pairs={{0,4},{4,0},{8,12},{12,8},{16,20},{20,16},{24,28},{28,24},{1,5},{5... | collective-permute-start | bytes 522248 | tf_op jit(solution)/shard_map/ppermute | solution.py:416
  26.5 11.4 %collective-permute-start.21 = (bf16[136,640]{1,0:T(8,128)(2,1)S(1)}, bf16[136,640]{1,0:T(8,128)(2,1)S(1)}, u32[]{:S(2)}, u32[]{:S(2)}) collective-permute-start(bf16[136,640]{1,0:T(8,128)(2,1)S(1)} %collective-permute-done.17.refs_3_), channel_id=1, source_target_pairs={{0,4},{4,0},{8,12},{12,8},{16,20},{20,16},{24,28},{28,24},{1,5},{5... | collective-permute-start | bytes 522248 | tf_op jit(solution)/shard_map/ppermute | solution.py:416
  28.4 24.2 %collective-permute-start.3 = (bf16[136,640]{1,0:T(8,128)(2,1)S(1)}, bf16[136,640]{1,0:T(8,128)(2,1)S(1)}, u32[]{:S(2)}, u32[]{:S(2)}) collective-permute-start(bf16[136,640]{1,0:T(8,128)(2,1)S(1)} %pack.2.refs_0_.refs_8_), channel_id=1, source_target_pairs={{0,4},{4,0},{8,12},{12,8},{16,20},{20,16},{24,28},{28,24},{1,5},{5... | collective-permute-start | bytes 522248 | tf_op jit(solution)/shard_map/ppermute | solution.py:416
  30.5 22.2 %collective-permute-start.2 = (bf16[136,640]{1,0:T(8,128)(2,1)S(1)}, bf16[136,640]{1,0:T(8,128)(2,1)S(1)}, u32[]{:S(2)}, u32[]{:S(2)}) collective-permute-start(bf16[136,640]{1,0:T(8,128)(2,1)S(1)} %collective-permute-done.1.refs_2_.refs_10_), channel_id=1, source_target_pairs={{0,8},{4,12},{8,0},{12,4},{16,24},{20,28},{24,16},{28,20},{1,9},{5... | collective-permute-start | bytes 522248 | tf_op jit(solution)/shard_map/ppermute | solution.py:419
  34.2 19.1 %collective-permute-start.5 = (bf16[136,640]{1,0:T(8,128)(2,1)S(1)}, bf16[136,640]{1,0:T(8,128)(2,1)S(1)}, u32[]{:S(2)}, u32[]{:S(2)}) collective-permute-start(bf16[136,640]{1,0:T(8,128)(2,1)S(1)} %collective-permute-done.1.refs_2_.refs_10_), channel_id=1, source_target_pairs={{0,4},{4,0},{8,12},{12,8},{16,20},{20,16},{24,28},{28,24},{1,5},{5... | collective-permute-start | bytes 522248 | tf_op jit(solution)/shard_map/ppermute | solution.py:416
  37.9 17.3 %collective-permute-start.4 = (bf16[136,640]{1,0:T(8,128)(2,1)S(1)}, bf16[136,640]{1,0:T(8,128)(2,1)S(1)}, u32[]{:S(2)}, u32[]{:S(2)}) collective-permute-start(bf16[136,640]{1,0:T(8,128)(2,1)S(1)} %collective-permute-done.refs_1_.refs_9_), channel_id=1, source_target_pairs={{0,4},{4,0},{8,12},{12,8},{16,20},{20,16},{24,28},{28,24},{1,5},{5... | collective-permute-start | bytes 522248 | tf_op jit(solution)/shard_map/ppermute | solution.py:416
  52.6 17.3 %collective-permute-start.22 = (bf16[264,512]{1,0:T(8,128)(2,1)S(1)}, bf16[264,512]{1,0:T(8,128)(2,1)S(1)}, u32[]{:S(2)}, u32[]{:S(2)}) collective-permute-start(bf16[264,512]{1,0:T(8,128)(2,1)S(1)} %get-tuple-element.36), channel_id=1, source_target_pairs={{0,4},{4,0},{8,12},{12,8},{16,20},{20,16},{24,28},{28,24},{1,5},{5... | collective-permute-start | bytes 811016 | tf_op jit(solution)/shard_map/ppermute | solution.py:416
  52.7 31.2 %collective-permute-start.12 = (bf16[16,128,128]{2,1,0:T(8,128)(2,1)S(1)}, bf16[16,128,128]{2,1,0:T(8,128)(2,1)S(1)}, u32[]{:S(2)}, u32[]{:S(2)}) collective-permute-start(bf16[16,128,128]{2,1,0:T(8,128)(2,1)S(1)} %copy-done.18), channel_id=1, source_target_pairs={{0,1},{1,0},{2,3},{3,2},{4,5},{5,4},{6,7},{7,6},{8,9},{9,8},{10,11... | collective-permute-start | bytes 1572872 | tf_op jit(solution)/shard_map/ppermute | solution.py:422
  52.8 36.4 %collective-permute-start.14 = (bf16[16,128,128]{2,1,0:T(8,128)(2,1)}, bf16[16,128,128]{2,1,0:T(8,128)(2,1)S(1)}, u32[]{:S(2)}, u32[]{:S(2)}) collective-permute-start(bf16[16,128,128]{2,1,0:T(8,128)(2,1)} %collective-permute-done.13.refs_2_), channel_id=1, source_target_pairs={{0,1},{1,0},{2,3},{3,2},{4,5},{5,4},{6,7},{7,6},{8,9},{9,8},{10,11... | collective-permute-start | bytes 1572872 | tf_op jit(solution)/shard_map/ppermute | solution.py:422
  53.3 12.4 %collective-permute-start.6 = (bf16[136,640]{1,0:T(8,128)(2,1)S(1)}, bf16[136,640]{1,0:T(8,128)(2,1)S(1)}, u32[]{:S(2)}, u32[]{:S(2)}) collective-permute-start(bf16[136,640]{1,0:T(8,128)(2,1)S(1)} %collective-permute-done.2.refs_3_.refs_11_), channel_id=1, source_target_pairs={{0,4},{4,0},{8,12},{12,8},{16,20},{20,16},{24,28},{28,24},{1,5},{5... | collective-permute-start | bytes 522248 | tf_op jit(solution)/shard_map/ppermute | solution.py:416
  55.3 17.7 %collective-permute-start.23 = (bf16[256,512]{1,0:T(8,128)(2,1)S(1)}, bf16[256,512]{1,0:T(8,128)(2,1)S(1)}, u32[]{:S(2)}, u32[]{:S(2)}) collective-permute-start(bf16[256,512]{1,0:T(8,128)(2,1)S(1)} %get-tuple-element.40), channel_id=1, source_target_pairs={{0,4},{4,0},{8,12},{12,8},{16,20},{20,16},{24,28},{28,24},{1,5},{5... | collective-permute-start | bytes 786440 | tf_op jit(solution)/shard_map/ppermute | solution.py:416
  69.9 11.9 %collective-permute-start.8 = (bf16[256,512]{1,0:T(8,128)(2,1)S(1)}, bf16[256,512]{1,0:T(8,128)(2,1)S(1)}, u32[]{:S(2)}, u32[]{:S(2)}) collective-permute-start(bf16[256,512]{1,0:T(8,128)(2,1)S(1)} %get-tuple-element.29), channel_id=1, source_target_pairs={{0,4},{4,0},{8,12},{12,8},{16,20},{20,16},{24,28},{28,24},{1,5},{5... | collective-permute-start | bytes 786440 | tf_op jit(solution)/shard_map/ppermute | solution.py:416
  73.9 12.0 %collective-permute-start.24 = (bf16[136,512]{1,0:T(8,128)(2,1)S(1)}, bf16[136,512]{1,0:T(8,128)(2,1)S(1)}, u32[]{:S(2)}, u32[]{:S(2)}) collective-permute-start(bf16[136,512]{1,0:T(8,128)(2,1)S(1)} %get-tuple-element.43), channel_id=1, source_target_pairs={{0,8},{4,12},{8,0},{12,4},{16,24},{20,28},{24,16},{28,20},{1,9},{5... | collective-permute-start | bytes 417800 | tf_op jit(solution)/shard_map/ppermute | solution.py:419
  79.0 23.7 %collective-permute-start.25 = (bf16[136,512]{1,0:T(8,128)(2,1)}, bf16[136,512]{1,0:T(8,128)(2,1)}, u32[]{:S(2)}, u32[]{:S(2)}) collective-permute-start(bf16[136,512]{1,0:T(8,128)(2,1)} %get-tuple-element.44), channel_id=1, source_target_pairs={{0,16},{4,20},{8,24},{12,28},{16,0},{20,4},{24,8},{28,12},{1,17},{... | collective-permute-start | bytes 417800 | tf_op jit(solution)/shard_map/ppermute | solution.py:419
  81.8 20.9 %collective-permute-start.26 = (bf16[136,512]{1,0:T(8,128)(2,1)}, bf16[136,512]{1,0:T(8,128)(2,1)}, u32[]{:S(2)}, u32[]{:S(2)}) collective-permute-start(bf16[136,512]{1,0:T(8,128)(2,1)} %get-tuple-element.45), channel_id=1, source_target_pairs={{0,24},{4,28},{8,16},{12,20},{16,8},{20,12},{24,0},{28,4},{1,25},{... | collective-permute-start | bytes 417800 | tf_op jit(solution)/shard_map/ppermute | solution.py:419
  84.7 20.2 %collective-permute-start.9 = (bf16[136,512]{1,0:T(8,128)(2,1)}, bf16[136,512]{1,0:T(8,128)(2,1)}, u32[]{:S(2)}, u32[]{:S(2)}) collective-permute-start(bf16[136,512]{1,0:T(8,128)(2,1)} %get-tuple-element.32), channel_id=1, source_target_pairs={{0,8},{4,12},{8,0},{12,4},{16,24},{20,28},{24,16},{28,20},{1,9},{5... | collective-permute-start | bytes 417800 | tf_op jit(solution)/shard_map/ppermute | solution.py:419
  86.5 18.4 %collective-permute-start.10 = (bf16[136,512]{1,0:T(8,128)(2,1)}, bf16[136,512]{1,0:T(8,128)(2,1)}, u32[]{:S(2)}, u32[]{:S(2)}) collective-permute-start(bf16[136,512]{1,0:T(8,128)(2,1)} %get-tuple-element.33), channel_id=1, source_target_pairs={{0,16},{4,20},{8,24},{12,28},{16,0},{20,4},{24,8},{28,12},{1,17},{... | collective-permute-start | bytes 417800 | tf_op jit(solution)/shard_map/ppermute | solution.py:419
  90.0 14.9 %collective-permute-start.11 = (bf16[136,512]{1,0:T(8,128)(2,1)}, bf16[136,512]{1,0:T(8,128)(2,1)}, u32[]{:S(2)}, u32[]{:S(2)}) collective-permute-start(bf16[136,512]{1,0:T(8,128)(2,1)} %get-tuple-element.34), channel_id=1, source_target_pairs={{0,24},{4,28},{8,16},{12,20},{16,8},{20,12},{24,0},{28,4},{1,25},{... | collective-permute-start | bytes 417800 | tf_op jit(solution)/shard_map/ppermute | solution.py:419
  (39 other events, 250.5 us)

commit v2 on v0

--- a/solution.py
+++ b/solution.py
@@ -1,11 +1,638 @@
+import functools
+
 import jax
 import jax.numpy as jnp
 from jax import lax
+from jax.experimental import pallas as pl
+from jax.experimental.pallas import tpu as pltpu
 from jax.sharding import PartitionSpec as P
 
 KV = 512
 QK_DIM = 192
 BLOCK = 64
+VMEM_LIMIT = 16 * 1024 * 1024
+PACK_LIMIT = 63_000_000
+ATTEND_LIMIT = 20 * 1024 * 1024
+TABLE = 32
+GATHER_LIMIT = 16 * 1024 * 1024
+FAR = (1, 3)
+NEAR = (0, 2)
+
+CHUNKS = 2
+PAIRS = 8
+HEADS = 16
+ROWS = PAIRS * HEADS
+EXTRA = 8
+SENT = ROWS + EXTRA
+WIDE = 640
+SLOTS = 8
+LANES = 128
+
+
+def call(body, limit=VMEM_LIMIT, **kwargs):
+    return pl.pallas_call(
+        body,
+        compiler_params=pltpu.CompilerParams(vmem_limit_bytes=limit),
+        **kwargs,
+    )
+
+
+def after(value, *earlier):
+    return lax.optimization_barrier((value, *earlier))[0]
+
+
+def whole(shape):
+    return pl.BlockSpec(shape, lambda *_: (0,) * len(shape))
+
+
+def pack_kernel(q_hbm, iq_hbm, iw_hbm, out0_ref, out1_ref, both_ref, q_ref, iq_ref, iw_ref, sems):
+    small = pltpu.make_async_copy(iw_hbm, iw_ref, sems.at[4])
+    small.start()
+    copies = []
+    for chunk in range(CHUNKS):
+        requests = pl.ds(2 * chunk, 2)
+        copies.append(
+            (
+                pltpu.make_async_copy(
+                    q_hbm.at[:, requests], q_ref.at[chunk], sems.at[2 * chunk]
+                ),
+                pltpu.make_async_copy(
+                    iq_hbm.at[:, requests], iq_ref.at[chunk], sems.at[2 * chunk + 1]
+                ),
+            )
+        )
+        for copy in copies[-1]:
+            copy.start()
+    small.wait()
+    for chunk, out_ref in enumerate((out0_ref, out1_ref)):
+        for copy in copies[chunk]:
+            copy.wait()
+        rows = []
+        for local in range(2):
+            for step in range(4):
+                row = (local * 4 + step) * HEADS
+                query = q_ref[chunk, step, local]
+                index_query = iq_ref[chunk, step, local]
+                halves = jnp.concatenate([index_query[:, :64], index_query[:, 64:]], axis=0)
+                out_ref[row : row + HEADS, :512] = query[:, :512]
+                out_ref[row : row + HEADS, 512:] = jnp.concatenate(
+                    [query[:, 512:], halves], axis=1
+                )
+                request = 2 * chunk + local
+                rows.append(iw_ref[step, request : request + 1, :].astype(jnp.float32))
+        weights = jnp.concatenate(rows, axis=0)
+        weights = jnp.concatenate([weights, jnp.zeros((PAIRS, LANES - 8), jnp.float32)], axis=1)
+        out_ref[ROWS:, :LANES] = weights.astype(jnp.bfloat16)
+        out_ref[ROWS:, LANES:] = jnp.zeros((EXTRA, WIDE - LANES), jnp.bfloat16)
+        both_ref[chunk * SENT : (chunk + 1) * SENT, :] = out_ref[...]
+
+
+def pack(queries, index_queries, index_weights):
+    bf16 = jnp.bfloat16
+    return call(
+        pack_kernel,
+        limit=PACK_LIMIT,
+        in_specs=[pl.BlockSpec(memory_space=pltpu.HBM)] * 3,
+        out_shape=[jax.ShapeDtypeStruct((SENT, WIDE), bf16)] * 2
+        + [jax.ShapeDtypeStruct((2 * SENT, WIDE), bf16)],
+        scratch_shapes=[
+            pltpu.VMEM((2, 4, 2, HEADS, 576), bf16),
+            pltpu.VMEM((2, 4, 2, 8, 128), bf16),
+            pltpu.VMEM((4, 4, 8), bf16),
+            pltpu.SemaphoreType.DMA((5,)),
+        ],
+        name="pack",
+    )(queries, index_queries, index_weights)
+
+
+def pair_up_kernel(first_ref, second_ref, out_ref):
+    out_ref[:SENT, :] = first_ref[...]
+    out_ref[SENT:, :] = second_ref[...]
+
+
+def pair_up(first, second):
+    return call(
+        pair_up_kernel,
+        out_shape=jax.ShapeDtypeStruct((2 * SENT, WIDE), jnp.bfloat16),
+        name="pair_up",
+    )(first, second)
+
+
+def plan_kernel(selection_ref, counts_ref, lengths_ref, out_ref):
+    shard = lax.axis_index("ctx")
+    row = lax.broadcasted_iota(jnp.int32, (16, 1), 0)
+    count = jnp.zeros((16, 1), jnp.int32)
+    limit = jnp.zeros((16, 1), jnp.int32)
+    for step in range(4):
+        for request in range(4):
+            here = row == step * 4 + request
+            count = jnp.where(here, counts_ref[step, request], count)
+            limit = jnp.where(here, lengths_ref[request] + step - shard * 2048, limit)
+    selection = jnp.concatenate([selection_ref[step] for step in range(4)], axis=0)
+    local = selection - shard * (2048 // BLOCK)
+    slot = lax.broadcasted_iota(jnp.int32, (16, 32), 1)
+    owned = (local >= 0) & (local < 2048 // BLOCK) & (slot < count)
+    before = (
+        lax.broadcasted_iota(jnp.int32, (32, 32), 0) < lax.broadcasted_iota(jnp.int32, (32, 32), 1)
+    ).astype(jnp.float32)
+    lane = lax.broadcasted_iota(jnp.int32, (16, LANES), 1)
+    table = jnp.full((16, LANES), -1, jnp.int32)
+    most = jnp.zeros((16, 1), jnp.int32)
+    for parity in range(2):
+        mine = owned & (local % 2 == parity)
+        mine_f = jnp.where(mine, 1.0, 0.0)
+        rank = jnp.dot(mine_f, before, preferred_element_type=jnp.float32).astype(jnp.int32)
+        for place in range(SLOTS):
+            chosen = mine & (rank == place)
+            found = jnp.sum(jnp.where(chosen, local // 2 + 1, 0), axis=1, keepdims=True) - 1
+            table = jnp.where(lane == parity * SLOTS + place, found, table)
+        most = jnp.maximum(most, jnp.sum(mine_f, axis=1, keepdims=True).astype(jnp.int32))
+    table = jnp.where(lane == 16, most, table)
+    table = jnp.where(lane == 17, limit, table)
+    out_ref[...] = table[:, :TABLE]
+
+
+def plan(selection, counts, lengths):
+    smem = pl.BlockSpec(memory_space=pltpu.SMEM)
+    return call(
+        plan_kernel,
+        in_specs=[pl.BlockSpec(), smem, smem],
+        out_shape=jax.ShapeDtypeStruct((16, TABLE), jnp.int32),
+        name="plan",
+    )(selection, counts, lengths)
+
+
+def split3(value):
+    high = value.astype(jnp.bfloat16)
+    rest = value - high.astype(jnp.float32)
+    middle = rest.astype(jnp.bfloat16)
+    low = (rest - middle.astype(jnp.float32)).astype(jnp.bfloat16)
+    return high, middle, low
+
+
+def store_stats(out_ref, row, stats):
+    turned = stats.T[:PAIRS]
+    for place, part in enumerate(split3(turned)):
+        out_ref[row : row + PAIRS, place * LANES : (place + 1) * LANES] = part
+    out_ref[row : row + PAIRS, 3 * LANES :] = jnp.zeros((PAIRS, LANES), jnp.bfloat16)
+
+
+def load_stats(in_ref, row):
+    parts = [
+        in_ref[row : row + PAIRS, place * LANES : (place + 1) * LANES].astype(jnp.float32)
+        for place in range(3)
+    ]
+    turned = (parts[0] + parts[1]) + parts[2]
+    return jnp.concatenate([turned, jnp.zeros((LANES - PAIRS, LANES), jnp.float32)], axis=0).T
+
+
+def gather_kernel(chunk, table_ref, latent_hbm, out_ref, latent_ref, sems):
+    copies = []
+    for local in range(2):
+        for part in range(4):
+            rows = pl.ds(part * 144, 144)
+            copies.append(
+                pltpu.make_async_copy(
+                    latent_hbm.at[2 * chunk + local, rows],
+                    latent_ref.at[local, rows],
+                    sems.at[local * 4 + part],
+                )
+            )
+    for copy in copies:
+        copy.start()
+    in_even = lax.broadcasted_iota(jnp.int32, (576, LANES), 1) < BLOCK
+    for local in range(2):
+        request = 2 * chunk + local
+        for copy in copies[local * 4 : local * 4 + 4]:
+            copy.wait()
+
+        def tile(row, place, local=local):
+            start = pl.multiple_of(jnp.maximum(table_ref[row, place], 0) * LANES, LANES)
+            return latent_ref[local, :, pl.ds(start, LANES)]
+
+        def fill(places, request=request, local=local, tile=tile):
+            for step in range(4):
+                row = step * 4 + request
+                for place in places:
+                    out_ref[local * 4 + step, :, place * LANES : (place + 1) * LANES] = jnp.where(
+                        in_even, tile(row, place), tile(row, SLOTS + place)
+                    )
+
+        fill(range(4))
+
+        @pl.when(most_of(table_ref, request) > 4)
+        def _(fill=fill):
+            fill(range(4, SLOTS))
+
+
+def most_of(table_ref, request):
+    most = table_ref[request, 16]
+    for step in range(1, 4):
+        most = jnp.maximum(most, table_ref[step * 4 + request, 16])
+    return most
+
+
+def gather(chunk, table, latents_t):
+    bf16 = jnp.bfloat16
+    return call(
+        functools.partial(gather_kernel, chunk),
+        limit=GATHER_LIMIT,
+        in_specs=[pl.BlockSpec(memory_space=pltpu.SMEM), pl.BlockSpec(memory_space=pltpu.HBM)],
+        out_shape=jax.ShapeDtypeStruct((PAIRS, 576, SLOTS * LANES), bf16),
+        scratch_shapes=[pltpu.VMEM((2, 576, 2048), bf16), pltpu.SemaphoreType.DMA((8,))],
+        name="gather_blocks",
+    )(table, latents_t)
+
+
+def attend_kernel(chunk, offsets, table_ref, *refs):
+    q_refs = refs[:8]
+    block_ref = refs[8]
+    own_a, own_b, send_a, send_b, stats_ref, score_ref, weight_ref = refs[9:]
+    lane = lax.broadcasted_iota(jnp.int32, (LANES, LANES), 1)
+    position = lax.broadcasted_iota(jnp.int32, (1, LANES), 1)
+    stats_ref[...] = jnp.zeros((LANES, LANES), jnp.float32)
+
+    def work(local, request, tiles):
+        width = tiles * LANES
+        for step in range(4):
+            row = step * 4 + request
+            pair = local * 4 + step
+            query = jnp.concatenate(
+                [
+                    r[at + pair * HEADS : at + (pair + 1) * HEADS, :576]
+                    for r, at in zip(q_refs, offsets)
+                ],
+                axis=0,
+            )
+            bias = []
+            for place in range(tiles):
+                at = jnp.where(
+                    position < BLOCK, table_ref[row, place], table_ref[row, SLOTS + place]
+                )
+                usable = (at >= 0) & (at * LANES + position <= table_ref[row, 17])
+                bias.append(jnp.where(usable, 0.0, -1e30))
+            scores = jnp.dot(
+                query, block_ref[pair, :, :width], preferred_element_type=jnp.float32
+            )
+            score_ref[step, :, :width] = scores * (QK_DIM**-0.5) + jnp.concatenate(bias, axis=1)
+        scales = []
+        for step in range(4):
+            scores = score_ref[step, :, :width]
+            peak = jnp.maximum(jnp.max(scores, axis=1, keepdims=True), -1e29)
+            weights = jnp.exp(scores - peak)
+            total = jnp.maximum(jnp.sum(weights, axis=1, keepdims=True), 1e-30)
+            weight_ref[step, :, :width] = weights.astype(jnp.bfloat16)
+            scales.append(1.0 / total)
+            stats_ref[...] = jnp.where(
+                lane == local * 4 + step, peak + jnp.log(total), stats_ref[...]
+            )
+        for step in range(4):
+            mixed = lax.dot_general(
+                weight_ref[step, :, :width],
+                block_ref[local * 4 + step, :KV, :width],
+                (((1,), (1,)), ((), ())),
+                preferred_element_type=jnp.float32,
+            )
+            mixed = (mixed * scales[step]).astype(jnp.bfloat16)
+            for across, (out_a, out_b) in enumerate(((own_a, own_b), (send_a, send_b))):
+                for out, members in ((out_a, FAR), (out_b, NEAR)):
+                    for place, member in enumerate(members):
+                        source = (across * 4 + member) * HEADS
+                        row = place * ROWS + (local * 4 + step) * HEADS
+                        out[row : row + HEADS, :] = mixed[source : source + HEADS]
+
+    for local in range(2):
+        request = 2 * chunk + local
+        most = most_of(table_ref, request)
+
+        @pl.when(most <= 4)
+        def _(local=local, request=request):
+            work(local, request, 4)
+
+        @pl.when(most > 4)
+        def _(local=local, request=request):
+            work(local, request, 8)
+
+    store_stats(send_a, 2 * ROWS, stats_ref[...])
+
+
+def attend(chunk, table, gathered_queries, blocks):
+    bf16 = jnp.bfloat16
+    return call(
+        functools.partial(attend_kernel, chunk, tuple(at for _, at in gathered_queries)),
+        limit=ATTEND_LIMIT,
+        in_specs=[pl.BlockSpec(memory_space=pltpu.SMEM)] + [pl.BlockSpec()] * 9,
+        out_shape=[
+            jax.ShapeDtypeStruct((2 * ROWS, KV), bf16),
+            jax.ShapeDtypeStruct((2 * ROWS, KV), bf16),
+            jax.ShapeDtypeStruct((2 * ROWS + EXTRA, KV), bf16),
+            jax.ShapeDtypeStruct((2 * ROWS, KV), bf16),
+            jax.ShapeDtypeStruct((LANES, LANES), jnp.float32),
+        ],
+        scratch_shapes=[
+            pltpu.VMEM((4, LANES, SLOTS * LANES), jnp.float32),
+            pltpu.VMEM((4, LANES, SLOTS * LANES), bf16),
+        ],
+        name="attend",
+    )(table, *(array for array, _ in gathered_queries), blocks)
+
+
+def joined(own_ref, other_ref, place, weight_own, weight_other):
+    for pair in range(PAIRS):
+        row = place * ROWS + pair * HEADS
+        own = own_ref[row : row + HEADS, :].astype(jnp.float32)
+        other = other_ref[row : row + HEADS, :].astype(jnp.float32)
+        yield pair, (
+            own * weight_own[:, pair : pair + 1] + other * weight_other[:, pair : pair + 1]
+        )
+
+
+def weigh(own, other):
+    peak = jnp.maximum(own, other)
+    own, other = jnp.exp(own - peak), jnp.exp(other - peak)
+    total = own + other
+    return own / total, other / total, peak + jnp.log(total)
+
+
+def rows_of(member):
+    return slice(member * HEADS, (member + 1) * HEADS)
+
+
+def join_far_kernel(own_ref, other_ref, stats_ref, out_ref, weight_ref, lse_ref):
+    own, other, lse = weigh(stats_ref[:64], load_stats(other_ref, 2 * ROWS)[64:])
+    lse = jnp.concatenate([lse, jnp.zeros((64, LANES), jnp.float32)], axis=0)
+    weight_ref[0] = own
+    weight_ref[1] = other
+    lse_ref[...] = lse
+    for place, member in enumerate(FAR):
+        part = rows_of(member)
+        for pair, rows in joined(own_ref, other_ref, place, own[part], other[part]):
+            row = place * ROWS + pair * HEADS
+            out_ref[row : row + HEADS, :] = rows.astype(jnp.bfloat16)
+    store_stats(out_ref, 2 * ROWS, lse)
+
+
+def join_far(own, other, stats):
+    return call(
+        join_far_kernel,
+        out_shape=[
+            jax.ShapeDtypeStruct((2 * ROWS + EXTRA, KV), jnp.bfloat16),
+            jax.ShapeDtypeStruct((2, 64, LANES), jnp.float32),
+            jax.ShapeDtypeStruct((LANES, LANES), jnp.float32),
+        ],
+        name="join_far",
+    )(own, other, stats)
+
+
+def join_near_kernel(own_ref, other_ref, weight_ref, out_ref):
+    for place, member in enumerate(NEAR):
+        part = rows_of(member)
+        weights = weight_ref[0, part], weight_ref[1, part]
+        for pair, rows in joined(own_ref, other_ref, place, *weights):
+            row = place * ROWS + pair * HEADS
+            out_ref[row : row + HEADS, :] = rows
+
+
+def join_near(own, other, weights):
+    return call(
+        join_near_kernel,
+        out_shape=jax.ShapeDtypeStruct((2 * ROWS, KV), jnp.float32),
+        name="join_near",
+    )(own, other, weights)
+
+
+def join_line_kernel(own_ref, other_ref, lse_ref, out_ref, mine_ref, stats_ref):
+    own = jnp.concatenate([lse_ref[rows_of(member)] for member in NEAR], axis=0)
+    theirs = load_stats(other_ref, 2 * ROWS)
+    other = jnp.concatenate([theirs[rows_of(member)] for member in FAR], axis=0)
+    own, other, lse = weigh(own, other)
+    lse = jnp.concatenate([lse, jnp.zeros((LANES - 2 * HEADS, LANES), jnp.float32)], axis=0)
+    part = rows_of(1)
+    for pair, rows in joined(own_ref, other_ref, 1, own[part], other[part]):
+        out_ref[pair * HEADS : (pair + 1) * HEADS, :] = rows.astype(jnp.bfloat16)
+    store_stats(out_ref, ROWS, lse)
+    part = rows_of(0)
+    for pair, rows in joined(own_ref, other_ref, 0, own[part], other[part]):
+        mine_ref[pair * HEADS : (pair + 1) * HEADS, :] = rows
+    stats_ref[...] = lse
+
+
+def join_line(own, other, lse):
+    return call(
+        join_line_kernel,
+        out_shape=[
+            jax.ShapeDtypeStruct((SENT, KV), jnp.bfloat16),
+            jax.ShapeDtypeStruct((ROWS, KV), jnp.float32),
+            jax.ShapeDtypeStruct((LANES, LANES), jnp.float32),
+        ],
+        name="join_line",
+    )(own, other, lse)
+
+
+def finish_kernel(stats_ref, own_ref, other_ref, up_ref, *rest):
+    out_ref, rows_ref, lifted_ref = rest[-3:]
+    own, other, _ = weigh(stats_ref[:HEADS], load_stats(other_ref, ROWS)[rows_of(1)])
+    for pair, rows in joined(own_ref, other_ref, 0, own, other):
+        part = slice(pair * HEADS, (pair + 1) * HEADS)
+        for tile in range(4):
+            rows_ref[tile, part, :] = rows[:, tile * LANES : (tile + 1) * LANES]
+    for head in range(HEADS):
+        attended = jnp.concatenate(
+            [rows_ref[tile, pl.ds(head, PAIRS, stride=HEADS), :] for tile in range(4)], axis=1
+        ).astype(jnp.bfloat16)
+        lifted_ref[pl.ds(head, PAIRS, stride=HEADS), :] = jnp.dot(
+            attended, up_ref[head], preferred_element_type=jnp.float32
+        )
+    for step in range(4):
+        for local in range(2):
+            row = (local * 4 + step) * HEADS
+            out_ref[step, local] = lifted_ref[row : row + HEADS, :].astype(jnp.bfloat16)
+
+
+def finish(chunk, stats, own, other, up, before):
+    specs = [whole((LANES, LANES)), whole((ROWS, KV)), whole((SENT, KV))]
+    specs.append(whole((HEADS, KV, 128)))
+    args = [stats, own, other, up]
+    aliases = {}
+    if before is not None:
+        specs.append(pl.BlockSpec(memory_space=pl.ANY))
+        args.append(before)
+        aliases = {len(args) - 1: 0}
+    return call(
+        finish_kernel,
+        grid=(1,),
+        in_specs=specs,
+        out_specs=pl.BlockSpec((4, 2, HEADS, 128), lambda _: (0, chunk, 0, 0)),
+        out_shape=jax.ShapeDtypeStruct((4, 4, HEADS, 128), jnp.bfloat16),
+        scratch_shapes=[
+            pltpu.VMEM((4, ROWS, LANES), jnp.float32),
+            pltpu.VMEM((ROWS, 128), jnp.float32),
+        ],
+        input_output_aliases=aliases,
+        name="finish",
+    )(*args)
+
+
+def assemble_kernel(_, *refs):
+    out_ref = refs[-1]
+    own = lax.axis_index("req")
+    for relative, ref in enumerate(refs[:-1]):
+        start = pl.multiple_of((own ^ relative) * 128, 128)
+        out_ref[:, pl.ds(start, 128), :] = ref[...]
+
+
+def assemble(earlier, pieces):
+    return call(
+        assemble_kernel,
+        in_specs=[pl.BlockSpec(memory_space=pl.ANY)] + [pl.BlockSpec()] * 4,
+        out_shape=jax.ShapeDtypeStruct((HEADS, KV, 128), jnp.bfloat16),
+        name="assemble_up",
+    )(earlier, *pieces)
+
+
+def index_kernel(offsets, table_ref, *refs):
+    arrays = refs[:16]
+    key_ref, out_ref = refs[16:]
+    request = pl.program_id(0)
+    local = request % 2
+    lane = lax.broadcasted_iota(jnp.int32, (64, LANES), 1)
+
+    def work(members):
+        columns = []
+        for r, at in members:
+            rows = r[at + ROWS : at + SENT, :LANES].astype(jnp.float32)
+            rows = jnp.concatenate([rows, jnp.zeros((LANES - PAIRS, LANES), jnp.float32)], axis=0)
+            columns.append(rows.T[:8])
+        columns = jnp.concatenate(columns, axis=0)
+        query_rows, weight_rows = [], []
+        for step in range(4):
+            pair = local * 4 + step
+            tail = jnp.concatenate(
+                [r[pl.ds(at + pl.multiple_of(pair * HEADS, HEADS), HEADS), 512:] for r, at in members],
+                axis=0,
+            )
+            tail = tail.astype(jnp.float32).reshape(8, 2, 8, LANES)
+            first = tail[:, 0].reshape(64, LANES)
+            second = tail[:, 1].reshape(64, LANES)
+            query_rows.append(jnp.concatenate([first[:, 64:], second[:, 64:]], axis=1))
+            weight_rows.append(
+                jnp.sum(jnp.where(lane == pair, columns, 0.0), axis=1, keepdims=True)
+            )
+        queries = jnp.concatenate(query_rows, axis=0).astype(jnp.bfloat16)
+        for part in range(4):
+            at = slice(part * 512, (part + 1) * 512)
+            products = lax.dot_general(
+                queries,
+                key_ref[0, at, :],
+                (((1,), (1,)), ((), ())),
+                preferred_element_type=jnp.float32,
+            )
+            position = part * 512 + lax.broadcasted_iota(jnp.int32, (1, 512), 1)
+            for step in range(4):
+                mine = jnp.maximum(products[step * 64 : (step + 1) * 64], 0.0)
+                summed = jnp.sum(mine * weight_rows[step], axis=0, keepdims=True)
+                out_ref[step, pl.ds(request, 1), at] = jnp.where(
+                    position <= table_ref[step * 4 + request, 17], summed, 0.0
+                )
+
+    for chunk in range(CHUNKS):
+
+        @pl.when(request // 2 == chunk)
+        def _(members=list(zip(arrays[8 * chunk : 8 * chunk + 8], offsets[8 * chunk : 8 * chunk + 8]))):
+            work(members)
+
+
+def index_rows(table, gathered, index_keys):
+    members = [*gathered[0], *gathered[1]]
+    return call(
+        functools.partial(index_kernel, tuple(at for _, at in members)),
+        grid_spec=pltpu.PrefetchScalarGridSpec(
+            num_scalar_prefetch=1,
+            grid=(4,),
+            in_specs=[whole(array.shape) for array, _ in members]
+            + [pl.BlockSpec((1, 2048, 128), lambda i, _: (i, 0, 0))],
+            out_specs=whole((4, 4, 2048)),
+        ),
+        out_shape=jax.ShapeDtypeStruct((4, 4, 2048), jnp.float32),
+        name="index_scores",
+    )(table, *(array for array, _ in members), index_keys)
+
+
+def fast(
+    latents,
+    index_keys,
+    queries,
+    index_queries,
+    index_weights,
+    value_up_weight,
+    selection,
+    counts,
+    lengths,
+):
+    def across_x(value):
+        return lax.ppermute(value, "ctx", [(i, i ^ 1) for i in range(8)])
+
+    def across_z(value, distance):
+        return lax.ppermute(value, "ctx", [(i, i ^ (2 * distance)) for i in range(8)])
+
+    def across_req(value, distance):
+        return lax.ppermute(value, "req", [(i, i ^ distance) for i in range(4)])
+
+    own0, own1, both = pack(queries, index_queries, index_weights)
+    table = plan(after(selection, own0), counts, lengths)
+    latents_t = jnp.transpose(latents, (0, 2, 1))
+
+    x0 = across_x(both)
+    z2c0, z1c0 = across_z(own0, 2), across_z(own0, 1)
+
+    round1 = (x0, z2c0, z1c0, table)
+    x12 = across_x(pair_up(after(z1c0, *round1), z2c0))
+    z3c0 = across_z(after(z2c0, *round1), 1)
+    z2c1 = across_z(after(own1, *round1), 2)
+    blocks0 = gather(0, after(table, *round1), latents_t)
+
+    round2 = (x12, z3c0, z2c1, blocks0)
+    x32 = across_x(pair_up(after(z3c0, *round2), z2c1))
+    z1c1 = across_z(after(own1, *round2), 1)
+    z3c1 = across_z(after(z2c1, *round2), 1)
+    blocks1 = gather(1, after(table, *round2), latents_t)
+    up_y = across_req(after(value_up_weight, *round2), 2)
+
+    round3 = (x32, z1c1, z3c1, blocks1)
+    last = pair_up(after(z1c1, *round3), z3c1)
+    x13 = across_x(last)
+    up_core = across_req(after(value_up_weight, *round3), 1)
+    up_both = across_req(after(up_y, *round3), 1)
+    gathered = [
+        [(own0, 0), (z1c0, 0), (z2c0, 0), (z3c0, 0), (x0, 0), (x12, 0), (x12, SENT), (x32, 0)],
+        [(own1, 0), (z1c1, 0), (z2c1, 0), (z3c1, 0), (x0, SENT), (x13, 0), (x32, SENT), (x13, SENT)],
+    ]
+
+    own_a0, own_b0, send_a0, send_b0, stats0 = attend(
+        0, after(table, last), gathered[0], blocks0
+    )
+    xa0, xb0 = across_x(send_a0), across_x(send_b0)
+    own_a1, own_b1, send_a1, send_b1, stats1 = attend(
+        1, after(table, stats0), gathered[1], blocks1
+    )
+    xa1, xb1 = across_x(send_a1), across_x(send_b1)
+
+    far0, weights0, lse0 = join_far(own_a0, after(xa0, stats1), stats0)
+    l0 = across_z(far0, 1)
+    near0 = join_near(own_b0, xb0, weights0)
+    index_scores = index_rows(after(table, far0), gathered, index_keys)
+    up = assemble(index_scores, [value_up_weight, up_core, up_y, up_both])
+
+    message0, mine0, stats0 = join_line(near0, l0, lse0)
+    f0 = across_z(message0, 2)
+    far1, weights1, lse1 = join_far(own_a1, xa1, stats1)
+    l1 = across_z(far1, 1)
+    near1 = join_near(own_b1, xb1, weights1)
+    message1, mine1, stats1 = join_line(near1, l1, lse1)
+    f1 = across_z(message1, 2)
+    head_values = finish(0, stats0, mine0, f0, up, None)
+    head_values = finish(1, stats1, mine1, f1, up, head_values)
+    return (head_values, index_scores)
 
 
 def compact_slots(owned_slot, local_block, capacity):
@@ -119,8 +746,10 @@
         P(None, "req"),
         P("req"),
     )
+    sizes = dict(mesh.shape)
+    plan = fast if (sizes["ctx"], sizes["req"]) == (8, 4) else per_device
     return jax.shard_map(
-        per_device,
+        plan,
         mesh=mesh,
         in_specs=placed,
         out_specs=(P(None, "req", "ctx", None), P(None, "req", "ctx")),

time: 270 us -> 83.4 us (0.31)
  waiting for transfers between devices: 113 us -> 24.7 us
  blocking collectives: 77.2 us -> 0 us
  local copies, waits for them, and re-layouts: 33.4 us -> 6.63 us
  Pallas kernels: 0 us -> 26.5 us
  starting transfers between devices: 0.16 us -> 24.5 us
  matrix products: 19.5 us -> 0 us
  between operations: 16 us -> 0.79 us
  other arithmetic: 9.22 us -> 0 us
    unnamed x6 -> x0, waiting for transfers between devices: 82.9 us -> none
    all_gather x2 -> x0, blocking collectives: 58 us -> none  [the longest x1 30.5 us: per_device(): lax.all_gather(index_weights, 'ctx', axis=2, tiled=True)]
    all_gather x2 -> x0, waiting for transfers between devices: 30.5 us -> none  [the longest x1 30.5 us: per_device(): lax.all_gather(queries, 'ctx', axis=2, tiled=True)]
    pallas_call x0 -> x19, Pallas kernels: none -> 26.5 us  [the longest x2 8.55 us: gather(): call(functools.partial(gather_kernel, chunk), limit=GATHER_LIMIT, in_spec...]
    ppermute x0 -> x21, waiting for transfers between devices: none -> 24.7 us  [the longest x8 17.8 us: across_x(): return lax.ppermute(value, 'ctx', [(i, i ^ 1) for i in range(8)])]
    ppermute x0 -> x21, starting transfers between devices: none -> 24.5 us  [the longest x10 12.9 us: across_z(): return lax.ppermute(value, 'ctx', [(i, i ^ 2 * distance) for i in range(8)])]
    dot_general x5 -> x0, matrix products: 19.5 us -> none  [the longest x1 7.72 us: per_device(): jnp.einsum('srht,srtk->srhk', exp_weights.astype(jnp.bfloat16), gathered[...]
    pmax x1 -> x0, blocking collectives: 19.2 us -> none  [per_device(): global_peak = lax.pmax(peak_score, 'ctx')]
  transfers between devices with their start and end apart: 4 -> 21, of which waited for: 2 -> 10; matrix products, arithmetic and copies ran while one was open for 17% -> 0% of each run, Pallas kernels for 0% -> 28%
where the time goes in v2:
time: 83.4 us; the launch traced here: 83.1 us
  Pallas kernels  26.5 us (32%)
  waiting for transfers between devices  24.7 us (30%)
  starting transfers between devices  24.5 us (29%)
  local copies, waits for them, and re-layouts  6.63 us (8%)
    ppermute x8, waiting for transfers between devices, across_x(): return lax.ppermute(value, 'ctx', [(i, i ^ 1) for i in range(8)])  17.8 us
    ppermute x10, starting transfers between devices, across_z(): return lax.ppermute(value, 'ctx', [(i, i ^ 2 * distance) for i in range(8)])  12.9 us
    ppermute x8, starting transfers between devices, across_x(): return lax.ppermute(value, 'ctx', [(i, i ^ 1) for i in range(8)])  9.59 us
    pallas_call x2, Pallas kernels, gather(): call(functools.partial(gather_kernel, chunk), limit=GATHER_LIMIT, in_spec...  8.55 us
    pallas_call x2, Pallas kernels, attend(): call(functools.partial(attend_kernel, chunk, tuple((at for _, at in gathe...  7.25 us
    ppermute x10, waiting for transfers between devices, across_z(): return lax.ppermute(value, 'ctx', [(i, i ^ 2 * distance) for i in range(8)])  6.91 us
    unnamed x20, local copies, waits for them, and re-layouts  6.63 us
    pallas_call x1, Pallas kernels, index_rows(): call(functools.partial(index_kernel, tuple((at for _, at in members))), g...  3.52 us
  transfers between devices with their start and end apart: 21, of which 10 were waited for; matrix products, arithmetic and copies ran while one was open for 0% of the time, Pallas kernels for 28%

profile of v2, /device:TPU:0, one launch (start us, length us, event | category | flops | bytes accessed | tf_op | source)
XLA Modules:
  0.0 83.1 jit_solution(15690990656096476384)
XLA Ops:
  0.6 2.1 %pack.1 = (bf16[136,640]{1,0:T(8,128)(2,1)}, bf16[136,640]{1,0:T(8,128)(2,1)}, bf16[272,640]{1,0:T(8,128)(2,1)}) custom-call(bf16[4,4,16,576]{3,2,1,0:T(8,128)(2,1)} %q_hbm.1, bf16[4,4,8,128]{3,2,1,0:T(8,128)(2,1)} %iq_hbm.1, bf16[4,4,8]{2,1,0:T(4,128)(2,1)} %iw_hbm.1), custom_call_target="tpu_custom_call" | custom-call | tf_op jit(solution)/shard_map/pack/pallas_call | solution.py:92
  2.7 3.0 %collective-permute-start.1 = (bf16[272,640]{1,0:T(8,128)(2,1)}, bf16[272,640]{1,0:T(8,128)(2,1)S(1)}, u32[]{:S(2)}, u32[]{:S(2)}) collective-permute-start(bf16[272,640]{1,0:T(8,128)(2,1)} %get-tuple-element.47), channel_id=1, source_target_pairs={{0,4},{4,0},{8,12},{12,8},{16,20},{20,16},{24,28},{28,24},{1,5},{5... | collective-permute-start | bytes 1044488 | tf_op jit(solution)/shard_map/ppermute | solution.py:573
  5.7 2.6 %collective-permute-start.2 = (bf16[136,640]{1,0:T(8,128)(2,1)}, bf16[136,640]{1,0:T(8,128)(2,1)S(1)}, u32[]{:S(2)}, u32[]{:S(2)}) collective-permute-start(bf16[136,640]{1,0:T(8,128)(2,1)} %get-tuple-element.44.refs_0_), channel_id=1, source_target_pairs={{0,16},{4,20},{8,24},{12,28},{16,0},{20,4},{24,8},{28,12},{1,17},{... | collective-permute-start | bytes 522248 | tf_op jit(solution)/shard_map/ppermute | solution.py:576
  8.3 1.6 %collective-permute-start = (bf16[136,640]{1,0:T(8,128)(2,1)}, bf16[136,640]{1,0:T(8,128)(2,1)S(1)}, u32[]{:S(2)}, u32[]{:S(2)}) collective-permute-start(bf16[136,640]{1,0:T(8,128)(2,1)} %get-tuple-element.44.refs_0_), channel_id=1, source_target_pairs={{0,8},{4,12},{8,0},{12,4},{16,24},{20,28},{24,16},{28,20},{1,9},{5... | collective-permute-start | bytes 522248 | tf_op jit(solution)/shard_map/ppermute | solution.py:576
  12.8 3.8 %collective-permute-done.2.second_ref.refs_2_ = bf16[136,640]{1,0:T(8,128)(2,1)S(1)} collective-permute-done((bf16[136,640]{1,0:T(8,128)(2,1)}, bf16[136,640]{1,0:T(8,128)(2,1)S(1)}, u32[]{:S(2)}, u32[]{:S(2)}) %collective-permute-start.2) | collective-permute-done | bytes 174112 | tf_op jit(solution)/shard_map/ppermute | solution.py:576
  17.3 1.5 %collective-permute-start.4 = (bf16[136,640]{1,0:T(8,128)(2,1)S(1)}, bf16[136,640]{1,0:T(8,128)(2,1)S(1)}, u32[]{:S(2)}, u32[]{:S(2)}) collective-permute-start(bf16[136,640]{1,0:T(8,128)(2,1)S(1)} %collective-permute-done.2.second_ref.refs_2_), channel_id=1, source_target_pairs={{0,8},{4,12},{8,0},{12,4},{16,24},{20,28},{24,16},{28,20},{1,9},{5... | collective-permute-start | bytes 522248 | tf_op jit(solution)/shard_map/ppermute | solution.py:576
  18.8 2.3 %collective-permute-start.5 = (bf16[136,640]{1,0:T(8,128)(2,1)}, bf16[136,640]{1,0:T(8,128)(2,1)S(1)}, u32[]{:S(2)}, u32[]{:S(2)}) collective-permute-start(bf16[136,640]{1,0:T(8,128)(2,1)} %get-tuple-element.52.refs_0_.refs_8_), channel_id=1, source_target_pairs={{0,16},{4,20},{8,24},{12,28},{16,0},{20,4},{24,8},{28,12},{1,17},{... | collective-permute-start | bytes 522248 | tf_op jit(solution)/shard_map/ppermute | solution.py:576
  21.2 3.7 %copy-done = bf16[4,2048,576]{1,2,0:T(8,128)(2,1)S(1)} copy-done((bf16[4,2048,576]{1,2,0:T(8,128)(2,1)S(1)}, bf16[4,2048,576]{1,2,0:T(8,128)(2,1)}, u32[]{:S(2)}) %copy-start) | copy-done | bytes 9437208
  24.8 4.2 %gather_blocks.2.refs_8_ = bf16[8,576,1024]{2,1,0:T(8,128)(2,1)S(1)} custom-call(s32[16,32]{1,0:T(8,128)S(1)} %plan.1.table_ref, bf16[4,576,2048]{2,1,0:T(8,128)(2,1)S(1)} %bitcast.1), custom_call_target="tpu_custom_call" | custom-call | tf_op jit(solution)/shard_map/gather_blocks/pallas_call | solution.py:237
  29.2 1.6 %collective-permute-start.7 = (bf16[272,640]{1,0:T(8,128)(2,1)S(1)}, bf16[272,640]{1,0:T(8,128)(2,1)S(1)}, u32[]{:S(2)}, u32[]{:S(2)}) collective-permute-start(bf16[272,640]{1,0:T(8,128)(2,1)S(1)} %pair_up.4), channel_id=1, source_target_pairs={{0,4},{4,0},{8,12},{12,8},{16,20},{20,16},{24,28},{28,24},{1,5},{5... | collective-permute-start | bytes 1044488 | tf_op jit(solution)/shard_map/ppermute | solution.py:573
  30.9 1.9 %collective-permute-start.8 = (bf16[136,640]{1,0:T(8,128)(2,1)S(1)}, bf16[136,640]{1,0:T(8,128)(2,1)S(1)}, u32[]{:S(2)}, u32[]{:S(2)}) collective-permute-start(bf16[136,640]{1,0:T(8,128)(2,1)S(1)} %collective-permute-done.5.second_ref.refs_2_.refs_10_), channel_id=1, source_target_pairs={{0,8},{4,12},{8,0},{12,4},{16,24},{20,28},{24,16},{28,20},{1,9},{5... | collective-permute-start | bytes 522248 | tf_op jit(solution)/shard_map/ppermute | solution.py:576
  32.8 1.5 %collective-permute-start.16 = (bf16[16,128,128]{2,1,0:T(8,128)(2,1)S(1)}, bf16[16,128,128]{2,1,0:T(8,128)(2,1)S(1)}, u32[]{:S(2)}, u32[]{:S(2)}) collective-permute-start(bf16[16,128,128]{2,1,0:T(8,128)(2,1)S(1)} %copy-done.5), channel_id=1, source_target_pairs={{0,2},{1,3},{2,0},{3,1},{4,6},{5,7},{6,4},{7,5},{8,10},{9,11},{10,... | collective-permute-start | bytes 1572872 | tf_op jit(solution)/shard_map/ppermute | solution.py:579
  34.3 4.3 %gather_blocks.3.refs_8_ = bf16[8,576,1024]{2,1,0:T(8,128)(2,1)S(1)} custom-call(s32[16,32]{1,0:T(8,128)S(1)} %plan.1.table_ref, bf16[4,576,2048]{2,1,0:T(8,128)(2,1)S(1)} %bitcast.2), custom_call_target="tpu_custom_call" | custom-call | tf_op jit(solution)/shard_map/gather_blocks/pallas_call | solution.py:237
  40.3 3.5 %attend.2 = (bf16[256,512]{1,0:T(8,128)(2,1)S(1)}, bf16[256,512]{1,0:T(8,128)(2,1)S(1)}, bf16[264,512]{1,0:T(8,128)(2,1)S(1)}, bf16[256,512]{1,0:T(8,128)(2,1)S(1)}, f32[128,128]{1,0:T(8,128)S(1)}) custom-call(s32[16,32]{1,0:T(8,128)S(1)} %plan.1.table_ref, bf16[136,640]{1,0:T(8,128)(2,1)S(1)} %copy-done.3, ...), custom_call_target="tpu_custom_call" | custom-call | tf_op jit(solution)/shard_map/attend/pallas_call | solution.py:321
  43.8 1.5 %collective-permute-start.14 = (bf16[264,512]{1,0:T(8,128)(2,1)S(1)}, bf16[264,512]{1,0:T(8,128)(2,1)S(1)}, u32[]{:S(2)}, u32[]{:S(2)}) collective-permute-start(bf16[264,512]{1,0:T(8,128)(2,1)S(1)} %get-tuple-element.72), channel_id=1, source_target_pairs={{0,4},{4,0},{8,12},{12,8},{16,20},{20,16},{24,28},{28,24},{1,5},{5... | collective-permute-start | bytes 811016 | tf_op jit(solution)/shard_map/ppermute | solution.py:573
  45.3 5.3 %collective-permute-done.9.refs_5_.refs_7_.refs_13_.refs_15_ = bf16[272,640]{1,0:T(8,128)(2,1)S(1)} collective-permute-done((bf16[272,640]{1,0:T(8,128)(2,1)S(1)}, bf16[272,640]{1,0:T(8,128)(2,1)S(1)}, u32[]{:S(2)}, u32[]{:S(2)}) %collective-permute-start.9) | collective-permute-done | bytes 348192 | tf_op jit(solution)/shard_map/ppermute | solution.py:573
  50.6 3.7 %attend.3 = (bf16[256,512]{1,0:T(8,128)(2,1)S(1)}, bf16[256,512]{1,0:T(8,128)(2,1)S(1)}, bf16[264,512]{1,0:T(8,128)(2,1)S(1)}, bf16[256,512]{1,0:T(8,128)(2,1)S(1)}, f32[128,128]{1,0:T(8,128)S(1)}) custom-call(s32[16,32]{1,0:T(8,128)S(1)} %plan.1.table_ref, bf16[136,640]{1,0:T(8,128)(2,1)S(1)} %copy-done.4, ...), custom_call_target="tpu_custom_call" | custom-call | tf_op jit(solution)/shard_map/attend/pallas_call | solution.py:321
  54.6 1.7 %collective-permute-start.18 = (bf16[256,512]{1,0:T(8,128)(2,1)S(1)}, bf16[256,512]{1,0:T(8,128)(2,1)S(1)}, u32[]{:S(2)}, u32[]{:S(2)}) collective-permute-start(bf16[256,512]{1,0:T(8,128)(2,1)S(1)} %get-tuple-element.80), channel_id=1, source_target_pairs={{0,4},{4,0},{8,12},{12,8},{16,20},{20,16},{24,28},{28,24},{1,5},{5... | collective-permute-start | bytes 786440 | tf_op jit(solution)/shard_map/ppermute | solution.py:573
  57.7 4.4 %collective-permute-done.11.other_ref = bf16[264,512]{1,0:T(8,128)(2,1)S(1)} collective-permute-done((bf16[264,512]{1,0:T(8,128)(2,1)S(1)}, bf16[264,512]{1,0:T(8,128)(2,1)S(1)}, u32[]{:S(2)}, u32[]{:S(2)}) %collective-permute-start.11) | collective-permute-done | bytes 270368 | tf_op jit(solution)/shard_map/ppermute | solution.py:573
  62.9 3.7 %collective-permute-done.18.other_ref = bf16[256,512]{1,0:T(8,128)(2,1)S(1)} collective-permute-done((bf16[256,512]{1,0:T(8,128)(2,1)S(1)}, bf16[256,512]{1,0:T(8,128)(2,1)S(1)}, u32[]{:S(2)}, u32[]{:S(2)}) %collective-permute-start.18) | collective-permute-done | bytes 262176 | tf_op jit(solution)/shard_map/ppermute | solution.py:573
  68.5 4.5 %collective-permute-done.10.other_ref = bf16[256,512]{1,0:T(8,128)(2,1)S(1)} collective-permute-done((bf16[256,512]{1,0:T(8,128)(2,1)S(1)}, bf16[256,512]{1,0:T(8,128)(2,1)S(1)}, u32[]{:S(2)}, u32[]{:S(2)}) %collective-permute-start.10) | collective-permute-done | bytes 262176 | tf_op jit(solution)/shard_map/ppermute | solution.py:573
  74.7 3.5 %index_scores.1._ = f32[4,4,2048]{2,1,0:T(4,128)} custom-call(s32[16,32]{1,0:T(8,128)S(1)} %plan.1.table_ref, bf16[136,640]{1,0:T(8,128)(2,1)S(1)} %copy-done.3, bf16[136,640]{1,0:T(8,128)(2,1)S(1)} %collective-permute-done.first_ref.refs_1_, bf16[136,640]{1,0:T(8,128)(2,1)S(1)} %collective-permute-done.2.second_ref.refs_2_, ...), custom_call_target="tpu_custom_call" | custom-call | tf_op jit(solution)/shard_map/index_scores/pallas_call | solution.py:547
  79.3 1.2 %finish.2.rest_0_ = bf16[4,4,16,128]{3,2,1,0:T(8,128)(2,1)} custom-call(f32[128,128]{1,0:T(8,128)S(1)} %get-tuple-element.83.stats_ref, f32[128,512]{1,0:T(8,128)S(1)} %get-tuple-element.84.own_ref, bf16[136,512]{1,0:T(8,128)(2,1)S(1)} %collective-permute-done.20.other_ref, bf16[16,512,128]{2,1,0:T(8,128)(2,1)S(1)} %assemble_up.1.up_ref), custom_call_target="tpu_custom_call" | custom-call | tf_op jit(solution)/shard_map/finish/pallas_call | solution.py:461
  80.5 1.5 %collective-permute-done.13.other_ref = bf16[136,512]{1,0:T(8,128)(2,1)S(1)} collective-permute-done((bf16[136,512]{1,0:T(8,128)(2,1)S(1)}, bf16[136,512]{1,0:T(8,128)(2,1)S(1)}, u32[]{:S(2)}, u32[]{:S(2)}) %collective-permute-start.13) | collective-permute-done | bytes 139296 | tf_op jit(solution)/shard_map/ppermute | solution.py:576
  (57 shorter events, 13.8 us)
Async XLA Ops:
  2.7 14.0 %collective-permute-start.1 = (bf16[272,640]{1,0:T(8,128)(2,1)}, bf16[272,640]{1,0:T(8,128)(2,1)S(1)}, u32[]{:S(2)}, u32[]{:S(2)}) collective-permute-start(bf16[272,640]{1,0:T(8,128)(2,1)} %get-tuple-element.47), channel_id=1, source_target_pairs={{0,4},{4,0},{8,12},{12,8},{16,20},{20,16},{24,28},{28,24},{1,5},{5... | collective-permute-start | bytes 1044488 | tf_op jit(solution)/shard_map/ppermute | solution.py:573
  5.7 10.8 %collective-permute-start.2 = (bf16[136,640]{1,0:T(8,128)(2,1)}, bf16[136,640]{1,0:T(8,128)(2,1)S(1)}, u32[]{:S(2)}, u32[]{:S(2)}) collective-permute-start(bf16[136,640]{1,0:T(8,128)(2,1)} %get-tuple-element.44.refs_0_), channel_id=1, source_target_pairs={{0,16},{4,20},{8,24},{12,28},{16,0},{20,4},{24,8},{28,12},{1,17},{... | collective-permute-start | bytes 522248 | tf_op jit(solution)/shard_map/ppermute | solution.py:576
  8.3 8.4 %collective-permute-start = (bf16[136,640]{1,0:T(8,128)(2,1)}, bf16[136,640]{1,0:T(8,128)(2,1)S(1)}, u32[]{:S(2)}, u32[]{:S(2)}) collective-permute-start(bf16[136,640]{1,0:T(8,128)(2,1)} %get-tuple-element.44.refs_0_), channel_id=1, source_target_pairs={{0,8},{4,12},{8,0},{12,4},{16,24},{20,28},{24,16},{28,20},{1,9},{5... | collective-permute-start | bytes 522248 | tf_op jit(solution)/shard_map/ppermute | solution.py:576
  16.8 12.4 %collective-permute-start.3 = (bf16[272,640]{1,0:T(8,128)(2,1)S(1)}, bf16[272,640]{1,0:T(8,128)(2,1)S(1)}, u32[]{:S(2)}, u32[]{:S(2)}) collective-permute-start(bf16[272,640]{1,0:T(8,128)(2,1)S(1)} %pair_up.3), channel_id=1, source_target_pairs={{0,4},{4,0},{8,12},{12,8},{16,20},{20,16},{24,28},{28,24},{1,5},{5... | collective-permute-start | bytes 1044488 | tf_op jit(solution)/shard_map/ppermute | solution.py:573
  17.3 11.7 %collective-permute-start.4 = (bf16[136,640]{1,0:T(8,128)(2,1)S(1)}, bf16[136,640]{1,0:T(8,128)(2,1)S(1)}, u32[]{:S(2)}, u32[]{:S(2)}) collective-permute-start(bf16[136,640]{1,0:T(8,128)(2,1)S(1)} %collective-permute-done.2.second_ref.refs_2_), channel_id=1, source_target_pairs={{0,8},{4,12},{8,0},{12,4},{16,24},{20,28},{24,16},{28,20},{1,9},{5... | collective-permute-start | bytes 522248 | tf_op jit(solution)/shard_map/ppermute | solution.py:576
  18.8 10.3 %collective-permute-start.5 = (bf16[136,640]{1,0:T(8,128)(2,1)}, bf16[136,640]{1,0:T(8,128)(2,1)S(1)}, u32[]{:S(2)}, u32[]{:S(2)}) collective-permute-start(bf16[136,640]{1,0:T(8,128)(2,1)} %get-tuple-element.52.refs_0_.refs_8_), channel_id=1, source_target_pairs={{0,16},{4,20},{8,24},{12,28},{16,0},{20,4},{24,8},{28,12},{1,17},{... | collective-permute-start | bytes 522248 | tf_op jit(solution)/shard_map/ppermute | solution.py:576
  24.8 9.5 %copy-start.1 = (bf16[4,2048,576]{1,2,0:T(8,128)(2,1)S(1)}, bf16[4,2048,576]{1,2,0:T(8,128)(2,1)}, u32[]{:S(2)}) copy-start(bf16[4,2048,576]{1,2,0:T(8,128)(2,1)} %param.9) | copy-start | bytes 28311556
  29.2 11.1 %copy-start.3 = (bf16[136,640]{1,0:T(8,128)(2,1)S(1)}, bf16[136,640]{1,0:T(8,128)(2,1)}, u32[]{:S(2)}) copy-start(bf16[136,640]{1,0:T(8,128)(2,1)} %get-tuple-element.44.refs_0_) | copy-start | bytes 522244
  29.2 10.4 %collective-permute-start.7 = (bf16[272,640]{1,0:T(8,128)(2,1)S(1)}, bf16[272,640]{1,0:T(8,128)(2,1)S(1)}, u32[]{:S(2)}, u32[]{:S(2)}) collective-permute-start(bf16[272,640]{1,0:T(8,128)(2,1)S(1)} %pair_up.4), channel_id=1, source_target_pairs={{0,4},{4,0},{8,12},{12,8},{16,20},{20,16},{24,28},{28,24},{1,5},{5... | collective-permute-start | bytes 1044488 | tf_op jit(solution)/shard_map/ppermute | solution.py:573
  30.8 7.9 %collective-permute-start.6 = (bf16[136,640]{1,0:T(8,128)(2,1)S(1)}, bf16[136,640]{1,0:T(8,128)(2,1)S(1)}, u32[]{:S(2)}, u32[]{:S(2)}) collective-permute-start(bf16[136,640]{1,0:T(8,128)(2,1)S(1)} %copy-done.4), channel_id=1, source_target_pairs={{0,8},{4,12},{8,0},{12,4},{16,24},{20,28},{24,16},{28,20},{1,9},{5... | collective-permute-start | bytes 522248 | tf_op jit(solution)/shard_map/ppermute | solution.py:576
  30.9 8.7 %collective-permute-start.8 = (bf16[136,640]{1,0:T(8,128)(2,1)S(1)}, bf16[136,640]{1,0:T(8,128)(2,1)S(1)}, u32[]{:S(2)}, u32[]{:S(2)}) collective-permute-start(bf16[136,640]{1,0:T(8,128)(2,1)S(1)} %collective-permute-done.5.second_ref.refs_2_.refs_10_), channel_id=1, source_target_pairs={{0,8},{4,12},{8,0},{12,4},{16,24},{20,28},{24,16},{28,20},{1,9},{5... | collective-permute-start | bytes 522248 | tf_op jit(solution)/shard_map/ppermute | solution.py:576
  32.8 23.6 %collective-permute-start.16 = (bf16[16,128,128]{2,1,0:T(8,128)(2,1)S(1)}, bf16[16,128,128]{2,1,0:T(8,128)(2,1)S(1)}, u32[]{:S(2)}, u32[]{:S(2)}) collective-permute-start(bf16[16,128,128]{2,1,0:T(8,128)(2,1)S(1)} %copy-done.5), channel_id=1, source_target_pairs={{0,2},{1,3},{2,0},{3,1},{4,6},{5,7},{6,4},{7,5},{8,10},{9,11},{10,... | collective-permute-start | bytes 1572872 | tf_op jit(solution)/shard_map/ppermute | solution.py:579
  39.7 10.9 %collective-permute-start.9 = (bf16[272,640]{1,0:T(8,128)(2,1)S(1)}, bf16[272,640]{1,0:T(8,128)(2,1)S(1)}, u32[]{:S(2)}, u32[]{:S(2)}) collective-permute-start(bf16[272,640]{1,0:T(8,128)(2,1)S(1)} %pair_up.5), channel_id=1, source_target_pairs={{0,4},{4,0},{8,12},{12,8},{16,20},{20,16},{24,28},{28,24},{1,5},{5... | collective-permute-start | bytes 1044488 | tf_op jit(solution)/shard_map/ppermute | solution.py:573
  43.8 30.9 %copy-start.2 = (bf16[4,2048,128]{2,1,0:T(8,128)(2,1)S(1)}, bf16[4,2048,128]{2,1,0:T(8,128)(2,1)}, u32[]{:S(2)}) copy-start(bf16[4,2048,128]{2,1,0:T(8,128)(2,1)} %refs_16_.1) | copy-start | bytes 6291460
  43.8 13.1 %collective-permute-start.14 = (bf16[264,512]{1,0:T(8,128)(2,1)S(1)}, bf16[264,512]{1,0:T(8,128)(2,1)S(1)}, u32[]{:S(2)}, u32[]{:S(2)}) collective-permute-start(bf16[264,512]{1,0:T(8,128)(2,1)S(1)} %get-tuple-element.72), channel_id=1, source_target_pairs={{0,4},{4,0},{8,12},{12,8},{16,20},{20,16},{24,28},{28,24},{1,5},{5... | collective-permute-start | bytes 811016 | tf_op jit(solution)/shard_map/ppermute | solution.py:573
  54.3 7.8 %collective-permute-start.11 = (bf16[264,512]{1,0:T(8,128)(2,1)S(1)}, bf16[264,512]{1,0:T(8,128)(2,1)S(1)}, u32[]{:S(2)}, u32[]{:S(2)}) collective-permute-start(bf16[264,512]{1,0:T(8,128)(2,1)S(1)} %get-tuple-element.63), channel_id=1, source_target_pairs={{0,4},{4,0},{8,12},{12,8},{16,20},{20,16},{24,28},{28,24},{1,5},{5... | collective-permute-start | bytes 811016 | tf_op jit(solution)/shard_map/ppermute | solution.py:573
  54.6 12.0 %collective-permute-start.18 = (bf16[256,512]{1,0:T(8,128)(2,1)S(1)}, bf16[256,512]{1,0:T(8,128)(2,1)S(1)}, u32[]{:S(2)}, u32[]{:S(2)}) collective-permute-start(bf16[256,512]{1,0:T(8,128)(2,1)S(1)} %get-tuple-element.80), channel_id=1, source_target_pairs={{0,4},{4,0},{8,12},{12,8},{16,20},{20,16},{24,28},{28,24},{1,5},{5... | collective-permute-start | bytes 786440 | tf_op jit(solution)/shard_map/ppermute | solution.py:573
  56.4 21.8 %collective-permute-start.15 = (bf16[16,128,128]{2,1,0:T(8,128)(2,1)S(1)}, bf16[16,128,128]{2,1,0:T(8,128)(2,1)S(1)}, u32[]{:S(2)}, u32[]{:S(2)}) collective-permute-start(bf16[16,128,128]{2,1,0:T(8,128)(2,1)S(1)} %copy-done.5), channel_id=1, source_target_pairs={{0,1},{1,0},{2,3},{3,2},{4,5},{5,4},{6,7},{7,6},{8,9},{9,8},{10,11... | collective-permute-start | bytes 1572872 | tf_op jit(solution)/shard_map/ppermute | solution.py:579
  56.4 21.8 %collective-permute-start.17 = (bf16[16,128,128]{2,1,0:T(8,128)(2,1)S(1)}, bf16[16,128,128]{2,1,0:T(8,128)(2,1)S(1)}, u32[]{:S(2)}, u32[]{:S(2)}) collective-permute-start(bf16[16,128,128]{2,1,0:T(8,128)(2,1)S(1)} %collective-permute-done.16.refs_2_), channel_id=1, source_target_pairs={{0,1},{1,0},{2,3},{3,2},{4,5},{5,4},{6,7},{7,6},{8,9},{9,8},{10,11... | collective-permute-start | bytes 1572872 | tf_op jit(solution)/shard_map/ppermute | solution.py:579
  57.2 9.9 %collective-permute-start.19 = (bf16[264,512]{1,0:T(8,128)(2,1)S(1)}, bf16[264,512]{1,0:T(8,128)(2,1)S(1)}, u32[]{:S(2)}, u32[]{:S(2)}) collective-permute-start(bf16[264,512]{1,0:T(8,128)(2,1)S(1)} %get-tuple-element.74), channel_id=1, source_target_pairs={{0,8},{4,12},{8,0},{12,4},{16,24},{20,28},{24,16},{28,20},{1,9},{5... | collective-permute-start | bytes 811016 | tf_op jit(solution)/shard_map/ppermute | solution.py:576
  62.4 11.2 %collective-permute-start.12 = (bf16[264,512]{1,0:T(8,128)(2,1)S(1)}, bf16[264,512]{1,0:T(8,128)(2,1)S(1)}, u32[]{:S(2)}, u32[]{:S(2)}) collective-permute-start(bf16[264,512]{1,0:T(8,128)(2,1)S(1)} %get-tuple-element.66), channel_id=1, source_target_pairs={{0,8},{4,12},{8,0},{12,4},{16,24},{20,28},{24,16},{28,20},{1,9},{5... | collective-permute-start | bytes 811016 | tf_op jit(solution)/shard_map/ppermute | solution.py:576
  66.6 6.4 %collective-permute-start.10 = (bf16[256,512]{1,0:T(8,128)(2,1)S(1)}, bf16[256,512]{1,0:T(8,128)(2,1)S(1)}, u32[]{:S(2)}, u32[]{:S(2)}) collective-permute-start(bf16[256,512]{1,0:T(8,128)(2,1)S(1)} %get-tuple-element.61), channel_id=1, source_target_pairs={{0,4},{4,0},{8,12},{12,8},{16,20},{20,16},{24,28},{28,24},{1,5},{5... | collective-permute-start | bytes 786440 | tf_op jit(solution)/shard_map/ppermute | solution.py:573
  67.4 11.9 %collective-permute-start.20 = (bf16[136,512]{1,0:T(8,128)(2,1)S(1)}, bf16[136,512]{1,0:T(8,128)(2,1)S(1)}, u32[]{:S(2)}, u32[]{:S(2)}) collective-permute-start(bf16[136,512]{1,0:T(8,128)(2,1)S(1)} %get-tuple-element.85), channel_id=1, source_target_pairs={{0,16},{4,20},{8,24},{12,28},{16,0},{20,4},{24,8},{28,12},{1,17},{... | collective-permute-start | bytes 417800 | tf_op jit(solution)/shard_map/ppermute | solution.py:576
  73.9 8.1 %collective-permute-start.13 = (bf16[136,512]{1,0:T(8,128)(2,1)S(1)}, bf16[136,512]{1,0:T(8,128)(2,1)S(1)}, u32[]{:S(2)}, u32[]{:S(2)}) collective-permute-start(bf16[136,512]{1,0:T(8,128)(2,1)S(1)} %get-tuple-element.70), channel_id=1, source_target_pairs={{0,16},{4,20},{8,24},{12,28},{16,0},{20,4},{24,8},{28,12},{1,17},{... | collective-permute-start | bytes 417800 | tf_op jit(solution)/shard_map/ppermute | solution.py:576
  (7 other events, 20.5 us)

commit v3 on v2

--- a/solution.py
+++ b/solution.py
@@ -14,9 +14,7 @@
 PACK_LIMIT = 63_000_000
 ATTEND_LIMIT = 20 * 1024 * 1024
 TABLE = 32
-GATHER_LIMIT = 16 * 1024 * 1024
-FAR = (1, 3)
-NEAR = (0, 2)
+GATHER_LIMIT = (47_000_000, 38_000_000)
 
 CHUNKS = 2
 PAIRS = 8
@@ -29,9 +27,12 @@
 LANES = 128
 
 
-def call(body, limit=VMEM_LIMIT, **kwargs):
+def call(body, limit=VMEM_LIMIT, us=0.3, **kwargs):
     return pl.pallas_call(
         body,
+        cost_estimate=pl.CostEstimate(
+            flops=int(us * 1e9), bytes_accessed=int(us * 3e6), transcendentals=0
+        ),
         compiler_params=pltpu.CompilerParams(vmem_limit_bytes=limit),
         **kwargs,
     )
@@ -102,6 +103,7 @@
             pltpu.SemaphoreType.DMA((5,)),
         ],
         name="pack",
+        us=2,
     )(queries, index_queries, index_weights)
 
 
@@ -116,6 +118,18 @@
         out_shape=jax.ShapeDtypeStruct((2 * SENT, WIDE), jnp.bfloat16),
         name="pair_up",
     )(first, second)
+
+
+def second_of_kernel(both_ref, out_ref):
+    out_ref[...] = both_ref[SENT:, :]
+
+
+def second_of(both):
+    return call(
+        second_of_kernel,
+        out_shape=jax.ShapeDtypeStruct((SENT, WIDE), jnp.bfloat16),
+        name="second_of",
+    )(both)
 
 
 def plan_kernel(selection_ref, counts_ref, lengths_ref, out_ref):
@@ -159,6 +173,7 @@
         in_specs=[pl.BlockSpec(), smem, smem],
         out_shape=jax.ShapeDtypeStruct((16, TABLE), jnp.int32),
         name="plan",
+        us=0.9,
     )(selection, counts, lengths)
 
 
@@ -236,18 +251,19 @@
     bf16 = jnp.bfloat16
     return call(
         functools.partial(gather_kernel, chunk),
-        limit=GATHER_LIMIT,
+        limit=GATHER_LIMIT[chunk],
         in_specs=[pl.BlockSpec(memory_space=pltpu.SMEM), pl.BlockSpec(memory_space=pltpu.HBM)],
         out_shape=jax.ShapeDtypeStruct((PAIRS, 576, SLOTS * LANES), bf16),
         scratch_shapes=[pltpu.VMEM((2, 576, 2048), bf16), pltpu.SemaphoreType.DMA((8,))],
         name="gather_blocks",
+        us=5,
     )(table, latents_t)
 
 
 def attend_kernel(chunk, offsets, table_ref, *refs):
     q_refs = refs[:8]
     block_ref = refs[8]
-    own_a, own_b, send_a, send_b, stats_ref, score_ref, weight_ref = refs[9:]
+    near, far, cross, send_x, send_z, stats_ref, score_ref, weight_ref = refs[9:]
     lane = lax.broadcasted_iota(jnp.int32, (LANES, LANES), 1)
     position = lax.broadcasted_iota(jnp.int32, (1, LANES), 1)
     stats_ref[...] = jnp.zeros((LANES, LANES), jnp.float32)
@@ -294,12 +310,17 @@
                 preferred_element_type=jnp.float32,
             )
             mixed = (mixed * scales[step]).astype(jnp.bfloat16)
-            for across, (out_a, out_b) in enumerate(((own_a, own_b), (send_a, send_b))):
-                for out, members in ((out_a, FAR), (out_b, NEAR)):
-                    for place, member in enumerate(members):
-                        source = (across * 4 + member) * HEADS
-                        row = place * ROWS + (local * 4 + step) * HEADS
-                        out[row : row + HEADS, :] = mixed[source : source + HEADS]
+            row = (local * 4 + step) * HEADS
+            for out, places in (
+                (near, (0, 2)),
+                (far, (1, 3)),
+                (cross, (4, 6)),
+                (send_x, (5,)),
+                (send_z, (7,)),
+            ):
+                for half, place in enumerate(places):
+                    at = half * ROWS + row
+                    out[at : at + HEADS, :] = mixed[place * HEADS : (place + 1) * HEADS]
 
     for local in range(2):
         request = 2 * chunk + local
@@ -313,7 +334,8 @@
         def _(local=local, request=request):
             work(local, request, 8)
 
-    store_stats(send_a, 2 * ROWS, stats_ref[...])
+    store_stats(send_x, ROWS, stats_ref[...])
+    store_stats(send_z, ROWS, stats_ref[...])
 
 
 def attend(chunk, table, gathered_queries, blocks):
@@ -325,8 +347,9 @@
         out_shape=[
             jax.ShapeDtypeStruct((2 * ROWS, KV), bf16),
             jax.ShapeDtypeStruct((2 * ROWS, KV), bf16),
-            jax.ShapeDtypeStruct((2 * ROWS + EXTRA, KV), bf16),
             jax.ShapeDtypeStruct((2 * ROWS, KV), bf16),
+            jax.ShapeDtypeStruct((SENT, KV), bf16),
+            jax.ShapeDtypeStruct((SENT, KV), bf16),
             jax.ShapeDtypeStruct((LANES, LANES), jnp.float32),
         ],
         scratch_shapes=[
@@ -334,106 +357,93 @@
             pltpu.VMEM((4, LANES, SLOTS * LANES), bf16),
         ],
         name="attend",
+        us=3.6,
     )(table, *(array for array, _ in gathered_queries), blocks)
 
 
-def joined(own_ref, other_ref, place, weight_own, weight_other):
+def group(number):
+    return slice(number * HEADS, (number + 1) * HEADS)
+
+
+def weigh(*stats):
+    peak = functools.reduce(jnp.maximum, stats)
+    weights = [jnp.exp(value - peak) for value in stats]
+    total = functools.reduce(jnp.add, weights)
+    return [value / total for value in weights], peak + jnp.log(total)
+
+
+def joined(parts, weights):
     for pair in range(PAIRS):
-        row = place * ROWS + pair * HEADS
-        own = own_ref[row : row + HEADS, :].astype(jnp.float32)
-        other = other_ref[row : row + HEADS, :].astype(jnp.float32)
-        yield pair, (
-            own * weight_own[:, pair : pair + 1] + other * weight_other[:, pair : pair + 1]
-        )
-
-
-def weigh(own, other):
-    peak = jnp.maximum(own, other)
-    own, other = jnp.exp(own - peak), jnp.exp(other - peak)
-    total = own + other
-    return own / total, other / total, peak + jnp.log(total)
-
-
-def rows_of(member):
-    return slice(member * HEADS, (member + 1) * HEADS)
-
-
-def join_far_kernel(own_ref, other_ref, stats_ref, out_ref, weight_ref, lse_ref):
-    own, other, lse = weigh(stats_ref[:64], load_stats(other_ref, 2 * ROWS)[64:])
-    lse = jnp.concatenate([lse, jnp.zeros((64, LANES), jnp.float32)], axis=0)
-    weight_ref[0] = own
-    weight_ref[1] = other
-    lse_ref[...] = lse
-    for place, member in enumerate(FAR):
-        part = rows_of(member)
-        for pair, rows in joined(own_ref, other_ref, place, own[part], other[part]):
-            row = place * ROWS + pair * HEADS
-            out_ref[row : row + HEADS, :] = rows.astype(jnp.bfloat16)
-    store_stats(out_ref, 2 * ROWS, lse)
-
-
-def join_far(own, other, stats):
-    return call(
-        join_far_kernel,
-        out_shape=[
-            jax.ShapeDtypeStruct((2 * ROWS + EXTRA, KV), jnp.bfloat16),
-            jax.ShapeDtypeStruct((2, 64, LANES), jnp.float32),
-            jax.ShapeDtypeStruct((LANES, LANES), jnp.float32),
-        ],
-        name="join_far",
-    )(own, other, stats)
-
-
-def join_near_kernel(own_ref, other_ref, weight_ref, out_ref):
-    for place, member in enumerate(NEAR):
-        part = rows_of(member)
-        weights = weight_ref[0, part], weight_ref[1, part]
-        for pair, rows in joined(own_ref, other_ref, place, *weights):
-            row = place * ROWS + pair * HEADS
-            out_ref[row : row + HEADS, :] = rows
-
-
-def join_near(own, other, weights):
+        rows = None
+        for (ref, start), weight in zip(parts, weights):
+            at = start + pair * HEADS
+            part = ref[at : at + HEADS, :].astype(jnp.float32) * weight[:, pair : pair + 1]
+            rows = part if rows is None else rows + part
+        yield slice(pair * HEADS, (pair + 1) * HEADS), rows
+
+
+def stack(stats, new):
+    return jnp.concatenate([new.get(number, stats[group(number)]) for number in range(8)], axis=0)
+
+
+def join_cross_kernel(far, cross, from_x, from_z, stats_ref, to_z, to_x, out_stats):
+    stats = stats_ref[...]
+    weights, lse1 = weigh(stats[group(1)], load_stats(from_x, ROWS)[group(5)])
+    for rows, value in joined(((far, 0), (from_x, 0)), weights):
+        to_z[rows, :] = value.astype(jnp.bfloat16)
+    to_z[ROWS : 2 * ROWS, :] = far[ROWS:, :]
+    weights, lse6 = weigh(stats[group(6)], load_stats(from_z, ROWS)[group(7)])
+    to_x[:ROWS, :] = cross[:ROWS, :]
+    for rows, value in joined(((cross, ROWS), (from_z, 0)), weights):
+        to_x[ROWS + rows.start : ROWS + rows.stop, :] = value.astype(jnp.bfloat16)
+    stats = stack(stats, {1: lse1, 6: lse6})
+    out_stats[...] = stats
+    store_stats(to_z, 2 * ROWS, stats)
+    store_stats(to_x, 2 * ROWS, stats)
+
+
+def join_cross(far, cross, from_x, from_z, stats):
+    message = jax.ShapeDtypeStruct((2 * ROWS + EXTRA, KV), jnp.bfloat16)
+    return call(
+        join_cross_kernel,
+        out_shape=[message, message, jax.ShapeDtypeStruct((LANES, LANES), jnp.float32)],
+        name="join_cross",
+    )(far, cross, from_x, from_z, stats)
+
+
+def join_near_kernel(near, from_x, from_z, stats_ref, to_z2, mine, out_stats):
+    stats, stats_x, stats_z = (
+        stats_ref[...],
+        load_stats(from_x, 2 * ROWS),
+        load_stats(from_z, 2 * ROWS),
+    )
+    weights, lse2 = weigh(stats[group(2)], stats_x[group(6)], stats_z[group(3)])
+    for rows, value in joined(((near, ROWS), (from_x, ROWS), (from_z, ROWS)), weights):
+        to_z2[rows, :] = value.astype(jnp.bfloat16)
+    weights, lse0 = weigh(stats[group(0)], stats_x[group(4)], stats_z[group(1)])
+    for rows, value in joined(((near, 0), (from_x, 0), (from_z, 0)), weights):
+        mine[rows, :] = value
+    stats = stack(stats, {0: lse0, 2: lse2})
+    out_stats[...] = stats
+    store_stats(to_z2, ROWS, stats)
+
+
+def join_near(near, from_x, from_z, stats):
     return call(
         join_near_kernel,
-        out_shape=jax.ShapeDtypeStruct((2 * ROWS, KV), jnp.float32),
-        name="join_near",
-    )(own, other, weights)
-
-
-def join_line_kernel(own_ref, other_ref, lse_ref, out_ref, mine_ref, stats_ref):
-    own = jnp.concatenate([lse_ref[rows_of(member)] for member in NEAR], axis=0)
-    theirs = load_stats(other_ref, 2 * ROWS)
-    other = jnp.concatenate([theirs[rows_of(member)] for member in FAR], axis=0)
-    own, other, lse = weigh(own, other)
-    lse = jnp.concatenate([lse, jnp.zeros((LANES - 2 * HEADS, LANES), jnp.float32)], axis=0)
-    part = rows_of(1)
-    for pair, rows in joined(own_ref, other_ref, 1, own[part], other[part]):
-        out_ref[pair * HEADS : (pair + 1) * HEADS, :] = rows.astype(jnp.bfloat16)
-    store_stats(out_ref, ROWS, lse)
-    part = rows_of(0)
-    for pair, rows in joined(own_ref, other_ref, 0, own[part], other[part]):
-        mine_ref[pair * HEADS : (pair + 1) * HEADS, :] = rows
-    stats_ref[...] = lse
-
-
-def join_line(own, other, lse):
-    return call(
-        join_line_kernel,
         out_shape=[
             jax.ShapeDtypeStruct((SENT, KV), jnp.bfloat16),
             jax.ShapeDtypeStruct((ROWS, KV), jnp.float32),
             jax.ShapeDtypeStruct((LANES, LANES), jnp.float32),
         ],
-        name="join_line",
-    )(own, other, lse)
+        name="join_near",
+    )(near, from_x, from_z, stats)
 
 
 def finish_kernel(stats_ref, own_ref, other_ref, up_ref, *rest):
     out_ref, rows_ref, lifted_ref = rest[-3:]
-    own, other, _ = weigh(stats_ref[:HEADS], load_stats(other_ref, ROWS)[rows_of(1)])
-    for pair, rows in joined(own_ref, other_ref, 0, own, other):
-        part = slice(pair * HEADS, (pair + 1) * HEADS)
+    weights, _ = weigh(stats_ref[group(0)], load_stats(other_ref, ROWS)[group(2)])
+    for part, rows in joined(((own_ref, 0), (other_ref, 0)), weights):
         for tile in range(4):
             rows_ref[tile, part, :] = rows[:, tile * LANES : (tile + 1) * LANES]
     for head in range(HEADS):
@@ -470,6 +480,7 @@
         ],
         input_output_aliases=aliases,
         name="finish",
+        us=1.2,
     )(*args)
 
 
@@ -487,6 +498,7 @@
         in_specs=[pl.BlockSpec(memory_space=pl.ANY)] + [pl.BlockSpec()] * 4,
         out_shape=jax.ShapeDtypeStruct((HEADS, KV, 128), jnp.bfloat16),
         name="assemble_up",
+        us=1.0,
     )(earlier, *pieces)
 
 
@@ -555,6 +567,7 @@
         ),
         out_shape=jax.ShapeDtypeStruct((4, 4, 2048), jnp.float32),
         name="index_scores",
+        us=3.5,
     )(table, *(array for array, _ in members), index_keys)
 
 
@@ -591,47 +604,42 @@
     z2c1 = across_z(after(own1, *round1), 2)
     blocks0 = gather(0, after(table, *round1), latents_t)
 
+    up_y = across_req(after(value_up_weight, *round1), 2)
+    up_core = across_req(after(value_up_weight, *round1), 1)
+
     round2 = (x12, z3c0, z2c1, blocks0)
     x32 = across_x(pair_up(after(z3c0, *round2), z2c1))
     z1c1 = across_z(after(own1, *round2), 1)
     z3c1 = across_z(after(z2c1, *round2), 1)
     blocks1 = gather(1, after(table, *round2), latents_t)
-    up_y = across_req(after(value_up_weight, *round2), 2)
+    up_both = across_req(after(up_y, *round2), 1)
 
     round3 = (x32, z1c1, z3c1, blocks1)
-    last = pair_up(after(z1c1, *round3), z3c1)
-    x13 = across_x(last)
-    up_core = across_req(after(value_up_weight, *round3), 1)
-    up_both = across_req(after(up_y, *round3), 1)
+    xz1c1 = across_x(after(z1c1, *round3))
+    xz2c1 = second_of(after(x32, *round3))
+    xz3c1 = across_z(xz2c1, 1)
     gathered = [
         [(own0, 0), (z1c0, 0), (z2c0, 0), (z3c0, 0), (x0, 0), (x12, 0), (x12, SENT), (x32, 0)],
-        [(own1, 0), (z1c1, 0), (z2c1, 0), (z3c1, 0), (x0, SENT), (x13, 0), (x32, SENT), (x13, SENT)],
+        [(own1, 0), (z1c1, 0), (z2c1, 0), (z3c1, 0), (x0, SENT), (xz1c1, 0), (xz2c1, 0), (xz3c1, 0)],
     ]
 
-    own_a0, own_b0, send_a0, send_b0, stats0 = attend(
-        0, after(table, last), gathered[0], blocks0
-    )
-    xa0, xb0 = across_x(send_a0), across_x(send_b0)
-    own_a1, own_b1, send_a1, send_b1, stats1 = attend(
-        1, after(table, stats0), gathered[1], blocks1
-    )
-    xa1, xb1 = across_x(send_a1), across_x(send_b1)
-
-    far0, weights0, lse0 = join_far(own_a0, after(xa0, stats1), stats0)
-    l0 = across_z(far0, 1)
-    near0 = join_near(own_b0, xb0, weights0)
-    index_scores = index_rows(after(table, far0), gathered, index_keys)
-    up = assemble(index_scores, [value_up_weight, up_core, up_y, up_both])
-
-    message0, mine0, stats0 = join_line(near0, l0, lse0)
-    f0 = across_z(message0, 2)
-    far1, weights1, lse1 = join_far(own_a1, xa1, stats1)
-    l1 = across_z(far1, 1)
-    near1 = join_near(own_b1, xb1, weights1)
-    message1, mine1, stats1 = join_line(near1, l1, lse1)
-    f1 = across_z(message1, 2)
-    head_values = finish(0, stats0, mine0, f0, up, None)
-    head_values = finish(1, stats1, mine1, f1, up, head_values)
+    near0, far0, cross0, x5, z7, stats0 = attend(0, after(table, xz2c1), gathered[0], blocks0)
+    x5, z7 = across_x(x5), across_z(z7, 1)
+    up = assemble(stats0, [value_up_weight, up_core, up_y, up_both])
+    near1, far1, cross1, x5c1, z7c1, stats1 = attend(1, after(table, up), gathered[1], blocks1)
+    x5c1, z7c1 = across_x(x5c1), across_z(z7c1, 1)
+
+    to_z, to_x, stats0 = join_cross(far0, cross0, after(x5, stats1), z7, stats0)
+    from_x, from_z = across_x(to_x), across_z(to_z, 1)
+    to_z, to_x, stats1 = join_cross(far1, cross1, after(x5c1, stats0), z7c1, stats1)
+    from_xc1, from_zc1 = across_x(to_x), across_z(to_z, 1)
+    index_scores = index_rows(after(table, stats1), gathered, index_keys)
+    message, mine0, stats0 = join_near(near0, from_x, from_z, stats0)
+    last0 = across_z(message, 2)
+    message, mine1, stats1 = join_near(near1, from_xc1, from_zc1, stats1)
+    last1 = across_z(message, 2)
+    head_values = finish(0, stats0, mine0, last0, up, None)
+    head_values = finish(1, stats1, mine1, last1, up, head_values)
     return (head_values, index_scores)
 
 
@@ -747,9 +755,9 @@
         P("req"),
     )
     sizes = dict(mesh.shape)
-    plan = fast if (sizes["ctx"], sizes["req"]) == (8, 4) else per_device
+    plan_here = fast if (sizes["ctx"], sizes["req"]) == (8, 4) else per_device
     return jax.shard_map(
-        plan,
+        plan_here,
         mesh=mesh,
         in_specs=placed,
         out_specs=(P(None, "req", "ctx", None), P(None, "req", "ctx")),

time: 83.4 us -> 80.6 us (0.966)
  starting transfers between devices: 24.5 us -> 33.1 us
  waiting for transfers between devices: 24.7 us -> 16.9 us
  local copies, waits for them, and re-layouts: 6.63 us -> 2.05 us
  Pallas kernels: 26.5 us -> 27.5 us
    ppermute x8, waiting for transfers between devices: 17.8 us -> 5.12 us  [across_x(): return lax.ppermute(value, 'ctx', [(i, i ^ 1) for i in range(8)])]
    ppermute x10 -> x13, starting transfers between devices: 12.9 us -> 22.4 us  [across_z(): return lax.ppermute(value, 'ctx', [(i, i ^ 2 * distance) for i in range(8)])]
    ppermute x10 -> x13, waiting for transfers between devices: 6.91 us -> 11.8 us  [across_z(): return lax.ppermute(value, 'ctx', [(i, i ^ 2 * distance) for i in range(8)])]
    unnamed x20 -> x14, local copies, waits for them, and re-layouts: 6.63 us -> 2.05 us
    pallas_call x8 -> x7, Pallas kernels: 10.1 us -> 11.2 us  [the longest x2 9.76 us: gather(): call(functools.partial(gather_kernel, chunk), limit=GATHER_LIMIT[chunk],...]
  transfers between devices with their start and end apart: 21 -> 24, of which waited for: 10 -> 10; matrix products, arithmetic and copies ran while one was open for 0% -> 0% of each run, Pallas kernels for 28% -> 30%
where the time goes in v3:
time: 80.6 us; the launch traced here: 80.3 us
  starting transfers between devices  33.1 us (41%)
  Pallas kernels  27.5 us (34%)
  waiting for transfers between devices  16.9 us (21%)
  local copies, waits for them, and re-layouts  2.05 us (3%)
    ppermute x13, starting transfers between devices, across_z(): return lax.ppermute(value, 'ctx', [(i, i ^ 2 * distance) for i in range(8)])  22.4 us
    ppermute x13, waiting for transfers between devices, across_z(): return lax.ppermute(value, 'ctx', [(i, i ^ 2 * distance) for i in range(8)])  11.8 us
    pallas_call x2, Pallas kernels, gather(): call(functools.partial(gather_kernel, chunk), limit=GATHER_LIMIT[chunk],...  9.76 us
    ppermute x8, starting transfers between devices, across_x(): return lax.ppermute(value, 'ctx', [(i, i ^ 1) for i in range(8)])  9.23 us
    pallas_call x2, Pallas kernels, attend(): call(functools.partial(attend_kernel, chunk, tuple((at for _, at in gathe...  7.12 us
    ppermute x8, waiting for transfers between devices, across_x(): return lax.ppermute(value, 'ctx', [(i, i ^ 1) for i in range(8)])  5.12 us
    pallas_call x1, Pallas kernels, index_rows(): call(functools.partial(index_kernel, tuple((at for _, at in members))), g...  3.5 us
    pallas_call x2, Pallas kernels, finish(): call(finish_kernel, grid=(1,), in_specs=specs, out_specs=pl.BlockSpec((4,...  2.42 us
  transfers between devices with their start and end apart: 24, of which 10 were waited for; matrix products, arithmetic and copies ran while one was open for 0% of the time, Pallas kernels for 30%

profile of v3, /device:TPU:0, one launch (start us, length us, event | category | flops | bytes accessed | tf_op | source)
XLA Modules:
  0.0 80.3 jit_solution(17531101051016912368)
XLA Ops:
  0.6 2.2 %pack.1 = (bf16[136,640]{1,0:T(8,128)(2,1)}, bf16[136,640]{1,0:T(8,128)(2,1)}, bf16[272,640]{1,0:T(8,128)(2,1)}) custom-call(bf16[4,4,16,576]{3,2,1,0:T(8,128)(2,1)} %q_hbm.1, bf16[4,4,8,128]{3,2,1,0:T(8,128)(2,1)} %iq_hbm.1, bf16[4,4,8]{2,1,0:T(4,128)(2,1)} %iw_hbm.1), custom_call_target="tpu_custom_call" | custom-call | flops 2000000000 | bytes 6000000 | tf_op jit(solution)/shard_map/pack/pallas_call | solution.py:93
  2.8 3.0 %collective-permute-start.1 = (bf16[272,640]{1,0:T(8,128)(2,1)}, bf16[272,640]{1,0:T(8,128)(2,1)S(1)}, u32[]{:S(2)}, u32[]{:S(2)}) collective-permute-start(bf16[272,640]{1,0:T(8,128)(2,1)} %get-tuple-element.49), channel_id=1, source_target_pairs={{0,4},{4,0},{8,12},{12,8},{16,20},{20,16},{24,28},{28,24},{1,5},{5... | collective-permute-start | bytes 1044488 | tf_op jit(solution)/shard_map/ppermute | solution.py:586
  5.8 2.6 %collective-permute-start = (bf16[136,640]{1,0:T(8,128)(2,1)}, bf16[136,640]{1,0:T(8,128)(2,1)S(1)}, u32[]{:S(2)}, u32[]{:S(2)}) collective-permute-start(bf16[136,640]{1,0:T(8,128)(2,1)} %get-tuple-element.47.refs_0_), channel_id=1, source_target_pairs={{0,16},{4,20},{8,24},{12,28},{16,0},{20,4},{24,8},{28,12},{1,17},{... | collective-permute-start | bytes 522248 | tf_op jit(solution)/shard_map/ppermute | solution.py:589
  8.4 1.6 %collective-permute-start.2 = (bf16[136,640]{1,0:T(8,128)(2,1)}, bf16[136,640]{1,0:T(8,128)(2,1)S(1)}, u32[]{:S(2)}, u32[]{:S(2)}) collective-permute-start(bf16[136,640]{1,0:T(8,128)(2,1)} %get-tuple-element.47.refs_0_), channel_id=1, source_target_pairs={{0,8},{4,12},{8,0},{12,4},{16,24},{20,28},{24,16},{28,20},{1,9},{5... | collective-permute-start | bytes 522248 | tf_op jit(solution)/shard_map/ppermute | solution.py:589
  12.9 3.8 %collective-permute-done.second_ref.refs_2_ = bf16[136,640]{1,0:T(8,128)(2,1)S(1)} collective-permute-done((bf16[136,640]{1,0:T(8,128)(2,1)}, bf16[136,640]{1,0:T(8,128)(2,1)S(1)}, u32[]{:S(2)}, u32[]{:S(2)}) %collective-permute-start) | collective-permute-done | bytes 174112 | tf_op jit(solution)/shard_map/ppermute | solution.py:589
  16.8 1.5 %collective-permute-start.10 = (bf16[16,128,128]{2,1,0:T(8,128)(2,1)S(1)}, bf16[16,128,128]{2,1,0:T(8,128)(2,1)S(1)}, u32[]{:S(2)}, u32[]{:S(2)}) collective-permute-start(bf16[16,128,128]{2,1,0:T(8,128)(2,1)S(1)} %copy-done), channel_id=1, source_target_pairs={{0,2},{1,3},{2,0},{3,1},{4,6},{5,7},{6,4},{7,5},{8,10},{9,11},{10,... | collective-permute-start | bytes 1572872 | tf_op jit(solution)/shard_map/ppermute | solution.py:592
  20.3 2.5 %collective-permute-start.3 = (bf16[136,640]{1,0:T(8,128)(2,1)S(1)}, bf16[136,640]{1,0:T(8,128)(2,1)S(1)}, u32[]{:S(2)}, u32[]{:S(2)}) collective-permute-start(bf16[136,640]{1,0:T(8,128)(2,1)S(1)} %collective-permute-done.second_ref.refs_2_), channel_id=1, source_target_pairs={{0,8},{4,12},{8,0},{12,4},{16,24},{20,28},{24,16},{28,20},{1,9},{5... | collective-permute-start | bytes 522248 | tf_op jit(solution)/shard_map/ppermute | solution.py:589
  22.8 4.8 %gather_blocks.2.refs_8_ = bf16[8,576,1024]{2,1,0:T(8,128)(2,1)S(1)} custom-call(s32[16,32]{1,0:T(8,128)S(1)} %plan.1.table_ref, bf16[4,576,2048]{2,1,0:T(8,128)(2,1)} %bitcast.1), custom_call_target="tpu_custom_call" | custom-call | flops 5000000000 | bytes 15000000 | tf_op jit(solution)/shard_map/gather_blocks/pallas_call | solution.py:252
  27.6 2.8 %collective-permute-done.5.second_ref.refs_2_.refs_10_ = bf16[136,640]{1,0:T(8,128)(2,1)S(1)} collective-permute-done((bf16[136,640]{1,0:T(8,128)(2,1)}, bf16[136,640]{1,0:T(8,128)(2,1)S(1)}, u32[]{:S(2)}, u32[]{:S(2)}) %collective-permute-start.5) | collective-permute-done | bytes 174112 | tf_op jit(solution)/shard_map/ppermute | solution.py:589
  30.9 1.6 %collective-permute-start.7 = (bf16[136,640]{1,0:T(8,128)(2,1)S(1)}, bf16[136,640]{1,0:T(8,128)(2,1)S(1)}, u32[]{:S(2)}, u32[]{:S(2)}) collective-permute-start(bf16[136,640]{1,0:T(8,128)(2,1)S(1)} %copy-done.3), channel_id=1, source_target_pairs={{0,8},{4,12},{8,0},{12,4},{16,24},{20,28},{24,16},{28,20},{1,9},{5... | collective-permute-start | bytes 522248 | tf_op jit(solution)/shard_map/ppermute | solution.py:589
  32.5 1.6 %collective-permute-start.6 = (bf16[272,640]{1,0:T(8,128)(2,1)S(1)}, bf16[272,640]{1,0:T(8,128)(2,1)S(1)}, u32[]{:S(2)}, u32[]{:S(2)}) collective-permute-start(bf16[272,640]{1,0:T(8,128)(2,1)S(1)} %pair_up.3), channel_id=1, source_target_pairs={{0,4},{4,0},{8,12},{12,8},{16,20},{20,16},{24,28},{28,24},{1,5},{5... | collective-permute-start | bytes 1044488 | tf_op jit(solution)/shard_map/ppermute | solution.py:586
  34.0 5.0 %gather_blocks.3.refs_8_ = bf16[8,576,1024]{2,1,0:T(8,128)(2,1)S(1)} custom-call(s32[16,32]{1,0:T(8,128)S(1)} %plan.1.table_ref, bf16[4,576,2048]{2,1,0:T(8,128)(2,1)} %bitcast.2), custom_call_target="tpu_custom_call" | custom-call | flops 5000000000 | bytes 15000000 | tf_op jit(solution)/shard_map/gather_blocks/pallas_call | solution.py:252
  39.9 1.6 %collective-permute-done.6.both_ref.refs_7_ = bf16[272,640]{1,0:T(8,128)(2,1)S(1)} collective-permute-done((bf16[272,640]{1,0:T(8,128)(2,1)S(1)}, bf16[272,640]{1,0:T(8,128)(2,1)S(1)}, u32[]{:S(2)}, u32[]{:S(2)}) %collective-permute-start.6) | collective-permute-done | bytes 348192 | tf_op jit(solution)/shard_map/ppermute | solution.py:586
  43.5 3.4 %attend.2 = (bf16[256,512]{1,0:T(8,128)(2,1)S(1)}, bf16[256,512]{1,0:T(8,128)(2,1)S(1)}, bf16[256,512]{1,0:T(8,128)(2,1)S(1)}, bf16[136,512]{1,0:T(8,128)(2,1)S(...) custom-call(s32[16,32]{1,0:T(8,128)S(1)} %plan.1.table_ref, bf16[136,640]{1,0:T(8,128)(2,1)S(1)} %copy-done.2, ...), custom_call_target="tpu_custom_call" | custom-call | flops 3600000000 | bytes 10800000 | tf_op jit(solution)/shard_map/attend/pallas_call | solution.py:343
  47.5 1.6 %collective-permute-start.16 = (bf16[136,512]{1,0:T(8,128)(2,1)S(1)}, bf16[136,512]{1,0:T(8,128)(2,1)S(1)}, u32[]{:S(2)}, u32[]{:S(2)}) collective-permute-start(bf16[136,512]{1,0:T(8,128)(2,1)S(1)} %get-tuple-element.75), channel_id=1, source_target_pairs={{0,8},{4,12},{8,0},{12,4},{16,24},{20,28},{24,16},{28,20},{1,9},{5... | collective-permute-start | bytes 417800 | tf_op jit(solution)/shard_map/ppermute | solution.py:589
  49.2 3.7 %attend.3 = (bf16[256,512]{1,0:T(8,128)(2,1)S(1)}, bf16[256,512]{1,0:T(8,128)(2,1)S(1)}, bf16[256,512]{1,0:T(8,128)(2,1)S(1)}, bf16[136,512]{1,0:T(8,128)(2,1)S(...) custom-call(s32[16,32]{1,0:T(8,128)S(1)} %plan.1.table_ref, bf16[136,640]{1,0:T(8,128)(2,1)S(1)} %copy-done.3, ...), custom_call_target="tpu_custom_call" | custom-call | flops 3600000000 | bytes 10800000 | tf_op jit(solution)/shard_map/attend/pallas_call | solution.py:343
  52.9 1.5 %collective-permute-start.14 = (bf16[136,512]{1,0:T(8,128)(2,1)S(1)}, bf16[136,512]{1,0:T(8,128)(2,1)S(1)}, u32[]{:S(2)}, u32[]{:S(2)}) collective-permute-start(bf16[136,512]{1,0:T(8,128)(2,1)S(1)} %get-tuple-element.69), channel_id=1, source_target_pairs={{0,4},{4,0},{8,12},{12,8},{16,20},{20,16},{24,28},{28,24},{1,5},{5... | collective-permute-start | bytes 417800 | tf_op jit(solution)/shard_map/ppermute | solution.py:586
  57.4 1.8 %collective-permute-done.14.from_x = bf16[136,512]{1,0:T(8,128)(2,1)S(1)} collective-permute-done((bf16[136,512]{1,0:T(8,128)(2,1)S(1)}, bf16[136,512]{1,0:T(8,128)(2,1)S(1)}, u32[]{:S(2)}, u32[]{:S(2)}) %collective-permute-start.14) | collective-permute-done | bytes 139296 | tf_op jit(solution)/shard_map/ppermute | solution.py:586
  59.2 1.5 %collective-permute-done.17.from_z = bf16[136,512]{1,0:T(8,128)(2,1)S(1)} collective-permute-done((bf16[136,512]{1,0:T(8,128)(2,1)S(1)}, bf16[136,512]{1,0:T(8,128)(2,1)S(1)}, u32[]{:S(2)}, u32[]{:S(2)}) %collective-permute-start.17) | collective-permute-done | bytes 139296 | tf_op jit(solution)/shard_map/ppermute | solution.py:589
  62.6 1.8 %collective-permute-done.21.from_x = bf16[264,512]{1,0:T(8,128)(2,1)S(1)} collective-permute-done((bf16[264,512]{1,0:T(8,128)(2,1)S(1)}, bf16[264,512]{1,0:T(8,128)(2,1)S(1)}, u32[]{:S(2)}, u32[]{:S(2)}) %collective-permute-start.21) | collective-permute-done | bytes 270368 | tf_op jit(solution)/shard_map/ppermute | solution.py:586
  64.4 2.4 %collective-permute-done.22.from_z = bf16[264,512]{1,0:T(8,128)(2,1)S(1)} collective-permute-done((bf16[264,512]{1,0:T(8,128)(2,1)S(1)}, bf16[264,512]{1,0:T(8,128)(2,1)S(1)}, u32[]{:S(2)}, u32[]{:S(2)}) %collective-permute-start.22) | collective-permute-done | bytes 270368 | tf_op jit(solution)/shard_map/ppermute | solution.py:589
  67.2 2.3 %collective-permute-start.23 = (bf16[136,512]{1,0:T(8,128)(2,1)S(1)}, bf16[136,512]{1,0:T(8,128)(2,1)S(1)}, u32[]{:S(2)}, u32[]{:S(2)}) collective-permute-start(bf16[136,512]{1,0:T(8,128)(2,1)S(1)} %get-tuple-element.90), channel_id=1, source_target_pairs={{0,16},{4,20},{8,24},{12,28},{16,0},{20,4},{24,8},{28,12},{1,17},{... | collective-permute-start | bytes 417800 | tf_op jit(solution)/shard_map/ppermute | solution.py:589
  70.1 4.3 %collective-permute-start.20 = (bf16[136,512]{1,0:T(8,128)(2,1)S(1)}, bf16[136,512]{1,0:T(8,128)(2,1)S(1)}, u32[]{:S(2)}, u32[]{:S(2)}) collective-permute-start(bf16[136,512]{1,0:T(8,128)(2,1)S(1)} %get-tuple-element.84), channel_id=1, source_target_pairs={{0,16},{4,20},{8,24},{12,28},{16,0},{20,4},{24,8},{28,12},{1,17},{... | collective-permute-start | bytes 417800 | tf_op jit(solution)/shard_map/ppermute | solution.py:589
  74.4 3.5 %index_scores.1 = f32[4,4,2048]{2,1,0:T(4,128)} custom-call(s32[16,32]{1,0:T(8,128)S(1)} %plan.1.table_ref, bf16[136,640]{1,0:T(8,128)(2,1)S(1)} %copy-done.2, bf16[136,640]{1,0:T(8,128)(2,1)S(1)} %collective-permute-done.2.first_ref.refs_1_, bf16[136,640]{1,0:T(8,128)(2,1)S(1)} %collective-permute-done.second_ref.refs_2_, ...), custom_call_target="tpu_custom_call" | custom-call | flops 3500000000 | bytes 10500000 | tf_op jit(solution)/shard_map/index_scores/pallas_call | solution.py:559
  (55 shorter events, 17.4 us)
Async XLA Ops:
  2.8 14.0 %collective-permute-start.1 = (bf16[272,640]{1,0:T(8,128)(2,1)}, bf16[272,640]{1,0:T(8,128)(2,1)S(1)}, u32[]{:S(2)}, u32[]{:S(2)}) collective-permute-start(bf16[272,640]{1,0:T(8,128)(2,1)} %get-tuple-element.49), channel_id=1, source_target_pairs={{0,4},{4,0},{8,12},{12,8},{16,20},{20,16},{24,28},{28,24},{1,5},{5... | collective-permute-start | bytes 1044488 | tf_op jit(solution)/shard_map/ppermute | solution.py:586
  5.8 10.8 %collective-permute-start = (bf16[136,640]{1,0:T(8,128)(2,1)}, bf16[136,640]{1,0:T(8,128)(2,1)S(1)}, u32[]{:S(2)}, u32[]{:S(2)}) collective-permute-start(bf16[136,640]{1,0:T(8,128)(2,1)} %get-tuple-element.47.refs_0_), channel_id=1, source_target_pairs={{0,16},{4,20},{8,24},{12,28},{16,0},{20,4},{24,8},{28,12},{1,17},{... | collective-permute-start | bytes 522248 | tf_op jit(solution)/shard_map/ppermute | solution.py:589
  8.4 8.4 %collective-permute-start.2 = (bf16[136,640]{1,0:T(8,128)(2,1)}, bf16[136,640]{1,0:T(8,128)(2,1)S(1)}, u32[]{:S(2)}, u32[]{:S(2)}) collective-permute-start(bf16[136,640]{1,0:T(8,128)(2,1)} %get-tuple-element.47.refs_0_), channel_id=1, source_target_pairs={{0,8},{4,12},{8,0},{12,4},{16,24},{20,28},{24,16},{28,20},{1,9},{5... | collective-permute-start | bytes 522248 | tf_op jit(solution)/shard_map/ppermute | solution.py:589
  16.8 17.2 %collective-permute-start.10 = (bf16[16,128,128]{2,1,0:T(8,128)(2,1)S(1)}, bf16[16,128,128]{2,1,0:T(8,128)(2,1)S(1)}, u32[]{:S(2)}, u32[]{:S(2)}) collective-permute-start(bf16[16,128,128]{2,1,0:T(8,128)(2,1)S(1)} %copy-done), channel_id=1, source_target_pairs={{0,2},{1,3},{2,0},{3,1},{4,6},{5,7},{6,4},{7,5},{8,10},{9,11},{10,... | collective-permute-start | bytes 1572872 | tf_op jit(solution)/shard_map/ppermute | solution.py:592
  18.4 29.1 %collective-permute-start.9 = (bf16[16,128,128]{2,1,0:T(8,128)(2,1)S(1)}, bf16[16,128,128]{2,1,0:T(8,128)(2,1)S(1)}, u32[]{:S(2)}, u32[]{:S(2)}) collective-permute-start(bf16[16,128,128]{2,1,0:T(8,128)(2,1)S(1)} %copy-done), channel_id=1, source_target_pairs={{0,1},{1,0},{2,3},{3,2},{4,5},{5,4},{6,7},{7,6},{8,9},{9,8},{10,11... | collective-permute-start | bytes 1572872 | tf_op jit(solution)/shard_map/ppermute | solution.py:592
  18.4 12.0 %collective-permute-start.4 = (bf16[272,640]{1,0:T(8,128)(2,1)S(1)}, bf16[272,640]{1,0:T(8,128)(2,1)S(1)}, u32[]{:S(2)}, u32[]{:S(2)}) collective-permute-start(bf16[272,640]{1,0:T(8,128)(2,1)S(1)} %pair_up.2), channel_id=1, source_target_pairs={{0,4},{4,0},{8,12},{12,8},{16,20},{20,16},{24,28},{28,24},{1,5},{5... | collective-permute-start | bytes 1044488 | tf_op jit(solution)/shard_map/ppermute | solution.py:586
  19.0 11.4 %collective-permute-start.5 = (bf16[136,640]{1,0:T(8,128)(2,1)}, bf16[136,640]{1,0:T(8,128)(2,1)S(1)}, u32[]{:S(2)}, u32[]{:S(2)}) collective-permute-start(bf16[136,640]{1,0:T(8,128)(2,1)} %get-tuple-element.56.refs_0_.refs_8_), channel_id=1, source_target_pairs={{0,16},{4,20},{8,24},{12,28},{16,0},{20,4},{24,8},{28,12},{1,17},{... | collective-permute-start | bytes 522248 | tf_op jit(solution)/shard_map/ppermute | solution.py:589
  20.3 10.1 %collective-permute-start.3 = (bf16[136,640]{1,0:T(8,128)(2,1)S(1)}, bf16[136,640]{1,0:T(8,128)(2,1)S(1)}, u32[]{:S(2)}, u32[]{:S(2)}) collective-permute-start(bf16[136,640]{1,0:T(8,128)(2,1)S(1)} %collective-permute-done.second_ref.refs_2_), channel_id=1, source_target_pairs={{0,8},{4,12},{8,0},{12,4},{16,24},{20,28},{24,16},{28,20},{1,9},{5... | collective-permute-start | bytes 522248 | tf_op jit(solution)/shard_map/ppermute | solution.py:589
  30.4 8.6 %collective-permute-start.8 = (bf16[136,640]{1,0:T(8,128)(2,1)S(1)}, bf16[136,640]{1,0:T(8,128)(2,1)S(1)}, u32[]{:S(2)}, u32[]{:S(2)}) collective-permute-start(bf16[136,640]{1,0:T(8,128)(2,1)S(1)} %collective-permute-done.5.second_ref.refs_2_.refs_10_), channel_id=1, source_target_pairs={{0,8},{4,12},{8,0},{12,4},{16,24},{20,28},{24,16},{28,20},{1,9},{5... | collective-permute-start | bytes 522248 | tf_op jit(solution)/shard_map/ppermute | solution.py:589
  30.9 9.0 %collective-permute-start.7 = (bf16[136,640]{1,0:T(8,128)(2,1)S(1)}, bf16[136,640]{1,0:T(8,128)(2,1)S(1)}, u32[]{:S(2)}, u32[]{:S(2)}) collective-permute-start(bf16[136,640]{1,0:T(8,128)(2,1)S(1)} %copy-done.3), channel_id=1, source_target_pairs={{0,8},{4,12},{8,0},{12,4},{16,24},{20,28},{24,16},{28,20},{1,9},{5... | collective-permute-start | bytes 522248 | tf_op jit(solution)/shard_map/ppermute | solution.py:589
  32.5 9.0 %collective-permute-start.6 = (bf16[272,640]{1,0:T(8,128)(2,1)S(1)}, bf16[272,640]{1,0:T(8,128)(2,1)S(1)}, u32[]{:S(2)}, u32[]{:S(2)}) collective-permute-start(bf16[272,640]{1,0:T(8,128)(2,1)S(1)} %pair_up.3), channel_id=1, source_target_pairs={{0,4},{4,0},{8,12},{12,8},{16,20},{20,16},{24,28},{28,24},{1,5},{5... | collective-permute-start | bytes 1044488 | tf_op jit(solution)/shard_map/ppermute | solution.py:586
  34.0 15.0 %collective-permute-start.11 = (bf16[16,128,128]{2,1,0:T(8,128)(2,1)S(1)}, bf16[16,128,128]{2,1,0:T(8,128)(2,1)S(1)}, u32[]{:S(2)}, u32[]{:S(2)}) collective-permute-start(bf16[16,128,128]{2,1,0:T(8,128)(2,1)S(1)} %collective-permute-done.10.refs_2_), channel_id=1, source_target_pairs={{0,1},{1,0},{2,3},{3,2},{4,5},{5,4},{6,7},{7,6},{8,9},{9,8},{10,11... | collective-permute-start | bytes 1572872 | tf_op jit(solution)/shard_map/ppermute | solution.py:592
  41.4 7.8 %collective-permute-start.13 = (bf16[136,640]{1,0:T(8,128)(2,1)S(1)}, bf16[136,640]{1,0:T(8,128)(2,1)S(1)}, u32[]{:S(2)}, u32[]{:S(2)}) collective-permute-start(bf16[136,640]{1,0:T(8,128)(2,1)S(1)} %second_of.1.refs_6_.refs_14_), channel_id=1, source_target_pairs={{0,8},{4,12},{8,0},{12,4},{16,24},{20,28},{24,16},{28,20},{1,9},{5... | collective-permute-start | bytes 522248 | tf_op jit(solution)/shard_map/ppermute | solution.py:589
  42.0 7.2 %collective-permute-start.12 = (bf16[136,640]{1,0:T(8,128)(2,1)S(1)}, bf16[136,640]{1,0:T(8,128)(2,1)S(1)}, u32[]{:S(2)}, u32[]{:S(2)}) collective-permute-start(bf16[136,640]{1,0:T(8,128)(2,1)S(1)} %collective-permute-done.7.refs_1_.refs_9_), channel_id=1, source_target_pairs={{0,4},{4,0},{8,12},{12,8},{16,20},{20,16},{24,28},{28,24},{1,5},{5... | collective-permute-start | bytes 522248 | tf_op jit(solution)/shard_map/ppermute | solution.py:586
  46.9 8.6 %collective-permute-start.15 = (bf16[136,512]{1,0:T(8,128)(2,1)S(1)}, bf16[136,512]{1,0:T(8,128)(2,1)S(1)}, u32[]{:S(2)}, u32[]{:S(2)}) collective-permute-start(bf16[136,512]{1,0:T(8,128)(2,1)S(1)} %get-tuple-element.72), channel_id=1, source_target_pairs={{0,4},{4,0},{8,12},{12,8},{16,20},{20,16},{24,28},{28,24},{1,5},{5... | collective-permute-start | bytes 417800 | tf_op jit(solution)/shard_map/ppermute | solution.py:586
  47.5 8.0 %collective-permute-start.16 = (bf16[136,512]{1,0:T(8,128)(2,1)S(1)}, bf16[136,512]{1,0:T(8,128)(2,1)S(1)}, u32[]{:S(2)}, u32[]{:S(2)}) collective-permute-start(bf16[136,512]{1,0:T(8,128)(2,1)S(1)} %get-tuple-element.75), channel_id=1, source_target_pairs={{0,8},{4,12},{8,0},{12,4},{16,24},{20,28},{24,16},{28,20},{1,9},{5... | collective-permute-start | bytes 417800 | tf_op jit(solution)/shard_map/ppermute | solution.py:589
  52.9 6.3 %collective-permute-start.14 = (bf16[136,512]{1,0:T(8,128)(2,1)S(1)}, bf16[136,512]{1,0:T(8,128)(2,1)S(1)}, u32[]{:S(2)}, u32[]{:S(2)}) collective-permute-start(bf16[136,512]{1,0:T(8,128)(2,1)S(1)} %get-tuple-element.69), channel_id=1, source_target_pairs={{0,4},{4,0},{8,12},{12,8},{16,20},{20,16},{24,28},{28,24},{1,5},{5... | collective-permute-start | bytes 417800 | tf_op jit(solution)/shard_map/ppermute | solution.py:586
  54.4 6.2 %collective-permute-start.17 = (bf16[136,512]{1,0:T(8,128)(2,1)S(1)}, bf16[136,512]{1,0:T(8,128)(2,1)S(1)}, u32[]{:S(2)}, u32[]{:S(2)}) collective-permute-start(bf16[136,512]{1,0:T(8,128)(2,1)S(1)} %get-tuple-element.78), channel_id=1, source_target_pairs={{0,8},{4,12},{8,0},{12,4},{16,24},{20,28},{24,16},{28,20},{1,9},{5... | collective-permute-start | bytes 417800 | tf_op jit(solution)/shard_map/ppermute | solution.py:589
  55.9 8.5 %collective-permute-start.21 = (bf16[264,512]{1,0:T(8,128)(2,1)S(1)}, bf16[264,512]{1,0:T(8,128)(2,1)S(1)}, u32[]{:S(2)}, u32[]{:S(2)}) collective-permute-start(bf16[264,512]{1,0:T(8,128)(2,1)S(1)} %get-tuple-element.86), channel_id=1, source_target_pairs={{0,4},{4,0},{8,12},{12,8},{16,20},{20,16},{24,28},{28,24},{1,5},{5... | collective-permute-start | bytes 811016 | tf_op jit(solution)/shard_map/ppermute | solution.py:586
  56.0 10.8 %collective-permute-start.22 = (bf16[264,512]{1,0:T(8,128)(2,1)S(1)}, bf16[264,512]{1,0:T(8,128)(2,1)S(1)}, u32[]{:S(2)}, u32[]{:S(2)}) collective-permute-start(bf16[264,512]{1,0:T(8,128)(2,1)S(1)} %get-tuple-element.87), channel_id=1, source_target_pairs={{0,8},{4,12},{8,0},{12,4},{16,24},{20,28},{24,16},{28,20},{1,9},{5... | collective-permute-start | bytes 811016 | tf_op jit(solution)/shard_map/ppermute | solution.py:589
  61.0 8.4 %collective-permute-start.18 = (bf16[264,512]{1,0:T(8,128)(2,1)S(1)}, bf16[264,512]{1,0:T(8,128)(2,1)S(1)}, u32[]{:S(2)}, u32[]{:S(2)}) collective-permute-start(bf16[264,512]{1,0:T(8,128)(2,1)S(1)} %get-tuple-element.79), channel_id=1, source_target_pairs={{0,4},{4,0},{8,12},{12,8},{16,20},{20,16},{24,28},{28,24},{1,5},{5... | collective-permute-start | bytes 811016 | tf_op jit(solution)/shard_map/ppermute | solution.py:586
  61.4 8.3 %collective-permute-start.19 = (bf16[264,512]{1,0:T(8,128)(2,1)S(1)}, bf16[264,512]{1,0:T(8,128)(2,1)S(1)}, u32[]{:S(2)}, u32[]{:S(2)}) collective-permute-start(bf16[264,512]{1,0:T(8,128)(2,1)S(1)} %get-tuple-element.80), channel_id=1, source_target_pairs={{0,8},{4,12},{8,0},{12,4},{16,24},{20,28},{24,16},{28,20},{1,9},{5... | collective-permute-start | bytes 811016 | tf_op jit(solution)/shard_map/ppermute | solution.py:589
  67.2 10.7 %collective-permute-start.23 = (bf16[136,512]{1,0:T(8,128)(2,1)S(1)}, bf16[136,512]{1,0:T(8,128)(2,1)S(1)}, u32[]{:S(2)}, u32[]{:S(2)}) collective-permute-start(bf16[136,512]{1,0:T(8,128)(2,1)S(1)} %get-tuple-element.90), channel_id=1, source_target_pairs={{0,16},{4,20},{8,24},{12,28},{16,0},{20,4},{24,8},{28,12},{1,17},{... | collective-permute-start | bytes 417800 | tf_op jit(solution)/shard_map/ppermute | solution.py:589
  70.1 9.1 %collective-permute-start.20 = (bf16[136,512]{1,0:T(8,128)(2,1)S(1)}, bf16[136,512]{1,0:T(8,128)(2,1)S(1)}, u32[]{:S(2)}, u32[]{:S(2)}) collective-permute-start(bf16[136,512]{1,0:T(8,128)(2,1)S(1)} %get-tuple-element.84), channel_id=1, source_target_pairs={{0,16},{4,20},{8,24},{12,28},{16,0},{20,4},{24,8},{28,12},{1,17},{... | collective-permute-start | bytes 417800 | tf_op jit(solution)/shard_map/ppermute | solution.py:589
  (7 other events, 62.5 us)

commit v4 on v3

--- a/solution.py
+++ b/solution.py
@@ -484,22 +484,36 @@
     )(*args)
 
 
-def assemble_kernel(_, *refs):
-    out_ref = refs[-1]
-    own = lax.axis_index("req")
-    for relative, ref in enumerate(refs[:-1]):
-        start = pl.multiple_of((own ^ relative) * 128, 128)
-        out_ref[:, pl.ds(start, 128), :] = ref[...]
-
-
-def assemble(earlier, pieces):
+def pair_cores_kernel(own_ref, core_ref, out_ref):
+    own = lax.axis_index("req") % 2
+    out_ref[own] = own_ref[...]
+    out_ref[1 - own] = core_ref[...]
+
+
+def pair_cores(own, core):
+    return call(
+        pair_cores_kernel,
+        out_shape=jax.ShapeDtypeStruct((2, *own.shape), own.dtype),
+        name="pair_cores",
+    )(own, core)
+
+
+def assemble_kernel(_, here_ref, there_ref, out_ref):
+    row = lax.axis_index("req") // 2
+    for core in range(2):
+        for place, ref in ((row, here_ref), (1 - row, there_ref)):
+            start = pl.multiple_of((2 * place + core) * 128, 128)
+            out_ref[:, pl.ds(start, 128), :] = ref[core]
+
+
+def assemble(earlier, here, there):
     return call(
         assemble_kernel,
-        in_specs=[pl.BlockSpec(memory_space=pl.ANY)] + [pl.BlockSpec()] * 4,
+        in_specs=[pl.BlockSpec(memory_space=pl.ANY)] + [pl.BlockSpec()] * 2,
         out_shape=jax.ShapeDtypeStruct((HEADS, KV, 128), jnp.bfloat16),
         name="assemble_up",
         us=1.0,
-    )(earlier, *pieces)
+    )(earlier, here, there)
 
 
 def index_kernel(offsets, table_ref, *refs):
@@ -604,7 +618,6 @@
     z2c1 = across_z(after(own1, *round1), 2)
     blocks0 = gather(0, after(table, *round1), latents_t)
 
-    up_y = across_req(after(value_up_weight, *round1), 2)
     up_core = across_req(after(value_up_weight, *round1), 1)
 
     round2 = (x12, z3c0, z2c1, blocks0)
@@ -612,7 +625,8 @@
     z1c1 = across_z(after(own1, *round2), 1)
     z3c1 = across_z(after(z2c1, *round2), 1)
     blocks1 = gather(1, after(table, *round2), latents_t)
-    up_both = across_req(after(up_y, *round2), 1)
+    up_here = pair_cores(after(value_up_weight, *round2), up_core)
+    up_there = across_req(up_here, 2)
 
     round3 = (x32, z1c1, z3c1, blocks1)
     xz1c1 = across_x(after(z1c1, *round3))
@@ -625,8 +639,7 @@
 
     near0, far0, cross0, x5, z7, stats0 = attend(0, after(table, xz2c1), gathered[0], blocks0)
     x5, z7 = across_x(x5), across_z(z7, 1)
-    up = assemble(stats0, [value_up_weight, up_core, up_y, up_both])
-    near1, far1, cross1, x5c1, z7c1, stats1 = attend(1, after(table, up), gathered[1], blocks1)
+    near1, far1, cross1, x5c1, z7c1, stats1 = attend(1, after(table, stats0), gathered[1], blocks1)
     x5c1, z7c1 = across_x(x5c1), across_z(z7c1, 1)
 
     to_z, to_x, stats0 = join_cross(far0, cross0, after(x5, stats1), z7, stats0)
@@ -634,7 +647,8 @@
     to_z, to_x, stats1 = join_cross(far1, cross1, after(x5c1, stats0), z7c1, stats1)
     from_xc1, from_zc1 = across_x(to_x), across_z(to_z, 1)
     index_scores = index_rows(after(table, stats1), gathered, index_keys)
-    message, mine0, stats0 = join_near(near0, from_x, from_z, stats0)
+    up = assemble(index_scores, up_here, up_there)
+    message, mine0, stats0 = join_near(after(near0, index_scores), from_x, from_z, stats0)
     last0 = across_z(message, 2)
     message, mine1, stats1 = join_near(near1, from_xc1, from_zc1, stats1)
     last1 = across_z(message, 2)

time: 80.6 us -> 77.2 us (0.958)
  waiting for transfers between devices: 16.9 us -> 13.4 us
  local copies, waits for them, and re-layouts: 2.05 us -> 2.95 us
  starting transfers between devices: 33.1 us -> 32.2 us
    ppermute x8, waiting for transfers between devices: 5.12 us -> 2.17 us  [across_x(): return lax.ppermute(value, 'ctx', [(i, i ^ 1) for i in range(8)])]
    unnamed x14 -> x16, local copies, waits for them, and re-layouts: 2.05 us -> 2.95 us
    ppermute x13, starting transfers between devices: 22.4 us -> 21.5 us  [across_z(): return lax.ppermute(value, 'ctx', [(i, i ^ 2 * distance) for i in range(8)])]
  transfers between devices with their start and end apart: 24 -> 23, of which waited for: 10 -> 9; matrix products, arithmetic and copies ran while one was open for 0% -> 0% of each run, Pallas kernels for 30% -> 31%
where the time goes in v4:
time: 77.2 us; the launch traced here: 76.9 us
  starting transfers between devices  32.2 us (42%)
  Pallas kernels  27.6 us (36%)
  waiting for transfers between devices  13.4 us (17%)
  local copies, waits for them, and re-layouts  2.95 us (4%)
    ppermute x13, starting transfers between devices, across_z(): return lax.ppermute(value, 'ctx', [(i, i ^ 2 * distance) for i in range(8)])  21.5 us
    ppermute x13, waiting for transfers between devices, across_z(): return lax.ppermute(value, 'ctx', [(i, i ^ 2 * distance) for i in range(8)])  11.2 us
    pallas_call x2, Pallas kernels, gather(): call(functools.partial(gather_kernel, chunk), limit=GATHER_LIMIT[chunk],...  9.74 us
    ppermute x8, starting transfers between devices, across_x(): return lax.ppermute(value, 'ctx', [(i, i ^ 1) for i in range(8)])  9.11 us
    pallas_call x2, Pallas kernels, attend(): call(functools.partial(attend_kernel, chunk, tuple((at for _, at in gathe...  7.12 us
    pallas_call x1, Pallas kernels, index_rows(): call(functools.partial(index_kernel, tuple((at for _, at in members))), g...  3.52 us
    unnamed x16, local copies, waits for them, and re-layouts  2.95 us
    pallas_call x2, Pallas kernels, finish(): call(finish_kernel, grid=(1,), in_specs=specs, out_specs=pl.BlockSpec((4,...  2.42 us
  transfers between devices with their start and end apart: 23, of which 9 were waited for; matrix products, arithmetic and copies ran while one was open for 0% of the time, Pallas kernels for 31%

profile of v4, /device:TPU:0, one launch (start us, length us, event | category | flops | bytes accessed | tf_op | source)
XLA Modules:
  0.0 76.9 jit_solution(12814966974790496558)
XLA Ops:
  0.6 2.2 %pack.1 = (bf16[136,640]{1,0:T(8,128)(2,1)}, bf16[136,640]{1,0:T(8,128)(2,1)}, bf16[272,640]{1,0:T(8,128)(2,1)}) custom-call(bf16[4,4,16,576]{3,2,1,0:T(8,128)(2,1)} %q_hbm.1, bf16[4,4,8,128]{3,2,1,0:T(8,128)(2,1)} %iq_hbm.1, bf16[4,4,8]{2,1,0:T(4,128)(2,1)} %iw_hbm.1), custom_call_target="tpu_custom_call" | custom-call | flops 2000000000 | bytes 6000000 | tf_op jit(solution)/shard_map/pack/pallas_call | solution.py:93
  2.8 3.0 %collective-permute-start.1 = (bf16[272,640]{1,0:T(8,128)(2,1)}, bf16[272,640]{1,0:T(8,128)(2,1)S(1)}, u32[]{:S(2)}, u32[]{:S(2)}) collective-permute-start(bf16[272,640]{1,0:T(8,128)(2,1)} %get-tuple-element.50), channel_id=1, source_target_pairs={{0,4},{4,0},{8,12},{12,8},{16,20},{20,16},{24,28},{28,24},{1,5},{5... | collective-permute-start | bytes 1044488 | tf_op jit(solution)/shard_map/ppermute | solution.py:600
  5.8 2.6 %collective-permute-start = (bf16[136,640]{1,0:T(8,128)(2,1)}, bf16[136,640]{1,0:T(8,128)(2,1)S(1)}, u32[]{:S(2)}, u32[]{:S(2)}) collective-permute-start(bf16[136,640]{1,0:T(8,128)(2,1)} %get-tuple-element.48.refs_0_), channel_id=1, source_target_pairs={{0,16},{4,20},{8,24},{12,28},{16,0},{20,4},{24,8},{28,12},{1,17},{... | collective-permute-start | bytes 522248 | tf_op jit(solution)/shard_map/ppermute | solution.py:603
  8.4 1.6 %collective-permute-start.2 = (bf16[136,640]{1,0:T(8,128)(2,1)}, bf16[136,640]{1,0:T(8,128)(2,1)S(1)}, u32[]{:S(2)}, u32[]{:S(2)}) collective-permute-start(bf16[136,640]{1,0:T(8,128)(2,1)} %get-tuple-element.48.refs_0_), channel_id=1, source_target_pairs={{0,8},{4,12},{8,0},{12,4},{16,24},{20,28},{24,16},{28,20},{1,9},{5... | collective-permute-start | bytes 522248 | tf_op jit(solution)/shard_map/ppermute | solution.py:603
  12.9 3.8 %collective-permute-done.second_ref.refs_2_ = bf16[136,640]{1,0:T(8,128)(2,1)S(1)} collective-permute-done((bf16[136,640]{1,0:T(8,128)(2,1)}, bf16[136,640]{1,0:T(8,128)(2,1)S(1)}, u32[]{:S(2)}, u32[]{:S(2)}) %collective-permute-start) | collective-permute-done | bytes 174112 | tf_op jit(solution)/shard_map/ppermute | solution.py:603
  17.4 1.4 %collective-permute-start.5 = (bf16[136,640]{1,0:T(8,128)(2,1)}, bf16[136,640]{1,0:T(8,128)(2,1)S(1)}, u32[]{:S(2)}, u32[]{:S(2)}) collective-permute-start(bf16[136,640]{1,0:T(8,128)(2,1)} %get-tuple-element.57.refs_0_.refs_8_), channel_id=1, source_target_pairs={{0,16},{4,20},{8,24},{12,28},{16,0},{20,4},{24,8},{28,12},{1,17},{... | collective-permute-start | bytes 522248 | tf_op jit(solution)/shard_map/ppermute | solution.py:603
  18.8 2.4 %collective-permute-start.3 = (bf16[136,640]{1,0:T(8,128)(2,1)S(1)}, bf16[136,640]{1,0:T(8,128)(2,1)S(1)}, u32[]{:S(2)}, u32[]{:S(2)}) collective-permute-start(bf16[136,640]{1,0:T(8,128)(2,1)S(1)} %collective-permute-done.second_ref.refs_2_), channel_id=1, source_target_pairs={{0,8},{4,12},{8,0},{12,4},{16,24},{20,28},{24,16},{28,20},{1,9},{5... | collective-permute-start | bytes 522248 | tf_op jit(solution)/shard_map/ppermute | solution.py:603
  21.2 4.8 %gather_blocks.2.refs_8_ = bf16[8,576,1024]{2,1,0:T(8,128)(2,1)S(1)} custom-call(s32[16,32]{1,0:T(8,128)S(1)} %plan.1.table_ref, bf16[4,576,2048]{2,1,0:T(8,128)(2,1)} %bitcast.1), custom_call_target="tpu_custom_call" | custom-call | flops 5000000000 | bytes 15000000 | tf_op jit(solution)/shard_map/gather_blocks/pallas_call | solution.py:252
  29.2 1.6 %collective-permute-start.6 = (bf16[272,640]{1,0:T(8,128)(2,1)S(1)}, bf16[272,640]{1,0:T(8,128)(2,1)S(1)}, u32[]{:S(2)}, u32[]{:S(2)}) collective-permute-start(bf16[272,640]{1,0:T(8,128)(2,1)S(1)} %pair_up.3), channel_id=1, source_target_pairs={{0,4},{4,0},{8,12},{12,8},{16,20},{20,16},{24,28},{28,24},{1,5},{5... | collective-permute-start | bytes 1044488 | tf_op jit(solution)/shard_map/ppermute | solution.py:600
  30.8 5.0 %gather_blocks.3.refs_8_ = bf16[8,576,1024]{2,1,0:T(8,128)(2,1)S(1)} custom-call(s32[16,32]{1,0:T(8,128)S(1)} %plan.1.table_ref, bf16[4,576,2048]{2,1,0:T(8,128)(2,1)} %bitcast.2), custom_call_target="tpu_custom_call" | custom-call | flops 5000000000 | bytes 15000000 | tf_op jit(solution)/shard_map/gather_blocks/pallas_call | solution.py:252
  35.8 1.6 %collective-permute-start.19 = (bf16[2,16,128,128]{3,2,1,0:T(8,128)(2,1)S(1)}, bf16[2,16,128,128]{3,2,1,0:T(8,128)(2,1)S(1)}, u32[]{:S(2)}, u32[]{:S(2)}) collective-permute-start(bf16[2,16,128,128]{3,2,1,0:T(8,128)(2,1)S(1)} %pair_cores.1.here_ref), channel_id=1, source_target_pairs={{0,2},{1,3},{2,0},{3,1},{4,6},{5,7},{6,4},{7,5},{8,10},{9,11},{10,... | collective-permute-start | bytes 3145736 | tf_op jit(solution)/shard_map/ppermute | solution.py:606
  38.8 1.5 %collective-permute-start.9 = (bf16[136,640]{1,0:T(8,128)(2,1)S(1)}, bf16[136,640]{1,0:T(8,128)(2,1)S(1)}, u32[]{:S(2)}, u32[]{:S(2)}) collective-permute-start(bf16[136,640]{1,0:T(8,128)(2,1)S(1)} %collective-permute-done.7.refs_1_.refs_9_), channel_id=1, source_target_pairs={{0,4},{4,0},{8,12},{12,8},{16,20},{20,16},{24,28},{28,24},{1,5},{5... | collective-permute-start | bytes 522248 | tf_op jit(solution)/shard_map/ppermute | solution.py:600
  40.3 3.4 %attend.2 = (bf16[256,512]{1,0:T(8,128)(2,1)S(1)}, bf16[256,512]{1,0:T(8,128)(2,1)S(1)}, bf16[256,512]{1,0:T(8,128)(2,1)S(1)}, bf16[136,512]{1,0:T(8,128)(2,1)S(...) custom-call(s32[16,32]{1,0:T(8,128)S(1)} %plan.1.table_ref, bf16[136,640]{1,0:T(8,128)(2,1)S(1)} %copy-done.3, ...), custom_call_target="tpu_custom_call" | custom-call | flops 3600000000 | bytes 10800000 | tf_op jit(solution)/shard_map/attend/pallas_call | solution.py:343
  44.3 1.6 %collective-permute-start.13 = (bf16[136,512]{1,0:T(8,128)(2,1)S(1)}, bf16[136,512]{1,0:T(8,128)(2,1)S(1)}, u32[]{:S(2)}, u32[]{:S(2)}) collective-permute-start(bf16[136,512]{1,0:T(8,128)(2,1)S(1)} %get-tuple-element.74), channel_id=1, source_target_pairs={{0,8},{4,12},{8,0},{12,4},{16,24},{20,28},{24,16},{28,20},{1,9},{5... | collective-permute-start | bytes 417800 | tf_op jit(solution)/shard_map/ppermute | solution.py:603
  45.9 3.7 %attend.3 = (bf16[256,512]{1,0:T(8,128)(2,1)S(1)}, bf16[256,512]{1,0:T(8,128)(2,1)S(1)}, bf16[256,512]{1,0:T(8,128)(2,1)S(1)}, bf16[136,512]{1,0:T(8,128)(2,1)S(...) custom-call(s32[16,32]{1,0:T(8,128)S(1)} %plan.1.table_ref, bf16[136,640]{1,0:T(8,128)(2,1)S(1)} %copy-done.4, ...), custom_call_target="tpu_custom_call" | custom-call | flops 3600000000 | bytes 10800000 | tf_op jit(solution)/shard_map/attend/pallas_call | solution.py:343
  49.6 1.5 %collective-permute-start.11 = (bf16[136,512]{1,0:T(8,128)(2,1)S(1)}, bf16[136,512]{1,0:T(8,128)(2,1)S(1)}, u32[]{:S(2)}, u32[]{:S(2)}) collective-permute-start(bf16[136,512]{1,0:T(8,128)(2,1)S(1)} %get-tuple-element.68), channel_id=1, source_target_pairs={{0,4},{4,0},{8,12},{12,8},{16,20},{20,16},{24,28},{28,24},{1,5},{5... | collective-permute-start | bytes 417800 | tf_op jit(solution)/shard_map/ppermute | solution.py:600
  54.1 1.3 %collective-permute-done.11.from_x = bf16[136,512]{1,0:T(8,128)(2,1)S(1)} collective-permute-done((bf16[136,512]{1,0:T(8,128)(2,1)S(1)}, bf16[136,512]{1,0:T(8,128)(2,1)S(1)}, u32[]{:S(2)}, u32[]{:S(2)}) %collective-permute-start.11) | collective-permute-done | bytes 139296 | tf_op jit(solution)/shard_map/ppermute | solution.py:600
  55.4 1.7 %collective-permute-done.14.from_z = bf16[136,512]{1,0:T(8,128)(2,1)S(1)} collective-permute-done((bf16[136,512]{1,0:T(8,128)(2,1)S(1)}, bf16[136,512]{1,0:T(8,128)(2,1)S(1)}, u32[]{:S(2)}, u32[]{:S(2)}) %collective-permute-start.14) | collective-permute-done | bytes 139296 | tf_op jit(solution)/shard_map/ppermute | solution.py:603
  57.8 1.6 %collective-permute-start.16 = (bf16[264,512]{1,0:T(8,128)(2,1)S(1)}, bf16[264,512]{1,0:T(8,128)(2,1)S(1)}, u32[]{:S(2)}, u32[]{:S(2)}) collective-permute-start(bf16[264,512]{1,0:T(8,128)(2,1)S(1)} %get-tuple-element.79), channel_id=1, source_target_pairs={{0,8},{4,12},{8,0},{12,4},{16,24},{20,28},{24,16},{28,20},{1,9},{5... | collective-permute-start | bytes 811016 | tf_op jit(solution)/shard_map/ppermute | solution.py:603
  59.4 3.5 %index_scores.1._ = f32[4,4,2048]{2,1,0:T(4,128)} custom-call(s32[16,32]{1,0:T(8,128)S(1)} %plan.1.table_ref, bf16[136,640]{1,0:T(8,128)(2,1)S(1)} %copy-done.3, bf16[136,640]{1,0:T(8,128)(2,1)S(1)} %collective-permute-done.2.first_ref.refs_1_, bf16[136,640]{1,0:T(8,128)(2,1)S(1)} %collective-permute-done.second_ref.refs_2_, ...), custom_call_target="tpu_custom_call" | custom-call | flops 3500000000 | bytes 10500000 | tf_op jit(solution)/shard_map/index_scores/pallas_call | solution.py:573
  63.8 2.4 %collective-permute-start.22 = (bf16[136,512]{1,0:T(8,128)(2,1)S(1)}, bf16[136,512]{1,0:T(8,128)(2,1)S(1)}, u32[]{:S(2)}, u32[]{:S(2)}) collective-permute-start(bf16[136,512]{1,0:T(8,128)(2,1)S(1)} %get-tuple-element.93), channel_id=1, source_target_pairs={{0,16},{4,20},{8,24},{12,28},{16,0},{20,4},{24,8},{28,12},{1,17},{... | collective-permute-start | bytes 417800 | tf_op jit(solution)/shard_map/ppermute | solution.py:603
  66.3 1.5 %collective-permute-done.16.from_z = bf16[264,512]{1,0:T(8,128)(2,1)S(1)} collective-permute-done((bf16[264,512]{1,0:T(8,128)(2,1)S(1)}, bf16[264,512]{1,0:T(8,128)(2,1)S(1)}, u32[]{:S(2)}, u32[]{:S(2)}) %collective-permute-start.16) | collective-permute-done | bytes 270368 | tf_op jit(solution)/shard_map/ppermute | solution.py:603
  68.2 2.8 %collective-permute-start.17 = (bf16[136,512]{1,0:T(8,128)(2,1)S(1)}, bf16[136,512]{1,0:T(8,128)(2,1)S(1)}, u32[]{:S(2)}, u32[]{:S(2)}) collective-permute-start(bf16[136,512]{1,0:T(8,128)(2,1)S(1)} %get-tuple-element.83), channel_id=1, source_target_pairs={{0,16},{4,20},{8,24},{12,28},{16,0},{20,4},{24,8},{28,12},{1,17},{... | collective-permute-start | bytes 417800 | tf_op jit(solution)/shard_map/ppermute | solution.py:603
  73.3 2.4 %collective-permute-done.17.other_ref = bf16[136,512]{1,0:T(8,128)(2,1)S(1)} collective-permute-done((bf16[136,512]{1,0:T(8,128)(2,1)S(1)}, bf16[136,512]{1,0:T(8,128)(2,1)S(1)}, u32[]{:S(2)}, u32[]{:S(2)}) %collective-permute-start.17) | collective-permute-done | bytes 139296 | tf_op jit(solution)/shard_map/ppermute | solution.py:603
  (56 shorter events, 17.3 us)
Async XLA Ops:
  0.6 20.6 %copy-start = (bf16[16,128,128]{2,1,0:T(8,128)(2,1)S(1)}, bf16[16,128,128]{2,1,0:T(8,128)(2,1)}, u32[]{:S(2)}) copy-start(bf16[16,128,128]{2,1,0:T(8,128)(2,1)} %own_ref) | copy-start | bytes 1572868
  2.8 14.0 %collective-permute-start.1 = (bf16[272,640]{1,0:T(8,128)(2,1)}, bf16[272,640]{1,0:T(8,128)(2,1)S(1)}, u32[]{:S(2)}, u32[]{:S(2)}) collective-permute-start(bf16[272,640]{1,0:T(8,128)(2,1)} %get-tuple-element.50), channel_id=1, source_target_pairs={{0,4},{4,0},{8,12},{12,8},{16,20},{20,16},{24,28},{28,24},{1,5},{5... | collective-permute-start | bytes 1044488 | tf_op jit(solution)/shard_map/ppermute | solution.py:600
  5.8 10.8 %collective-permute-start = (bf16[136,640]{1,0:T(8,128)(2,1)}, bf16[136,640]{1,0:T(8,128)(2,1)S(1)}, u32[]{:S(2)}, u32[]{:S(2)}) collective-permute-start(bf16[136,640]{1,0:T(8,128)(2,1)} %get-tuple-element.48.refs_0_), channel_id=1, source_target_pairs={{0,16},{4,20},{8,24},{12,28},{16,0},{20,4},{24,8},{28,12},{1,17},{... | collective-permute-start | bytes 522248 | tf_op jit(solution)/shard_map/ppermute | solution.py:603
  8.4 8.4 %collective-permute-start.2 = (bf16[136,640]{1,0:T(8,128)(2,1)}, bf16[136,640]{1,0:T(8,128)(2,1)S(1)}, u32[]{:S(2)}, u32[]{:S(2)}) collective-permute-start(bf16[136,640]{1,0:T(8,128)(2,1)} %get-tuple-element.48.refs_0_), channel_id=1, source_target_pairs={{0,8},{4,12},{8,0},{12,4},{16,24},{20,28},{24,16},{28,20},{1,9},{5... | collective-permute-start | bytes 522248 | tf_op jit(solution)/shard_map/ppermute | solution.py:603
  16.9 10.3 %collective-permute-start.4 = (bf16[272,640]{1,0:T(8,128)(2,1)S(1)}, bf16[272,640]{1,0:T(8,128)(2,1)S(1)}, u32[]{:S(2)}, u32[]{:S(2)}) collective-permute-start(bf16[272,640]{1,0:T(8,128)(2,1)S(1)} %pair_up.2), channel_id=1, source_target_pairs={{0,4},{4,0},{8,12},{12,8},{16,20},{20,16},{24,28},{28,24},{1,5},{5... | collective-permute-start | bytes 1044488 | tf_op jit(solution)/shard_map/ppermute | solution.py:600
  17.4 9.7 %collective-permute-start.5 = (bf16[136,640]{1,0:T(8,128)(2,1)}, bf16[136,640]{1,0:T(8,128)(2,1)S(1)}, u32[]{:S(2)}, u32[]{:S(2)}) collective-permute-start(bf16[136,640]{1,0:T(8,128)(2,1)} %get-tuple-element.57.refs_0_.refs_8_), channel_id=1, source_target_pairs={{0,16},{4,20},{8,24},{12,28},{16,0},{20,4},{24,8},{28,12},{1,17},{... | collective-permute-start | bytes 522248 | tf_op jit(solution)/shard_map/ppermute | solution.py:603
  18.8 8.3 %collective-permute-start.3 = (bf16[136,640]{1,0:T(8,128)(2,1)S(1)}, bf16[136,640]{1,0:T(8,128)(2,1)S(1)}, u32[]{:S(2)}, u32[]{:S(2)}) collective-permute-start(bf16[136,640]{1,0:T(8,128)(2,1)S(1)} %collective-permute-done.second_ref.refs_2_), channel_id=1, source_target_pairs={{0,8},{4,12},{8,0},{12,4},{16,24},{20,28},{24,16},{28,20},{1,9},{5... | collective-permute-start | bytes 522248 | tf_op jit(solution)/shard_map/ppermute | solution.py:603
  21.2 14.5 %collective-permute-start.18 = (bf16[16,128,128]{2,1,0:T(8,128)(2,1)S(1)}, bf16[16,128,128]{2,1,0:T(8,128)(2,1)S(1)}, u32[]{:S(2)}, u32[]{:S(2)}) collective-permute-start(bf16[16,128,128]{2,1,0:T(8,128)(2,1)S(1)} %copy-done), channel_id=1, source_target_pairs={{0,1},{1,0},{2,3},{3,2},{4,5},{5,4},{6,7},{7,6},{8,9},{9,8},{10,11... | collective-permute-start | bytes 1572872 | tf_op jit(solution)/shard_map/ppermute | solution.py:606
  27.1 10.3 %collective-permute-start.8 = (bf16[136,640]{1,0:T(8,128)(2,1)S(1)}, bf16[136,640]{1,0:T(8,128)(2,1)S(1)}, u32[]{:S(2)}, u32[]{:S(2)}) collective-permute-start(bf16[136,640]{1,0:T(8,128)(2,1)S(1)} %collective-permute-done.5.second_ref.refs_2_.refs_10_), channel_id=1, source_target_pairs={{0,8},{4,12},{8,0},{12,4},{16,24},{20,28},{24,16},{28,20},{1,9},{5... | collective-permute-start | bytes 522248 | tf_op jit(solution)/shard_map/ppermute | solution.py:603
  28.2 9.3 %collective-permute-start.7 = (bf16[136,640]{1,0:T(8,128)(2,1)S(1)}, bf16[136,640]{1,0:T(8,128)(2,1)S(1)}, u32[]{:S(2)}, u32[]{:S(2)}) collective-permute-start(bf16[136,640]{1,0:T(8,128)(2,1)S(1)} %copy-done.4), channel_id=1, source_target_pairs={{0,8},{4,12},{8,0},{12,4},{16,24},{20,28},{24,16},{28,20},{1,9},{5... | collective-permute-start | bytes 522248 | tf_op jit(solution)/shard_map/ppermute | solution.py:603
  29.2 9.1 %collective-permute-start.6 = (bf16[272,640]{1,0:T(8,128)(2,1)S(1)}, bf16[272,640]{1,0:T(8,128)(2,1)S(1)}, u32[]{:S(2)}, u32[]{:S(2)}) collective-permute-start(bf16[272,640]{1,0:T(8,128)(2,1)S(1)} %pair_up.3), channel_id=1, source_target_pairs={{0,4},{4,0},{8,12},{12,8},{16,20},{20,16},{24,28},{28,24},{1,5},{5... | collective-permute-start | bytes 1044488 | tf_op jit(solution)/shard_map/ppermute | solution.py:600
  35.8 35.2 %collective-permute-start.19 = (bf16[2,16,128,128]{3,2,1,0:T(8,128)(2,1)S(1)}, bf16[2,16,128,128]{3,2,1,0:T(8,128)(2,1)S(1)}, u32[]{:S(2)}, u32[]{:S(2)}) collective-permute-start(bf16[2,16,128,128]{3,2,1,0:T(8,128)(2,1)S(1)} %pair_cores.1.here_ref), channel_id=1, source_target_pairs={{0,2},{1,3},{2,0},{3,1},{4,6},{5,7},{6,4},{7,5},{8,10},{9,11},{10,... | collective-permute-start | bytes 3145736 | tf_op jit(solution)/shard_map/ppermute | solution.py:606
  38.3 7.6 %collective-permute-start.10 = (bf16[136,640]{1,0:T(8,128)(2,1)S(1)}, bf16[136,640]{1,0:T(8,128)(2,1)S(1)}, u32[]{:S(2)}, u32[]{:S(2)}) collective-permute-start(bf16[136,640]{1,0:T(8,128)(2,1)S(1)} %second_of.1.refs_6_.refs_14_), channel_id=1, source_target_pairs={{0,8},{4,12},{8,0},{12,4},{16,24},{20,28},{24,16},{28,20},{1,9},{5... | collective-permute-start | bytes 522248 | tf_op jit(solution)/shard_map/ppermute | solution.py:603
  38.8 7.1 %collective-permute-start.9 = (bf16[136,640]{1,0:T(8,128)(2,1)S(1)}, bf16[136,640]{1,0:T(8,128)(2,1)S(1)}, u32[]{:S(2)}, u32[]{:S(2)}) collective-permute-start(bf16[136,640]{1,0:T(8,128)(2,1)S(1)} %collective-permute-done.7.refs_1_.refs_9_), channel_id=1, source_target_pairs={{0,4},{4,0},{8,12},{12,8},{16,20},{20,16},{24,28},{28,24},{1,5},{5... | collective-permute-start | bytes 522248 | tf_op jit(solution)/shard_map/ppermute | solution.py:600
  43.7 8.6 %collective-permute-start.12 = (bf16[136,512]{1,0:T(8,128)(2,1)S(1)}, bf16[136,512]{1,0:T(8,128)(2,1)S(1)}, u32[]{:S(2)}, u32[]{:S(2)}) collective-permute-start(bf16[136,512]{1,0:T(8,128)(2,1)S(1)} %get-tuple-element.71), channel_id=1, source_target_pairs={{0,4},{4,0},{8,12},{12,8},{16,20},{20,16},{24,28},{28,24},{1,5},{5... | collective-permute-start | bytes 417800 | tf_op jit(solution)/shard_map/ppermute | solution.py:600
  44.3 8.0 %collective-permute-start.13 = (bf16[136,512]{1,0:T(8,128)(2,1)S(1)}, bf16[136,512]{1,0:T(8,128)(2,1)S(1)}, u32[]{:S(2)}, u32[]{:S(2)}) collective-permute-start(bf16[136,512]{1,0:T(8,128)(2,1)S(1)} %get-tuple-element.74), channel_id=1, source_target_pairs={{0,8},{4,12},{8,0},{12,4},{16,24},{20,28},{24,16},{28,20},{1,9},{5... | collective-permute-start | bytes 417800 | tf_op jit(solution)/shard_map/ppermute | solution.py:603
  49.6 5.8 %collective-permute-start.11 = (bf16[136,512]{1,0:T(8,128)(2,1)S(1)}, bf16[136,512]{1,0:T(8,128)(2,1)S(1)}, u32[]{:S(2)}, u32[]{:S(2)}) collective-permute-start(bf16[136,512]{1,0:T(8,128)(2,1)S(1)} %get-tuple-element.68), channel_id=1, source_target_pairs={{0,4},{4,0},{8,12},{12,8},{16,20},{20,16},{24,28},{28,24},{1,5},{5... | collective-permute-start | bytes 417800 | tf_op jit(solution)/shard_map/ppermute | solution.py:600
  51.1 6.0 %collective-permute-start.14 = (bf16[136,512]{1,0:T(8,128)(2,1)S(1)}, bf16[136,512]{1,0:T(8,128)(2,1)S(1)}, u32[]{:S(2)}, u32[]{:S(2)}) collective-permute-start(bf16[136,512]{1,0:T(8,128)(2,1)S(1)} %get-tuple-element.77), channel_id=1, source_target_pairs={{0,8},{4,12},{8,0},{12,4},{16,24},{20,28},{24,16},{28,20},{1,9},{5... | collective-permute-start | bytes 417800 | tf_op jit(solution)/shard_map/ppermute | solution.py:603
  52.7 10.3 %collective-permute-start.20 = (bf16[264,512]{1,0:T(8,128)(2,1)S(1)}, bf16[264,512]{1,0:T(8,128)(2,1)S(1)}, u32[]{:S(2)}, u32[]{:S(2)}) collective-permute-start(bf16[264,512]{1,0:T(8,128)(2,1)S(1)} %get-tuple-element.89), channel_id=1, source_target_pairs={{0,4},{4,0},{8,12},{12,8},{16,20},{20,16},{24,28},{28,24},{1,5},{5... | collective-permute-start | bytes 811016 | tf_op jit(solution)/shard_map/ppermute | solution.py:600
  52.8 10.6 %collective-permute-start.21 = (bf16[264,512]{1,0:T(8,128)(2,1)S(1)}, bf16[264,512]{1,0:T(8,128)(2,1)S(1)}, u32[]{:S(2)}, u32[]{:S(2)}) collective-permute-start(bf16[264,512]{1,0:T(8,128)(2,1)S(1)} %get-tuple-element.90), channel_id=1, source_target_pairs={{0,8},{4,12},{8,0},{12,4},{16,24},{20,28},{24,16},{28,20},{1,9},{5... | collective-permute-start | bytes 811016 | tf_op jit(solution)/shard_map/ppermute | solution.py:603
  57.5 8.8 %collective-permute-start.15 = (bf16[264,512]{1,0:T(8,128)(2,1)S(1)}, bf16[264,512]{1,0:T(8,128)(2,1)S(1)}, u32[]{:S(2)}, u32[]{:S(2)}) collective-permute-start(bf16[264,512]{1,0:T(8,128)(2,1)S(1)} %get-tuple-element.78), channel_id=1, source_target_pairs={{0,4},{4,0},{8,12},{12,8},{16,20},{20,16},{24,28},{28,24},{1,5},{5... | collective-permute-start | bytes 811016 | tf_op jit(solution)/shard_map/ppermute | solution.py:600
  57.8 10.0 %collective-permute-start.16 = (bf16[264,512]{1,0:T(8,128)(2,1)S(1)}, bf16[264,512]{1,0:T(8,128)(2,1)S(1)}, u32[]{:S(2)}, u32[]{:S(2)}) collective-permute-start(bf16[264,512]{1,0:T(8,128)(2,1)S(1)} %get-tuple-element.79), channel_id=1, source_target_pairs={{0,8},{4,12},{8,0},{12,4},{16,24},{20,28},{24,16},{28,20},{1,9},{5... | collective-permute-start | bytes 811016 | tf_op jit(solution)/shard_map/ppermute | solution.py:603
  63.8 8.2 %collective-permute-start.22 = (bf16[136,512]{1,0:T(8,128)(2,1)S(1)}, bf16[136,512]{1,0:T(8,128)(2,1)S(1)}, u32[]{:S(2)}, u32[]{:S(2)}) collective-permute-start(bf16[136,512]{1,0:T(8,128)(2,1)S(1)} %get-tuple-element.93), channel_id=1, source_target_pairs={{0,16},{4,20},{8,24},{12,28},{16,0},{20,4},{24,8},{28,12},{1,17},{... | collective-permute-start | bytes 417800 | tf_op jit(solution)/shard_map/ppermute | solution.py:603
  68.2 7.5 %collective-permute-start.17 = (bf16[136,512]{1,0:T(8,128)(2,1)S(1)}, bf16[136,512]{1,0:T(8,128)(2,1)S(1)}, u32[]{:S(2)}, u32[]{:S(2)}) collective-permute-start(bf16[136,512]{1,0:T(8,128)(2,1)S(1)} %get-tuple-element.83), channel_id=1, source_target_pairs={{0,16},{4,20},{8,24},{12,28},{16,0},{20,4},{24,8},{28,12},{1,17},{... | collective-permute-start | bytes 417800 | tf_op jit(solution)/shard_map/ppermute | solution.py:603
  (7 other events, 36.7 us)

commit v5 on v4

--- a/solution.py
+++ b/solution.py
@@ -12,9 +12,10 @@
 BLOCK = 64
 VMEM_LIMIT = 16 * 1024 * 1024
 PACK_LIMIT = 63_000_000
-ATTEND_LIMIT = 20 * 1024 * 1024
+ATTEND_LIMIT = 30_000_000
 TABLE = 32
-GATHER_LIMIT = (47_000_000, 38_000_000)
+GATHER_LIMIT = (46_000_000, 38_000_000)
+SHORT = 4
 
 CHUNKS = 2
 PAIRS = 8
@@ -201,43 +202,40 @@
     return jnp.concatenate([turned, jnp.zeros((LANES - PAIRS, LANES), jnp.float32)], axis=0).T
 
 
-def gather_kernel(chunk, table_ref, latent_hbm, out_ref, latent_ref, sems):
+def gather_kernel(requests, table_ref, latent_hbm, out_ref, latent_ref, sems):
     copies = []
-    for local in range(2):
+    for local, request in enumerate(requests):
         for part in range(4):
             rows = pl.ds(part * 144, 144)
             copies.append(
                 pltpu.make_async_copy(
-                    latent_hbm.at[2 * chunk + local, rows],
+                    latent_hbm.at[request, rows],
                     latent_ref.at[local, rows],
                     sems.at[local * 4 + part],
                 )
             )
     for copy in copies:
         copy.start()
-    in_even = lax.broadcasted_iota(jnp.int32, (576, LANES), 1) < BLOCK
-    for local in range(2):
-        request = 2 * chunk + local
-        for copy in copies[local * 4 : local * 4 + 4]:
-            copy.wait()
-
-        def tile(row, place, local=local):
+    in_even = lax.broadcasted_iota(jnp.int32, (144, LANES), 1) < BLOCK
+    for index, copy in enumerate(copies):
+        copy.wait()
+        local, part = divmod(index, 4)
+        request = requests[local]
+        rows = slice(part * 144, (part + 1) * 144)
+
+        def tile(row, place, local=local, rows=rows):
             start = pl.multiple_of(jnp.maximum(table_ref[row, place], 0) * LANES, LANES)
-            return latent_ref[local, :, pl.ds(start, LANES)]
-
-        def fill(places, request=request, local=local, tile=tile):
+            return latent_ref[local, rows, pl.ds(start, LANES)]
+
+        def fill(places, local=local, request=request, rows=rows, tile=tile):
             for step in range(4):
                 row = step * 4 + request
                 for place in places:
-                    out_ref[local * 4 + step, :, place * LANES : (place + 1) * LANES] = jnp.where(
+                    out_ref[local * 4 + step, rows, place * LANES : (place + 1) * LANES] = jnp.where(
                         in_even, tile(row, place), tile(row, SLOTS + place)
                     )
 
-        fill(range(4))
-
-        @pl.when(most_of(table_ref, request) > 4)
-        def _(fill=fill):
-            fill(range(4, SLOTS))
+        fill(range(SHORT))
 
 
 def most_of(table_ref, request):
@@ -247,103 +245,125 @@
     return most
 
 
-def gather(chunk, table, latents_t):
+def gather(requests, limit, table, latents_t):
     bf16 = jnp.bfloat16
-    return call(
-        functools.partial(gather_kernel, chunk),
-        limit=GATHER_LIMIT[chunk],
+    count = len(requests)
+    return call(
+        functools.partial(gather_kernel, requests),
+        limit=limit,
         in_specs=[pl.BlockSpec(memory_space=pltpu.SMEM), pl.BlockSpec(memory_space=pltpu.HBM)],
-        out_shape=jax.ShapeDtypeStruct((PAIRS, 576, SLOTS * LANES), bf16),
-        scratch_shapes=[pltpu.VMEM((2, 576, 2048), bf16), pltpu.SemaphoreType.DMA((8,))],
+        out_shape=jax.ShapeDtypeStruct((4 * count, 576, SHORT * LANES), bf16),
+        scratch_shapes=[
+            pltpu.VMEM((count, 576, 2048), bf16),
+            pltpu.SemaphoreType.DMA((4 * count,)),
+        ],
         name="gather_blocks",
-        us=5,
+        us=2.6 * count,
     )(table, latents_t)
 
 
 def attend_kernel(chunk, offsets, table_ref, *refs):
     q_refs = refs[:8]
-    block_ref = refs[8]
-    near, far, cross, send_x, send_z, stats_ref, score_ref, weight_ref = refs[9:]
+    block_ref, latent_hbm = refs[8:10]
+    near, far, cross, send_x, send_z, stats_ref = refs[10:16]
+    score_ref, weight_ref, latent_ref, wide_ref, sem = refs[16:]
     lane = lax.broadcasted_iota(jnp.int32, (LANES, LANES), 1)
     position = lax.broadcasted_iota(jnp.int32, (1, LANES), 1)
     stats_ref[...] = jnp.zeros((LANES, LANES), jnp.float32)
 
-    def work(local, request, tiles):
-        width = tiles * LANES
+    def query_of(pair):
+        return jnp.concatenate(
+            [r[at + pair * HEADS : at + (pair + 1) * HEADS, :576] for r, at in zip(q_refs, offsets)],
+            axis=0,
+        )
+
+    def scores_of(pair, row, blocks, tiles):
+        bias = []
+        for place in range(tiles):
+            at = jnp.where(position < BLOCK, table_ref[row, place], table_ref[row, SLOTS + place])
+            usable = (at >= 0) & (at * LANES + position <= table_ref[row, 17])
+            bias.append(jnp.where(usable, 0.0, -1e30))
+        scores = jnp.dot(query_of(pair), blocks, preferred_element_type=jnp.float32)
+        return scores * (QK_DIM**-0.5) + jnp.concatenate(bias, axis=1)
+
+    def weights_of(pair, scores):
+        peak = jnp.maximum(jnp.max(scores, axis=1, keepdims=True), -1e29)
+        weights = jnp.exp(scores - peak)
+        total = jnp.maximum(jnp.sum(weights, axis=1, keepdims=True), 1e-30)
+        stats_ref[...] = jnp.where(lane == pair, peak + jnp.log(total), stats_ref[...])
+        return weights.astype(jnp.bfloat16), 1.0 / total
+
+    def mix(pair, weights, blocks, scale):
+        mixed = lax.dot_general(
+            weights, blocks, (((1,), (1,)), ((), ())), preferred_element_type=jnp.float32
+        )
+        mixed = (mixed * scale).astype(jnp.bfloat16)
+        row = pair * HEADS
+        for out, places in (
+            (near, (0, 2)),
+            (far, (1, 3)),
+            (cross, (4, 6)),
+            (send_x, (5,)),
+            (send_z, (7,)),
+        ):
+            for half, place in enumerate(places):
+                at = half * ROWS + row
+                out[at : at + HEADS, :] = mixed[place * HEADS : (place + 1) * HEADS]
+
+    def short(local, request):
         for step in range(4):
-            row = step * 4 + request
             pair = local * 4 + step
-            query = jnp.concatenate(
-                [
-                    r[at + pair * HEADS : at + (pair + 1) * HEADS, :576]
-                    for r, at in zip(q_refs, offsets)
-                ],
-                axis=0,
-            )
-            bias = []
-            for place in range(tiles):
-                at = jnp.where(
-                    position < BLOCK, table_ref[row, place], table_ref[row, SLOTS + place]
-                )
-                usable = (at >= 0) & (at * LANES + position <= table_ref[row, 17])
-                bias.append(jnp.where(usable, 0.0, -1e30))
-            scores = jnp.dot(
-                query, block_ref[pair, :, :width], preferred_element_type=jnp.float32
-            )
-            score_ref[step, :, :width] = scores * (QK_DIM**-0.5) + jnp.concatenate(bias, axis=1)
+            score_ref[step] = scores_of(pair, step * 4 + request, block_ref[pair], SHORT)
         scales = []
         for step in range(4):
-            scores = score_ref[step, :, :width]
-            peak = jnp.maximum(jnp.max(scores, axis=1, keepdims=True), -1e29)
-            weights = jnp.exp(scores - peak)
-            total = jnp.maximum(jnp.sum(weights, axis=1, keepdims=True), 1e-30)
-            weight_ref[step, :, :width] = weights.astype(jnp.bfloat16)
-            scales.append(1.0 / total)
-            stats_ref[...] = jnp.where(
-                lane == local * 4 + step, peak + jnp.log(total), stats_ref[...]
-            )
+            weight_ref[step], scale = weights_of(local * 4 + step, score_ref[step])
+            scales.append(scale)
         for step in range(4):
-            mixed = lax.dot_general(
-                weight_ref[step, :, :width],
-                block_ref[local * 4 + step, :KV, :width],
-                (((1,), (1,)), ((), ())),
-                preferred_element_type=jnp.float32,
-            )
-            mixed = (mixed * scales[step]).astype(jnp.bfloat16)
-            row = (local * 4 + step) * HEADS
-            for out, places in (
-                (near, (0, 2)),
-                (far, (1, 3)),
-                (cross, (4, 6)),
-                (send_x, (5,)),
-                (send_z, (7,)),
-            ):
-                for half, place in enumerate(places):
-                    at = half * ROWS + row
-                    out[at : at + HEADS, :] = mixed[place * HEADS : (place + 1) * HEADS]
+            pair = local * 4 + step
+            mix(pair, weight_ref[step], block_ref[pair, :KV], scales[step])
+
+    def long(local, request):
+        copy = pltpu.make_async_copy(latent_hbm.at[request], latent_ref, sem.at[0])
+        copy.start()
+        copy.wait()
+        in_even = lax.broadcasted_iota(jnp.int32, (576, LANES), 1) < BLOCK
+        for step in range(4):
+            pair, row = local * 4 + step, step * 4 + request
+
+            def tile(place, row=row):
+                start = pl.multiple_of(jnp.maximum(table_ref[row, place], 0) * LANES, LANES)
+                return latent_ref[:, pl.ds(start, LANES)]
+
+            for place in range(SLOTS):
+                wide_ref[:, place * LANES : (place + 1) * LANES] = jnp.where(
+                    in_even, tile(place), tile(SLOTS + place)
+                )
+            weights, scale = weights_of(pair, scores_of(pair, row, wide_ref[...], SLOTS))
+            mix(pair, weights, wide_ref[:KV], scale)
 
     for local in range(2):
         request = 2 * chunk + local
         most = most_of(table_ref, request)
 
-        @pl.when(most <= 4)
+        @pl.when(most <= SHORT)
         def _(local=local, request=request):
-            work(local, request, 4)
-
-        @pl.when(most > 4)
+            short(local, request)
+
+        @pl.when(most > SHORT)
         def _(local=local, request=request):
-            work(local, request, 8)
+            long(local, request)
 
     store_stats(send_x, ROWS, stats_ref[...])
     store_stats(send_z, ROWS, stats_ref[...])
 
 
-def attend(chunk, table, gathered_queries, blocks):
+def attend(chunk, table, gathered_queries, blocks, latents_t):
     bf16 = jnp.bfloat16
     return call(
         functools.partial(attend_kernel, chunk, tuple(at for _, at in gathered_queries)),
         limit=ATTEND_LIMIT,
-        in_specs=[pl.BlockSpec(memory_space=pltpu.SMEM)] + [pl.BlockSpec()] * 9,
+        in_specs=[pl.BlockSpec(memory_space=pltpu.SMEM)] + [pl.BlockSpec()] * 9
+        + [pl.BlockSpec(memory_space=pltpu.HBM)],
         out_shape=[
             jax.ShapeDtypeStruct((2 * ROWS, KV), bf16),
             jax.ShapeDtypeStruct((2 * ROWS, KV), bf16),
@@ -353,12 +373,15 @@
             jax.ShapeDtypeStruct((LANES, LANES), jnp.float32),
         ],
         scratch_shapes=[
-            pltpu.VMEM((4, LANES, SLOTS * LANES), jnp.float32),
-            pltpu.VMEM((4, LANES, SLOTS * LANES), bf16),
+            pltpu.VMEM((4, LANES, SHORT * LANES), jnp.float32),
+            pltpu.VMEM((4, LANES, SHORT * LANES), bf16),
+            pltpu.VMEM((576, 2048), bf16),
+            pltpu.VMEM((576, SLOTS * LANES), bf16),
+            pltpu.SemaphoreType.DMA((1,)),
         ],
         name="attend",
         us=3.6,
-    )(table, *(array for array, _ in gathered_queries), blocks)
+    )(table, *(array for array, _ in gathered_queries), blocks, latents_t)
 
 
 def group(number):
@@ -612,23 +635,23 @@
     x0 = across_x(both)
     z2c0, z1c0 = across_z(own0, 2), across_z(own0, 1)
 
-    round1 = (x0, z2c0, z1c0, table)
+    blocks_a = gather((0, 1), GATHER_LIMIT[0], table, latents_t)
+    round1 = (x0, z2c0, z1c0, blocks_a)
     x12 = across_x(pair_up(after(z1c0, *round1), z2c0))
     z3c0 = across_z(after(z2c0, *round1), 1)
     z2c1 = across_z(after(own1, *round1), 2)
-    blocks0 = gather(0, after(table, *round1), latents_t)
+    blocks_b = gather((2, 3), GATHER_LIMIT[1], after(table, *round1), latents_t)
 
     up_core = across_req(after(value_up_weight, *round1), 1)
 
-    round2 = (x12, z3c0, z2c1, blocks0)
+    round2 = (x12, z3c0, z2c1, blocks_b)
     x32 = across_x(pair_up(after(z3c0, *round2), z2c1))
     z1c1 = across_z(after(own1, *round2), 1)
     z3c1 = across_z(after(z2c1, *round2), 1)
-    blocks1 = gather(1, after(table, *round2), latents_t)
     up_here = pair_cores(after(value_up_weight, *round2), up_core)
     up_there = across_req(up_here, 2)
 
-    round3 = (x32, z1c1, z3c1, blocks1)
+    round3 = (x32, z1c1, z3c1)
     xz1c1 = across_x(after(z1c1, *round3))
     xz2c1 = second_of(after(x32, *round3))
     xz3c1 = across_z(xz2c1, 1)
@@ -637,9 +660,9 @@
         [(own1, 0), (z1c1, 0), (z2c1, 0), (z3c1, 0), (x0, SENT), (xz1c1, 0), (xz2c1, 0), (xz3c1, 0)],
     ]
 
-    near0, far0, cross0, x5, z7, stats0 = attend(0, after(table, xz2c1), gathered[0], blocks0)
+    near0, far0, cross0, x5, z7, stats0 = attend(0, after(table, xz2c1), gathered[0], blocks_a, latents_t)
     x5, z7 = across_x(x5), across_z(z7, 1)
-    near1, far1, cross1, x5c1, z7c1, stats1 = attend(1, after(table, stats0), gathered[1], blocks1)
+    near1, far1, cross1, x5c1, z7c1, stats1 = attend(1, after(table, stats0), gathered[1], blocks_b, latents_t)
     x5c1, z7c1 = across_x(x5c1), across_z(z7c1, 1)
 
     to_z, to_x, stats0 = join_cross(far0, cross0, after(x5, stats1), z7, stats0)

time: 77.2 us -> 75.6 us (0.979)
  waiting for transfers between devices: 13.4 us -> 15.6 us
  local copies, waits for them, and re-layouts: 2.95 us -> 0.95 us
  starting transfers between devices: 32.2 us -> 30.8 us
    unnamed x16 -> x22, local copies, waits for them, and re-layouts: 2.95 us -> 0.95 us
    ppermute x13, waiting for transfers between devices: 11.2 us -> 12.9 us  [across_z(): return lax.ppermute(value, 'ctx', [(i, i ^ 2 * distance) for i in range(8)])]
    ppermute x13, starting transfers between devices: 21.5 us -> 20 us  [across_z(): return lax.ppermute(value, 'ctx', [(i, i ^ 2 * distance) for i in range(8)])]
  transfers between devices with their start and end apart: 23 -> 23, of which waited for: 9 -> 10; matrix products, arithmetic and copies ran while one was open for 0% -> 0% of each run, Pallas kernels for 31% -> 32%
where the time goes in v5:
time: 75.6 us; the launch traced here: 75.5 us
  starting transfers between devices  30.8 us (41%)
  Pallas kernels  27.3 us (36%)
  waiting for transfers between devices  15.6 us (21%)
  local copies, waits for them, and re-layouts  0.95 us (1%)
  between operations  0.87 us (1%)
    ppermute x13, starting transfers between devices, across_z(): return lax.ppermute(value, 'ctx', [(i, i ^ 2 * distance) for i in range(8)])  20 us
    ppermute x13, waiting for transfers between devices, across_z(): return lax.ppermute(value, 'ctx', [(i, i ^ 2 * distance) for i in range(8)])  12.9 us
    pallas_call x2, Pallas kernels, gather(): call(functools.partial(gather_kernel, requests), limit=limit, in_specs=[p...  9.2 us
    ppermute x8, starting transfers between devices, across_x(): return lax.ppermute(value, 'ctx', [(i, i ^ 1) for i in range(8)])  9.18 us
    pallas_call x2, Pallas kernels, attend(): call(functools.partial(attend_kernel, chunk, tuple((at for _, at in gathe...  7.37 us
    pallas_call x1, Pallas kernels, index_rows(): call(functools.partial(index_kernel, tuple((at for _, at in members))), g...  3.52 us
    ppermute x8, waiting for transfers between devices, across_x(): return lax.ppermute(value, 'ctx', [(i, i ^ 1) for i in range(8)])  2.62 us
    pallas_call x2, Pallas kernels, finish(): call(finish_kernel, grid=(1,), in_specs=specs, out_specs=pl.BlockSpec((4,...  2.43 us
  transfers between devices with their start and end apart: 23, of which 10 were waited for; matrix products, arithmetic and copies ran while one was open for 0% of the time, Pallas kernels for 32%

profile of v5, /device:TPU:0, one launch (start us, length us, event | category | flops | bytes accessed | tf_op | source)
XLA Modules:
  0.0 75.5 jit_solution(17566584065463771555)
XLA Ops:
  0.7 2.1 %pack.1 = (bf16[136,640]{1,0:T(8,128)(2,1)}, bf16[136,640]{1,0:T(8,128)(2,1)}, bf16[272,640]{1,0:T(8,128)(2,1)}) custom-call(bf16[4,4,16,576]{3,2,1,0:T(8,128)(2,1)} %q_hbm.1, bf16[4,4,8,128]{3,2,1,0:T(8,128)(2,1)} %iq_hbm.1, bf16[4,4,8]{2,1,0:T(4,128)(2,1)} %iw_hbm.1), custom_call_target="tpu_custom_call" | custom-call | flops 2000000000 | bytes 6000000 | tf_op jit(solution)/shard_map/pack/pallas_call | solution.py:94
  2.8 3.1 %collective-permute-start.2 = (bf16[136,640]{1,0:T(8,128)(2,1)}, bf16[136,640]{1,0:T(8,128)(2,1)S(1)}, u32[]{:S(2)}, u32[]{:S(2)}) collective-permute-start(bf16[136,640]{1,0:T(8,128)(2,1)} %get-tuple-element.47.refs_0_), channel_id=1, source_target_pairs={{0,8},{4,12},{8,0},{12,4},{16,24},{20,28},{24,16},{28,20},{1,9},{5... | collective-permute-start | bytes 522248 | tf_op jit(solution)/shard_map/ppermute | solution.py:626
  5.9 2.6 %collective-permute-start = (bf16[136,640]{1,0:T(8,128)(2,1)}, bf16[136,640]{1,0:T(8,128)(2,1)S(1)}, u32[]{:S(2)}, u32[]{:S(2)}) collective-permute-start(bf16[136,640]{1,0:T(8,128)(2,1)} %get-tuple-element.47.refs_0_), channel_id=1, source_target_pairs={{0,16},{4,20},{8,24},{12,28},{16,0},{20,4},{24,8},{28,12},{1,17},{... | collective-permute-start | bytes 522248 | tf_op jit(solution)/shard_map/ppermute | solution.py:626
  8.5 1.5 %collective-permute-start.1 = (bf16[272,640]{1,0:T(8,128)(2,1)}, bf16[272,640]{1,0:T(8,128)(2,1)S(1)}, u32[]{:S(2)}, u32[]{:S(2)}) collective-permute-start(bf16[272,640]{1,0:T(8,128)(2,1)} %get-tuple-element.49), channel_id=1, source_target_pairs={{0,4},{4,0},{8,12},{12,8},{16,20},{20,16},{24,28},{28,24},{1,5},{5... | collective-permute-start | bytes 1044488 | tf_op jit(solution)/shard_map/ppermute | solution.py:623
  10.9 5.0 %gather_blocks.2.refs_8_ = bf16[8,576,512]{2,1,0:T(8,128)(2,1)S(1)} custom-call(s32[16,32]{1,0:T(8,128)S(1)} %plan.1.table_ref, bf16[4,576,2048]{2,1,0:T(8,128)(2,1)} %bitcast.1), custom_call_target="tpu_custom_call" | custom-call | flops 5200000000 | bytes 15600000 | tf_op jit(solution)/shard_map/gather_blocks/pallas_call | solution.py:251
  16.7 1.3 %collective-permute-done.1.refs_4_.refs_12_ = bf16[272,640]{1,0:T(8,128)(2,1)S(1)} collective-permute-done((bf16[272,640]{1,0:T(8,128)(2,1)}, bf16[272,640]{1,0:T(8,128)(2,1)S(1)}, u32[]{:S(2)}, u32[]{:S(2)}) %collective-permute-start.1) | collective-permute-done | bytes 348192 | tf_op jit(solution)/shard_map/ppermute | solution.py:623
  19.7 1.6 %collective-permute-start.4 = (bf16[272,640]{1,0:T(8,128)(2,1)S(1)}, bf16[272,640]{1,0:T(8,128)(2,1)S(1)}, u32[]{:S(2)}, u32[]{:S(2)}) collective-permute-start(bf16[272,640]{1,0:T(8,128)(2,1)S(1)} %pair_up.2), channel_id=1, source_target_pairs={{0,4},{4,0},{8,12},{12,8},{16,20},{20,16},{24,28},{28,24},{1,5},{5... | collective-permute-start | bytes 1044488 | tf_op jit(solution)/shard_map/ppermute | solution.py:623
  21.3 4.2 %gather_blocks.3.refs_8_ = bf16[8,576,512]{2,1,0:T(8,128)(2,1)S(1)} custom-call(s32[16,32]{1,0:T(8,128)S(1)} %plan.1.table_ref, bf16[4,576,2048]{2,1,0:T(8,128)(2,1)S(1)} %bitcast.4), custom_call_target="tpu_custom_call" | custom-call | flops 5200000000 | bytes 15600000 | tf_op jit(solution)/shard_map/gather_blocks/pallas_call | solution.py:251
  25.6 2.0 %collective-permute-done.5.second_ref.refs_2_.refs_10_ = bf16[136,640]{1,0:T(8,128)(2,1)S(1)} collective-permute-done((bf16[136,640]{1,0:T(8,128)(2,1)S(1)}, bf16[136,640]{1,0:T(8,128)(2,1)S(1)}, u32[]{:S(2)}, u32[]{:S(2)}) %collective-permute-start.5) | collective-permute-done | bytes 174112 | tf_op jit(solution)/shard_map/ppermute | solution.py:626
  27.6 1.6 %collective-permute-start.6 = (bf16[272,640]{1,0:T(8,128)(2,1)S(1)}, bf16[272,640]{1,0:T(8,128)(2,1)S(1)}, u32[]{:S(2)}, u32[]{:S(2)}) collective-permute-start(bf16[272,640]{1,0:T(8,128)(2,1)S(1)} %pair_up.3), channel_id=1, source_target_pairs={{0,4},{4,0},{8,12},{12,8},{16,20},{20,16},{24,28},{28,24},{1,5},{5... | collective-permute-start | bytes 1044488 | tf_op jit(solution)/shard_map/ppermute | solution.py:623
  31.3 1.6 %collective-permute-start.19 = (bf16[2,16,128,128]{3,2,1,0:T(8,128)(2,1)S(1)}, bf16[2,16,128,128]{3,2,1,0:T(8,128)(2,1)S(1)}, u32[]{:S(2)}, u32[]{:S(2)}) collective-permute-start(bf16[2,16,128,128]{3,2,1,0:T(8,128)(2,1)S(1)} %pair_cores.1.here_ref), channel_id=1, source_target_pairs={{0,2},{1,3},{2,0},{3,1},{4,6},{5,7},{6,4},{7,5},{8,10},{9,11},{10,... | collective-permute-start | bytes 3145736 | tf_op jit(solution)/shard_map/ppermute | solution.py:629
  32.8 1.8 %collective-permute-done.7.refs_1_.refs_9_ = bf16[136,640]{1,0:T(8,128)(2,1)S(1)} collective-permute-done((bf16[136,640]{1,0:T(8,128)(2,1)S(1)}, bf16[136,640]{1,0:T(8,128)(2,1)S(1)}, u32[]{:S(2)}, u32[]{:S(2)}) %collective-permute-start.7) | collective-permute-done | bytes 174112 | tf_op jit(solution)/shard_map/ppermute | solution.py:626
  34.6 1.9 %collective-permute-done.8.refs_3_.refs_11_ = bf16[136,640]{1,0:T(8,128)(2,1)S(1)} collective-permute-done((bf16[136,640]{1,0:T(8,128)(2,1)S(1)}, bf16[136,640]{1,0:T(8,128)(2,1)S(1)}, u32[]{:S(2)}, u32[]{:S(2)}) %collective-permute-start.8) | collective-permute-done | bytes 174112 | tf_op jit(solution)/shard_map/ppermute | solution.py:626
  37.4 1.4 %collective-permute-start.9 = (bf16[136,640]{1,0:T(8,128)(2,1)S(1)}, bf16[136,640]{1,0:T(8,128)(2,1)S(1)}, u32[]{:S(2)}, u32[]{:S(2)}) collective-permute-start(bf16[136,640]{1,0:T(8,128)(2,1)S(1)} %collective-permute-done.7.refs_1_.refs_9_), channel_id=1, source_target_pairs={{0,4},{4,0},{8,12},{12,8},{16,20},{20,16},{24,28},{28,24},{1,5},{5... | collective-permute-start | bytes 522248 | tf_op jit(solution)/shard_map/ppermute | solution.py:623
  38.8 3.5 %attend.2 = (bf16[256,512]{1,0:T(8,128)(2,1)S(1)}, bf16[256,512]{1,0:T(8,128)(2,1)S(1)}, bf16[256,512]{1,0:T(8,128)(2,1)S(1)}, bf16[136,512]{1,0:T(8,128)(2,1)S(...) custom-call(s32[16,32]{1,0:T(8,128)S(1)} %plan.1.table_ref, bf16[136,640]{1,0:T(8,128)(2,1)S(1)} %copy-done.1, ...), custom_call_target="tpu_custom_call" | custom-call | flops 3600000000 | bytes 10800000 | tf_op jit(solution)/shard_map/attend/pallas_call | solution.py:362
  44.2 3.8 %attend.3 = (bf16[256,512]{1,0:T(8,128)(2,1)S(1)}, bf16[256,512]{1,0:T(8,128)(2,1)S(1)}, bf16[256,512]{1,0:T(8,128)(2,1)S(1)}, bf16[136,512]{1,0:T(8,128)(2,1)S(...) custom-call(s32[16,32]{1,0:T(8,128)S(1)} %plan.1.table_ref, bf16[136,640]{1,0:T(8,128)(2,1)S(1)} %copy-done.2, ...), custom_call_target="tpu_custom_call" | custom-call | flops 3600000000 | bytes 10800000 | tf_op jit(solution)/shard_map/attend/pallas_call | solution.py:362
  48.1 1.6 %collective-permute-start.11 = (bf16[136,512]{1,0:T(8,128)(2,1)S(1)}, bf16[136,512]{1,0:T(8,128)(2,1)S(1)}, u32[]{:S(2)}, u32[]{:S(2)}) collective-permute-start(bf16[136,512]{1,0:T(8,128)(2,1)S(1)} %get-tuple-element.66), channel_id=1, source_target_pairs={{0,4},{4,0},{8,12},{12,8},{16,20},{20,16},{24,28},{28,24},{1,5},{5... | collective-permute-start | bytes 417800 | tf_op jit(solution)/shard_map/ppermute | solution.py:623
  53.9 1.7 %collective-permute-done.14.from_z = bf16[136,512]{1,0:T(8,128)(2,1)S(1)} collective-permute-done((bf16[136,512]{1,0:T(8,128)(2,1)S(1)}, bf16[136,512]{1,0:T(8,128)(2,1)S(1)}, u32[]{:S(2)}, u32[]{:S(2)}) %collective-permute-start.14) | collective-permute-done | bytes 139296 | tf_op jit(solution)/shard_map/ppermute | solution.py:626
  56.7 1.3 %collective-permute-start.16 = (bf16[264,512]{1,0:T(8,128)(2,1)S(1)}, bf16[264,512]{1,0:T(8,128)(2,1)S(1)}, u32[]{:S(2)}, u32[]{:S(2)}) collective-permute-start(bf16[264,512]{1,0:T(8,128)(2,1)S(1)} %get-tuple-element.77), channel_id=1, source_target_pairs={{0,8},{4,12},{8,0},{12,4},{16,24},{20,28},{24,16},{28,20},{1,9},{5... | collective-permute-start | bytes 811016 | tf_op jit(solution)/shard_map/ppermute | solution.py:626
  58.0 3.5 %index_scores.1._ = f32[4,4,2048]{2,1,0:T(4,128)} custom-call(s32[16,32]{1,0:T(8,128)S(1)} %plan.1.table_ref, bf16[136,640]{1,0:T(8,128)(2,1)S(1)} %copy-done.1, bf16[136,640]{1,0:T(8,128)(2,1)S(1)} %collective-permute-done.2.first_ref.refs_1_, bf16[136,640]{1,0:T(8,128)(2,1)S(1)} %collective-permute-done.second_ref.refs_2_, ...), custom_call_target="tpu_custom_call" | custom-call | flops 3500000000 | bytes 10500000 | tf_op jit(solution)/shard_map/index_scores/pallas_call | solution.py:596
  62.3 2.3 %collective-permute-start.22 = (bf16[136,512]{1,0:T(8,128)(2,1)S(1)}, bf16[136,512]{1,0:T(8,128)(2,1)S(1)}, u32[]{:S(2)}, u32[]{:S(2)}) collective-permute-start(bf16[136,512]{1,0:T(8,128)(2,1)S(1)} %get-tuple-element.91), channel_id=1, source_target_pairs={{0,16},{4,20},{8,24},{12,28},{16,0},{20,4},{24,8},{28,12},{1,17},{... | collective-permute-start | bytes 417800 | tf_op jit(solution)/shard_map/ppermute | solution.py:626
  64.6 1.7 %collective-permute-done.16.from_z = bf16[264,512]{1,0:T(8,128)(2,1)S(1)} collective-permute-done((bf16[264,512]{1,0:T(8,128)(2,1)S(1)}, bf16[264,512]{1,0:T(8,128)(2,1)S(1)}, u32[]{:S(2)}, u32[]{:S(2)}) %collective-permute-start.16) | collective-permute-done | bytes 270368 | tf_op jit(solution)/shard_map/ppermute | solution.py:626
  66.7 2.5 %collective-permute-start.17 = (bf16[136,512]{1,0:T(8,128)(2,1)S(1)}, bf16[136,512]{1,0:T(8,128)(2,1)S(1)}, u32[]{:S(2)}, u32[]{:S(2)}) collective-permute-start(bf16[136,512]{1,0:T(8,128)(2,1)S(1)} %get-tuple-element.81), channel_id=1, source_target_pairs={{0,16},{4,20},{8,24},{12,28},{16,0},{20,4},{24,8},{28,12},{1,17},{... | collective-permute-start | bytes 417800 | tf_op jit(solution)/shard_map/ppermute | solution.py:626
  71.5 2.7 %collective-permute-done.17.other_ref = bf16[136,512]{1,0:T(8,128)(2,1)S(1)} collective-permute-done((bf16[136,512]{1,0:T(8,128)(2,1)S(1)}, bf16[136,512]{1,0:T(8,128)(2,1)S(1)}, u32[]{:S(2)}, u32[]{:S(2)}) %collective-permute-start.17) | collective-permute-done | bytes 139296 | tf_op jit(solution)/shard_map/ppermute | solution.py:626
  (63 shorter events, 18.3 us)
Async XLA Ops:
  2.8 13.1 %collective-permute-start.2 = (bf16[136,640]{1,0:T(8,128)(2,1)}, bf16[136,640]{1,0:T(8,128)(2,1)S(1)}, u32[]{:S(2)}, u32[]{:S(2)}) collective-permute-start(bf16[136,640]{1,0:T(8,128)(2,1)} %get-tuple-element.47.refs_0_), channel_id=1, source_target_pairs={{0,8},{4,12},{8,0},{12,4},{16,24},{20,28},{24,16},{28,20},{1,9},{5... | collective-permute-start | bytes 522248 | tf_op jit(solution)/shard_map/ppermute | solution.py:626
  5.9 10.8 %collective-permute-start = (bf16[136,640]{1,0:T(8,128)(2,1)}, bf16[136,640]{1,0:T(8,128)(2,1)S(1)}, u32[]{:S(2)}, u32[]{:S(2)}) collective-permute-start(bf16[136,640]{1,0:T(8,128)(2,1)} %get-tuple-element.47.refs_0_), channel_id=1, source_target_pairs={{0,16},{4,20},{8,24},{12,28},{16,0},{20,4},{24,8},{28,12},{1,17},{... | collective-permute-start | bytes 522248 | tf_op jit(solution)/shard_map/ppermute | solution.py:626
  8.5 9.5 %collective-permute-start.1 = (bf16[272,640]{1,0:T(8,128)(2,1)}, bf16[272,640]{1,0:T(8,128)(2,1)S(1)}, u32[]{:S(2)}, u32[]{:S(2)}) collective-permute-start(bf16[272,640]{1,0:T(8,128)(2,1)} %get-tuple-element.49), channel_id=1, source_target_pairs={{0,4},{4,0},{8,12},{12,8},{16,20},{20,16},{24,28},{28,24},{1,5},{5... | collective-permute-start | bytes 1044488 | tf_op jit(solution)/shard_map/ppermute | solution.py:623
  18.0 7.5 %collective-permute-start.3 = (bf16[136,640]{1,0:T(8,128)(2,1)S(1)}, bf16[136,640]{1,0:T(8,128)(2,1)S(1)}, u32[]{:S(2)}, u32[]{:S(2)}) collective-permute-start(bf16[136,640]{1,0:T(8,128)(2,1)S(1)} %collective-permute-done.second_ref.refs_2_), channel_id=1, source_target_pairs={{0,8},{4,12},{8,0},{12,4},{16,24},{20,28},{24,16},{28,20},{1,9},{5... | collective-permute-start | bytes 522248 | tf_op jit(solution)/shard_map/ppermute | solution.py:626
  18.5 9.1 %collective-permute-start.5 = (bf16[136,640]{1,0:T(8,128)(2,1)S(1)}, bf16[136,640]{1,0:T(8,128)(2,1)S(1)}, u32[]{:S(2)}, u32[]{:S(2)}) collective-permute-start(bf16[136,640]{1,0:T(8,128)(2,1)S(1)} %copy-done.2), channel_id=1, source_target_pairs={{0,16},{4,20},{8,24},{12,28},{16,0},{20,4},{24,8},{28,12},{1,17},{... | collective-permute-start | bytes 522248 | tf_op jit(solution)/shard_map/ppermute | solution.py:626
  19.7 19.0 %copy-start.1 = (bf16[136,640]{1,0:T(8,128)(2,1)S(1)}, bf16[136,640]{1,0:T(8,128)(2,1)}, u32[]{:S(2)}) copy-start(bf16[136,640]{1,0:T(8,128)(2,1)} %get-tuple-element.47.refs_0_) | copy-start | bytes 522244
  19.7 7.8 %collective-permute-start.4 = (bf16[272,640]{1,0:T(8,128)(2,1)S(1)}, bf16[272,640]{1,0:T(8,128)(2,1)S(1)}, u32[]{:S(2)}, u32[]{:S(2)}) collective-permute-start(bf16[272,640]{1,0:T(8,128)(2,1)S(1)} %pair_up.2), channel_id=1, source_target_pairs={{0,4},{4,0},{8,12},{12,8},{16,20},{20,16},{24,28},{28,24},{1,5},{5... | collective-permute-start | bytes 1044488 | tf_op jit(solution)/shard_map/ppermute | solution.py:623
  21.3 9.9 %collective-permute-start.18 = (bf16[16,128,128]{2,1,0:T(8,128)(2,1)S(1)}, bf16[16,128,128]{2,1,0:T(8,128)(2,1)S(1)}, u32[]{:S(2)}, u32[]{:S(2)}) collective-permute-start(bf16[16,128,128]{2,1,0:T(8,128)(2,1)S(1)} %copy-done), channel_id=1, source_target_pairs={{0,1},{1,0},{2,3},{3,2},{4,5},{5,4},{6,7},{7,6},{8,9},{9,8},{10,11... | collective-permute-start | bytes 1572872 | tf_op jit(solution)/shard_map/ppermute | solution.py:629
  27.6 8.9 %collective-permute-start.6 = (bf16[272,640]{1,0:T(8,128)(2,1)S(1)}, bf16[272,640]{1,0:T(8,128)(2,1)S(1)}, u32[]{:S(2)}, u32[]{:S(2)}) collective-permute-start(bf16[272,640]{1,0:T(8,128)(2,1)S(1)} %pair_up.3), channel_id=1, source_target_pairs={{0,4},{4,0},{8,12},{12,8},{16,20},{20,16},{24,28},{28,24},{1,5},{5... | collective-permute-start | bytes 1044488 | tf_op jit(solution)/shard_map/ppermute | solution.py:623
  29.1 5.5 %collective-permute-start.7 = (bf16[136,640]{1,0:T(8,128)(2,1)S(1)}, bf16[136,640]{1,0:T(8,128)(2,1)S(1)}, u32[]{:S(2)}, u32[]{:S(2)}) collective-permute-start(bf16[136,640]{1,0:T(8,128)(2,1)S(1)} %copy-done.2), channel_id=1, source_target_pairs={{0,8},{4,12},{8,0},{12,4},{16,24},{20,28},{24,16},{28,20},{1,9},{5... | collective-permute-start | bytes 522248 | tf_op jit(solution)/shard_map/ppermute | solution.py:626
  29.9 6.5 %collective-permute-start.8 = (bf16[136,640]{1,0:T(8,128)(2,1)S(1)}, bf16[136,640]{1,0:T(8,128)(2,1)S(1)}, u32[]{:S(2)}, u32[]{:S(2)}) collective-permute-start(bf16[136,640]{1,0:T(8,128)(2,1)S(1)} %collective-permute-done.5.second_ref.refs_2_.refs_10_), channel_id=1, source_target_pairs={{0,8},{4,12},{8,0},{12,4},{16,24},{20,28},{24,16},{28,20},{1,9},{5... | collective-permute-start | bytes 522248 | tf_op jit(solution)/shard_map/ppermute | solution.py:626
  31.3 38.0 %collective-permute-start.19 = (bf16[2,16,128,128]{3,2,1,0:T(8,128)(2,1)S(1)}, bf16[2,16,128,128]{3,2,1,0:T(8,128)(2,1)S(1)}, u32[]{:S(2)}, u32[]{:S(2)}) collective-permute-start(bf16[2,16,128,128]{3,2,1,0:T(8,128)(2,1)S(1)} %pair_cores.1.here_ref), channel_id=1, source_target_pairs={{0,2},{1,3},{2,0},{3,1},{4,6},{5,7},{6,4},{7,5},{8,10},{9,11},{10,... | collective-permute-start | bytes 3145736 | tf_op jit(solution)/shard_map/ppermute | solution.py:629
  36.5 7.7 %collective-permute-start.10 = (bf16[136,640]{1,0:T(8,128)(2,1)S(1)}, bf16[136,640]{1,0:T(8,128)(2,1)S(1)}, u32[]{:S(2)}, u32[]{:S(2)}) collective-permute-start(bf16[136,640]{1,0:T(8,128)(2,1)S(1)} %second_of.1.refs_6_.refs_14_), channel_id=1, source_target_pairs={{0,8},{4,12},{8,0},{12,4},{16,24},{20,28},{24,16},{28,20},{1,9},{5... | collective-permute-start | bytes 522248 | tf_op jit(solution)/shard_map/ppermute | solution.py:626
  37.4 6.8 %collective-permute-start.9 = (bf16[136,640]{1,0:T(8,128)(2,1)S(1)}, bf16[136,640]{1,0:T(8,128)(2,1)S(1)}, u32[]{:S(2)}, u32[]{:S(2)}) collective-permute-start(bf16[136,640]{1,0:T(8,128)(2,1)S(1)} %collective-permute-done.7.refs_1_.refs_9_), channel_id=1, source_target_pairs={{0,4},{4,0},{8,12},{12,8},{16,20},{20,16},{24,28},{28,24},{1,5},{5... | collective-permute-start | bytes 522248 | tf_op jit(solution)/shard_map/ppermute | solution.py:623
  42.3 8.5 %collective-permute-start.12 = (bf16[136,512]{1,0:T(8,128)(2,1)S(1)}, bf16[136,512]{1,0:T(8,128)(2,1)S(1)}, u32[]{:S(2)}, u32[]{:S(2)}) collective-permute-start(bf16[136,512]{1,0:T(8,128)(2,1)S(1)} %get-tuple-element.69), channel_id=1, source_target_pairs={{0,4},{4,0},{8,12},{12,8},{16,20},{20,16},{24,28},{28,24},{1,5},{5... | collective-permute-start | bytes 417800 | tf_op jit(solution)/shard_map/ppermute | solution.py:623
  43.0 7.8 %collective-permute-start.13 = (bf16[136,512]{1,0:T(8,128)(2,1)S(1)}, bf16[136,512]{1,0:T(8,128)(2,1)S(1)}, u32[]{:S(2)}, u32[]{:S(2)}) collective-permute-start(bf16[136,512]{1,0:T(8,128)(2,1)S(1)} %get-tuple-element.72), channel_id=1, source_target_pairs={{0,8},{4,12},{8,0},{12,4},{16,24},{20,28},{24,16},{28,20},{1,9},{5... | collective-permute-start | bytes 417800 | tf_op jit(solution)/shard_map/ppermute | solution.py:626
  48.1 5.9 %collective-permute-start.11 = (bf16[136,512]{1,0:T(8,128)(2,1)S(1)}, bf16[136,512]{1,0:T(8,128)(2,1)S(1)}, u32[]{:S(2)}, u32[]{:S(2)}) collective-permute-start(bf16[136,512]{1,0:T(8,128)(2,1)S(1)} %get-tuple-element.66), channel_id=1, source_target_pairs={{0,4},{4,0},{8,12},{12,8},{16,20},{20,16},{24,28},{28,24},{1,5},{5... | collective-permute-start | bytes 417800 | tf_op jit(solution)/shard_map/ppermute | solution.py:623
  49.6 6.0 %collective-permute-start.14 = (bf16[136,512]{1,0:T(8,128)(2,1)S(1)}, bf16[136,512]{1,0:T(8,128)(2,1)S(1)}, u32[]{:S(2)}, u32[]{:S(2)}) collective-permute-start(bf16[136,512]{1,0:T(8,128)(2,1)S(1)} %get-tuple-element.75), channel_id=1, source_target_pairs={{0,8},{4,12},{8,0},{12,4},{16,24},{20,28},{24,16},{28,20},{1,9},{5... | collective-permute-start | bytes 417800 | tf_op jit(solution)/shard_map/ppermute | solution.py:626
  51.2 10.3 %collective-permute-start.20 = (bf16[264,512]{1,0:T(8,128)(2,1)S(1)}, bf16[264,512]{1,0:T(8,128)(2,1)S(1)}, u32[]{:S(2)}, u32[]{:S(2)}) collective-permute-start(bf16[264,512]{1,0:T(8,128)(2,1)S(1)} %get-tuple-element.87), channel_id=1, source_target_pairs={{0,4},{4,0},{8,12},{12,8},{16,20},{20,16},{24,28},{28,24},{1,5},{5... | collective-permute-start | bytes 811016 | tf_op jit(solution)/shard_map/ppermute | solution.py:623
  51.4 10.5 %collective-permute-start.21 = (bf16[264,512]{1,0:T(8,128)(2,1)S(1)}, bf16[264,512]{1,0:T(8,128)(2,1)S(1)}, u32[]{:S(2)}, u32[]{:S(2)}) collective-permute-start(bf16[264,512]{1,0:T(8,128)(2,1)S(1)} %get-tuple-element.88), channel_id=1, source_target_pairs={{0,8},{4,12},{8,0},{12,4},{16,24},{20,28},{24,16},{28,20},{1,9},{5... | collective-permute-start | bytes 811016 | tf_op jit(solution)/shard_map/ppermute | solution.py:626
  56.0 8.7 %collective-permute-start.15 = (bf16[264,512]{1,0:T(8,128)(2,1)S(1)}, bf16[264,512]{1,0:T(8,128)(2,1)S(1)}, u32[]{:S(2)}, u32[]{:S(2)}) collective-permute-start(bf16[264,512]{1,0:T(8,128)(2,1)S(1)} %get-tuple-element.76), channel_id=1, source_target_pairs={{0,4},{4,0},{8,12},{12,8},{16,20},{20,16},{24,28},{28,24},{1,5},{5... | collective-permute-start | bytes 811016 | tf_op jit(solution)/shard_map/ppermute | solution.py:623
  56.7 9.7 %collective-permute-start.16 = (bf16[264,512]{1,0:T(8,128)(2,1)S(1)}, bf16[264,512]{1,0:T(8,128)(2,1)S(1)}, u32[]{:S(2)}, u32[]{:S(2)}) collective-permute-start(bf16[264,512]{1,0:T(8,128)(2,1)S(1)} %get-tuple-element.77), channel_id=1, source_target_pairs={{0,8},{4,12},{8,0},{12,4},{16,24},{20,28},{24,16},{28,20},{1,9},{5... | collective-permute-start | bytes 811016 | tf_op jit(solution)/shard_map/ppermute | solution.py:626
  62.3 8.0 %collective-permute-start.22 = (bf16[136,512]{1,0:T(8,128)(2,1)S(1)}, bf16[136,512]{1,0:T(8,128)(2,1)S(1)}, u32[]{:S(2)}, u32[]{:S(2)}) collective-permute-start(bf16[136,512]{1,0:T(8,128)(2,1)S(1)} %get-tuple-element.91), channel_id=1, source_target_pairs={{0,16},{4,20},{8,24},{12,28},{16,0},{20,4},{24,8},{28,12},{1,17},{... | collective-permute-start | bytes 417800 | tf_op jit(solution)/shard_map/ppermute | solution.py:626
  66.7 7.5 %collective-permute-start.17 = (bf16[136,512]{1,0:T(8,128)(2,1)S(1)}, bf16[136,512]{1,0:T(8,128)(2,1)S(1)}, u32[]{:S(2)}, u32[]{:S(2)}) collective-permute-start(bf16[136,512]{1,0:T(8,128)(2,1)S(1)} %get-tuple-element.81), channel_id=1, source_target_pairs={{0,16},{4,20},{8,24},{12,28},{16,0},{20,4},{24,8},{28,12},{1,17},{... | collective-permute-start | bytes 417800 | tf_op jit(solution)/shard_map/ppermute | solution.py:626
  (10 other events, 94.2 us)

commit v6 on v5

--- a/solution.py
+++ b/solution.py
@@ -12,7 +12,7 @@
 BLOCK = 64
 VMEM_LIMIT = 16 * 1024 * 1024
 PACK_LIMIT = 63_000_000
-ATTEND_LIMIT = 30_000_000
+ATTEND_LIMIT = 24_000_000
 TABLE = 32
 GATHER_LIMIT = (46_000_000, 38_000_000)
 SHORT = 4
@@ -645,22 +645,23 @@
     up_core = across_req(after(value_up_weight, *round1), 1)
 
     round2 = (x12, z3c0, z2c1, blocks_b)
-    x32 = across_x(pair_up(after(z3c0, *round2), z2c1))
+    xz3c0 = across_x(after(z3c0, *round2))
+    xz2c1 = across_x(after(z2c1, *round2))
     z1c1 = across_z(after(own1, *round2), 1)
     z3c1 = across_z(after(z2c1, *round2), 1)
     up_here = pair_cores(after(value_up_weight, *round2), up_core)
     up_there = across_req(up_here, 2)
 
-    round3 = (x32, z1c1, z3c1)
-    xz1c1 = across_x(after(z1c1, *round3))
-    xz2c1 = second_of(after(x32, *round3))
+    xz1c1 = across_x(z1c1)
     xz3c1 = across_z(xz2c1, 1)
     gathered = [
-        [(own0, 0), (z1c0, 0), (z2c0, 0), (z3c0, 0), (x0, 0), (x12, 0), (x12, SENT), (x32, 0)],
+        [(own0, 0), (z1c0, 0), (z2c0, 0), (z3c0, 0), (x0, 0), (x12, 0), (x12, SENT), (xz3c0, 0)],
         [(own1, 0), (z1c1, 0), (z2c1, 0), (z3c1, 0), (x0, SENT), (xz1c1, 0), (xz2c1, 0), (xz3c1, 0)],
     ]
 
-    near0, far0, cross0, x5, z7, stats0 = attend(0, after(table, xz2c1), gathered[0], blocks_a, latents_t)
+    near0, far0, cross0, x5, z7, stats0 = attend(
+        0, after(table, z1c1), gathered[0], blocks_a, latents_t
+    )
     x5, z7 = across_x(x5), across_z(z7, 1)
     near1, far1, cross1, x5c1, z7c1, stats1 = attend(1, after(table, stats0), gathered[1], blocks_b, latents_t)
     x5c1, z7c1 = across_x(x5c1), across_z(z7c1, 1)

time: 75.6 us -> 75.9 us (level)
  waiting for transfers between devices: 15.6 us -> 17.8 us
  starting transfers between devices: 30.8 us -> 28.9 us
    ppermute x13, starting transfers between devices: 20 us -> 14.7 us  [across_z(): return lax.ppermute(value, 'ctx', [(i, i ^ 2 * distance) for i in range(8)])]
    ppermute x8 -> x9, starting transfers between devices: 9.18 us -> 12.6 us  [across_x(): return lax.ppermute(value, 'ctx', [(i, i ^ 1) for i in range(8)])]
    ppermute x8 -> x9, waiting for transfers between devices: 2.62 us -> 5.29 us  [across_x(): return lax.ppermute(value, 'ctx', [(i, i ^ 1) for i in range(8)])]
  transfers between devices with their start and end apart: 23 -> 24, of which waited for: 10 -> 10; matrix products, arithmetic and copies ran while one was open for 0% -> 0% of each run, Pallas kernels for 32% -> 32%
where the time goes in v6:
time: 75.9 us; the launch traced here: 75.7 us
  starting transfers between devices  28.9 us (38%)
  Pallas kernels  27.2 us (36%)
  waiting for transfers between devices  17.8 us (23%)
  local copies, waits for them, and re-layouts  0.95 us (1%)
  between operations  0.85 us (1%)
    ppermute x13, starting transfers between devices, across_z(): return lax.ppermute(value, 'ctx', [(i, i ^ 2 * distance) for i in range(8)])  14.7 us
    ppermute x9, starting transfers between devices, across_x(): return lax.ppermute(value, 'ctx', [(i, i ^ 1) for i in range(8)])  12.6 us
    ppermute x13, waiting for transfers between devices, across_z(): return lax.ppermute(value, 'ctx', [(i, i ^ 2 * distance) for i in range(8)])  12.5 us
    pallas_call x2, Pallas kernels, gather(): call(functools.partial(gather_kernel, requests), limit=limit, in_specs=[p...  9.2 us
    pallas_call x2, Pallas kernels, attend(): call(functools.partial(attend_kernel, chunk, tuple((at for _, at in gathe...  7.37 us
    ppermute x9, waiting for transfers between devices, across_x(): return lax.ppermute(value, 'ctx', [(i, i ^ 1) for i in range(8)])  5.29 us
    pallas_call x1, Pallas kernels, index_rows(): call(functools.partial(index_kernel, tuple((at for _, at in members))), g...  3.51 us
    pallas_call x2, Pallas kernels, finish(): call(finish_kernel, grid=(1,), in_specs=specs, out_specs=pl.BlockSpec((4,...  2.43 us
  transfers between devices with their start and end apart: 24, of which 10 were waited for; matrix products, arithmetic and copies ran while one was open for 0% of the time, Pallas kernels for 32%

profile of v6, /device:TPU:0, one launch (start us, length us, event | category | flops | bytes accessed | tf_op | source)
XLA Modules:
  0.0 75.7 jit_solution(1174352146668960993)
XLA Ops:
  0.7 2.1 %pack.1 = (bf16[136,640]{1,0:T(8,128)(2,1)}, bf16[136,640]{1,0:T(8,128)(2,1)}, bf16[272,640]{1,0:T(8,128)(2,1)}) custom-call(bf16[4,4,16,576]{3,2,1,0:T(8,128)(2,1)} %q_hbm.1, bf16[4,4,8,128]{3,2,1,0:T(8,128)(2,1)} %iq_hbm.1, bf16[4,4,8]{2,1,0:T(4,128)(2,1)} %iw_hbm.1), custom_call_target="tpu_custom_call" | custom-call | flops 2000000000 | bytes 6000000 | tf_op jit(solution)/shard_map/pack/pallas_call | solution.py:94
  2.8 4.1 %collective-permute-start.2 = (bf16[136,640]{1,0:T(8,128)(2,1)}, bf16[136,640]{1,0:T(8,128)(2,1)S(1)}, u32[]{:S(2)}, u32[]{:S(2)}) collective-permute-start(bf16[136,640]{1,0:T(8,128)(2,1)} %get-tuple-element.45.refs_0_), channel_id=1, source_target_pairs={{0,16},{4,20},{8,24},{12,28},{16,0},{20,4},{24,8},{28,12},{1,17},{... | collective-permute-start | bytes 522248 | tf_op jit(solution)/shard_map/ppermute | solution.py:626
  6.9 1.6 %collective-permute-start = (bf16[136,640]{1,0:T(8,128)(2,1)}, bf16[136,640]{1,0:T(8,128)(2,1)S(1)}, u32[]{:S(2)}, u32[]{:S(2)}) collective-permute-start(bf16[136,640]{1,0:T(8,128)(2,1)} %get-tuple-element.45.refs_0_), channel_id=1, source_target_pairs={{0,8},{4,12},{8,0},{12,4},{16,24},{20,28},{24,16},{28,20},{1,9},{5... | collective-permute-start | bytes 522248 | tf_op jit(solution)/shard_map/ppermute | solution.py:626
  8.5 1.5 %collective-permute-start.1 = (bf16[272,640]{1,0:T(8,128)(2,1)}, bf16[272,640]{1,0:T(8,128)(2,1)S(1)}, u32[]{:S(2)}, u32[]{:S(2)}) collective-permute-start(bf16[272,640]{1,0:T(8,128)(2,1)} %get-tuple-element.48), channel_id=1, source_target_pairs={{0,4},{4,0},{8,12},{12,8},{16,20},{20,16},{24,28},{28,24},{1,5},{5... | collective-permute-start | bytes 1044488 | tf_op jit(solution)/shard_map/ppermute | solution.py:623
  10.9 5.0 %gather_blocks.2.refs_8_ = bf16[8,576,512]{2,1,0:T(8,128)(2,1)S(1)} custom-call(s32[16,32]{1,0:T(8,128)S(1)} %plan.1.table_ref, bf16[4,576,2048]{2,1,0:T(8,128)(2,1)} %bitcast.1), custom_call_target="tpu_custom_call" | custom-call | flops 5200000000 | bytes 15600000 | tf_op jit(solution)/shard_map/gather_blocks/pallas_call | solution.py:251
  15.9 2.1 %collective-permute-done.1.refs_4_.refs_12_ = bf16[272,640]{1,0:T(8,128)(2,1)S(1)} collective-permute-done((bf16[272,640]{1,0:T(8,128)(2,1)}, bf16[272,640]{1,0:T(8,128)(2,1)S(1)}, u32[]{:S(2)}, u32[]{:S(2)}) %collective-permute-start.1) | collective-permute-done | bytes 348192 | tf_op jit(solution)/shard_map/ppermute | solution.py:623
  19.4 1.6 %collective-permute-start.3 = (bf16[272,640]{1,0:T(8,128)(2,1)S(1)}, bf16[272,640]{1,0:T(8,128)(2,1)S(1)}, u32[]{:S(2)}, u32[]{:S(2)}) collective-permute-start(bf16[272,640]{1,0:T(8,128)(2,1)S(1)} %pair_up.1), channel_id=1, source_target_pairs={{0,4},{4,0},{8,12},{12,8},{16,20},{20,16},{24,28},{28,24},{1,5},{5... | collective-permute-start | bytes 1044488 | tf_op jit(solution)/shard_map/ppermute | solution.py:623
  21.0 4.2 %gather_blocks.3.refs_8_ = bf16[8,576,512]{2,1,0:T(8,128)(2,1)S(1)} custom-call(s32[16,32]{1,0:T(8,128)S(1)} %plan.1.table_ref, bf16[4,576,2048]{2,1,0:T(8,128)(2,1)S(1)} %bitcast.4), custom_call_target="tpu_custom_call" | custom-call | flops 5200000000 | bytes 15600000 | tf_op jit(solution)/shard_map/gather_blocks/pallas_call | solution.py:251
  25.8 2.1 %collective-permute-done.5.refs_2_.refs_10_ = bf16[136,640]{1,0:T(8,128)(2,1)S(1)} collective-permute-done((bf16[136,640]{1,0:T(8,128)(2,1)S(1)}, bf16[136,640]{1,0:T(8,128)(2,1)S(1)}, u32[]{:S(2)}, u32[]{:S(2)}) %collective-permute-start.5) | collective-permute-done | bytes 174112 | tf_op jit(solution)/shard_map/ppermute | solution.py:626
  29.3 1.5 %collective-permute-start.10 = (bf16[136,640]{1,0:T(8,128)(2,1)S(1)}, bf16[136,640]{1,0:T(8,128)(2,1)S(1)}, u32[]{:S(2)}, u32[]{:S(2)}) collective-permute-start(bf16[136,640]{1,0:T(8,128)(2,1)S(1)} %collective-permute-done.5.refs_2_.refs_10_), channel_id=1, source_target_pairs={{0,4},{4,0},{8,12},{12,8},{16,20},{20,16},{24,28},{28,24},{1,5},{5... | collective-permute-start | bytes 522248 | tf_op jit(solution)/shard_map/ppermute | solution.py:623
  31.4 1.7 %collective-permute-start.8 = (bf16[136,640]{1,0:T(8,128)(2,1)S(1)}, bf16[136,640]{1,0:T(8,128)(2,1)S(1)}, u32[]{:S(2)}, u32[]{:S(2)}) collective-permute-start(bf16[136,640]{1,0:T(8,128)(2,1)S(1)} %collective-permute-done.5.refs_2_.refs_10_), channel_id=1, source_target_pairs={{0,8},{4,12},{8,0},{12,4},{16,24},{20,28},{24,16},{28,20},{1,9},{5... | collective-permute-start | bytes 522248 | tf_op jit(solution)/shard_map/ppermute | solution.py:626
  33.0 2.7 %collective-permute-done.6.refs_1_.refs_9_ = bf16[136,640]{1,0:T(8,128)(2,1)S(1)} collective-permute-done((bf16[136,640]{1,0:T(8,128)(2,1)S(1)}, bf16[136,640]{1,0:T(8,128)(2,1)S(1)}, u32[]{:S(2)}, u32[]{:S(2)}) %collective-permute-start.6) | collective-permute-done | bytes 174112 | tf_op jit(solution)/shard_map/ppermute | solution.py:626
  35.7 2.1 %collective-permute-start.9 = (bf16[136,640]{1,0:T(8,128)(2,1)S(1)}, bf16[136,640]{1,0:T(8,128)(2,1)S(1)}, u32[]{:S(2)}, u32[]{:S(2)}) collective-permute-start(bf16[136,640]{1,0:T(8,128)(2,1)S(1)} %collective-permute-done.6.refs_1_.refs_9_), channel_id=1, source_target_pairs={{0,4},{4,0},{8,12},{12,8},{16,20},{20,16},{24,28},{28,24},{1,5},{5... | collective-permute-start | bytes 522248 | tf_op jit(solution)/shard_map/ppermute | solution.py:623
  38.5 1.6 %collective-permute-start.20 = (bf16[2,16,128,128]{3,2,1,0:T(8,128)(2,1)S(1)}, bf16[2,16,128,128]{3,2,1,0:T(8,128)(2,1)S(1)}, u32[]{:S(2)}, u32[]{:S(2)}) collective-permute-start(bf16[2,16,128,128]{3,2,1,0:T(8,128)(2,1)S(1)} %pair_cores.1.here_ref), channel_id=1, source_target_pairs={{0,2},{1,3},{2,0},{3,1},{4,6},{5,7},{6,4},{7,5},{8,10},{9,11},{10,... | collective-permute-start | bytes 3145736 | tf_op jit(solution)/shard_map/ppermute | solution.py:629
  40.0 3.5 %attend.2 = (bf16[256,512]{1,0:T(8,128)(2,1)S(1)}, bf16[256,512]{1,0:T(8,128)(2,1)S(1)}, bf16[256,512]{1,0:T(8,128)(2,1)S(1)}, bf16[136,512]{1,0:T(8,128)(2,1)S(...) custom-call(s32[16,32]{1,0:T(8,128)S(1)} %plan.1.table_ref, bf16[136,640]{1,0:T(8,128)(2,1)S(1)} %copy-done.1, ...), custom_call_target="tpu_custom_call" | custom-call | flops 3600000000 | bytes 10800000 | tf_op jit(solution)/shard_map/attend/pallas_call | solution.py:362
  43.6 1.6 %collective-permute-start.13 = (bf16[136,512]{1,0:T(8,128)(2,1)S(1)}, bf16[136,512]{1,0:T(8,128)(2,1)S(1)}, u32[]{:S(2)}, u32[]{:S(2)}) collective-permute-start(bf16[136,512]{1,0:T(8,128)(2,1)S(1)} %get-tuple-element.65), channel_id=1, source_target_pairs={{0,4},{4,0},{8,12},{12,8},{16,20},{20,16},{24,28},{28,24},{1,5},{5... | collective-permute-start | bytes 417800 | tf_op jit(solution)/shard_map/ppermute | solution.py:623
  46.3 3.8 %attend.3 = (bf16[256,512]{1,0:T(8,128)(2,1)S(1)}, bf16[256,512]{1,0:T(8,128)(2,1)S(1)}, bf16[256,512]{1,0:T(8,128)(2,1)S(1)}, bf16[136,512]{1,0:T(8,128)(2,1)S(...) custom-call(s32[16,32]{1,0:T(8,128)S(1)} %plan.1.table_ref, bf16[136,640]{1,0:T(8,128)(2,1)S(1)} %copy-done.2, ...), custom_call_target="tpu_custom_call" | custom-call | flops 3600000000 | bytes 10800000 | tf_op jit(solution)/shard_map/attend/pallas_call | solution.py:362
  52.0 1.5 %collective-permute-start.21 = (bf16[264,512]{1,0:T(8,128)(2,1)S(1)}, bf16[264,512]{1,0:T(8,128)(2,1)S(1)}, u32[]{:S(2)}, u32[]{:S(2)}) collective-permute-start(bf16[264,512]{1,0:T(8,128)(2,1)S(1)} %get-tuple-element.83), channel_id=1, source_target_pairs={{0,4},{4,0},{8,12},{12,8},{16,20},{20,16},{24,28},{28,24},{1,5},{5... | collective-permute-start | bytes 811016 | tf_op jit(solution)/shard_map/ppermute | solution.py:623
  54.7 2.1 %collective-permute-done.12.from_x = bf16[136,512]{1,0:T(8,128)(2,1)S(1)} collective-permute-done((bf16[136,512]{1,0:T(8,128)(2,1)S(1)}, bf16[136,512]{1,0:T(8,128)(2,1)S(1)}, u32[]{:S(2)}, u32[]{:S(2)}) %collective-permute-start.12) | collective-permute-done | bytes 139296 | tf_op jit(solution)/shard_map/ppermute | solution.py:623
  57.7 1.4 %collective-permute-start.16 = (bf16[264,512]{1,0:T(8,128)(2,1)S(1)}, bf16[264,512]{1,0:T(8,128)(2,1)S(1)}, u32[]{:S(2)}, u32[]{:S(2)}) collective-permute-start(bf16[264,512]{1,0:T(8,128)(2,1)S(1)} %get-tuple-element.72), channel_id=1, source_target_pairs={{0,4},{4,0},{8,12},{12,8},{16,20},{20,16},{24,28},{28,24},{1,5},{5... | collective-permute-start | bytes 811016 | tf_op jit(solution)/shard_map/ppermute | solution.py:623
  60.1 3.5 %index_scores.1._ = f32[4,4,2048]{2,1,0:T(4,128)} custom-call(s32[16,32]{1,0:T(8,128)S(1)} %plan.1.table_ref, bf16[136,640]{1,0:T(8,128)(2,1)S(1)} %copy-done.1, bf16[136,640]{1,0:T(8,128)(2,1)S(1)} %collective-permute-done.first_ref.refs_1_, bf16[136,640]{1,0:T(8,128)(2,1)S(1)} %collective-permute-done.2.second_ref.refs_2_, ...), custom_call_target="tpu_custom_call" | custom-call | flops 3500000000 | bytes 10500000 | tf_op jit(solution)/shard_map/index_scores/pallas_call | solution.py:596
  64.5 2.1 %collective-permute-done.17.from_z = bf16[264,512]{1,0:T(8,128)(2,1)S(1)} collective-permute-done((bf16[264,512]{1,0:T(8,128)(2,1)S(1)}, bf16[264,512]{1,0:T(8,128)(2,1)S(1)}, u32[]{:S(2)}, u32[]{:S(2)}) %collective-permute-start.17) | collective-permute-done | bytes 270368 | tf_op jit(solution)/shard_map/ppermute | solution.py:626
  68.9 2.6 %collective-permute-done.23.other_ref = bf16[136,512]{1,0:T(8,128)(2,1)S(1)} collective-permute-done((bf16[136,512]{1,0:T(8,128)(2,1)S(1)}, bf16[136,512]{1,0:T(8,128)(2,1)S(1)}, u32[]{:S(2)}, u32[]{:S(2)}) %collective-permute-start.23) | collective-permute-done | bytes 139296 | tf_op jit(solution)/shard_map/ppermute | solution.py:626
  72.7 1.8 %collective-permute-done.18.other_ref = bf16[136,512]{1,0:T(8,128)(2,1)S(1)} collective-permute-done((bf16[136,512]{1,0:T(8,128)(2,1)S(1)}, bf16[136,512]{1,0:T(8,128)(2,1)S(1)}, u32[]{:S(2)}, u32[]{:S(2)}) %collective-permute-start.18) | collective-permute-done | bytes 139296 | tf_op jit(solution)/shard_map/ppermute | solution.py:626
  (63 shorter events, 17.1 us)
Async XLA Ops:
  2.8 13.1 %collective-permute-start.2 = (bf16[136,640]{1,0:T(8,128)(2,1)}, bf16[136,640]{1,0:T(8,128)(2,1)S(1)}, u32[]{:S(2)}, u32[]{:S(2)}) collective-permute-start(bf16[136,640]{1,0:T(8,128)(2,1)} %get-tuple-element.45.refs_0_), channel_id=1, source_target_pairs={{0,16},{4,20},{8,24},{12,28},{16,0},{20,4},{24,8},{28,12},{1,17},{... | collective-permute-start | bytes 522248 | tf_op jit(solution)/shard_map/ppermute | solution.py:626
  6.9 9.0 %collective-permute-start = (bf16[136,640]{1,0:T(8,128)(2,1)}, bf16[136,640]{1,0:T(8,128)(2,1)S(1)}, u32[]{:S(2)}, u32[]{:S(2)}) collective-permute-start(bf16[136,640]{1,0:T(8,128)(2,1)} %get-tuple-element.45.refs_0_), channel_id=1, source_target_pairs={{0,8},{4,12},{8,0},{12,4},{16,24},{20,28},{24,16},{28,20},{1,9},{5... | collective-permute-start | bytes 522248 | tf_op jit(solution)/shard_map/ppermute | solution.py:626
  8.5 9.5 %collective-permute-start.1 = (bf16[272,640]{1,0:T(8,128)(2,1)}, bf16[272,640]{1,0:T(8,128)(2,1)S(1)}, u32[]{:S(2)}, u32[]{:S(2)}) collective-permute-start(bf16[272,640]{1,0:T(8,128)(2,1)} %get-tuple-element.48), channel_id=1, source_target_pairs={{0,4},{4,0},{8,12},{12,8},{16,20},{20,16},{24,28},{28,24},{1,5},{5... | collective-permute-start | bytes 1044488 | tf_op jit(solution)/shard_map/ppermute | solution.py:623
  18.0 7.8 %collective-permute-start.4 = (bf16[136,640]{1,0:T(8,128)(2,1)S(1)}, bf16[136,640]{1,0:T(8,128)(2,1)S(1)}, u32[]{:S(2)}, u32[]{:S(2)}) collective-permute-start(bf16[136,640]{1,0:T(8,128)(2,1)S(1)} %collective-permute-done.2.second_ref.refs_2_), channel_id=1, source_target_pairs={{0,8},{4,12},{8,0},{12,4},{16,24},{20,28},{24,16},{28,20},{1,9},{5... | collective-permute-start | bytes 522248 | tf_op jit(solution)/shard_map/ppermute | solution.py:626
  18.5 9.4 %collective-permute-start.5 = (bf16[136,640]{1,0:T(8,128)(2,1)S(1)}, bf16[136,640]{1,0:T(8,128)(2,1)S(1)}, u32[]{:S(2)}, u32[]{:S(2)}) collective-permute-start(bf16[136,640]{1,0:T(8,128)(2,1)S(1)} %copy-done.2), channel_id=1, source_target_pairs={{0,16},{4,20},{8,24},{12,28},{16,0},{20,4},{24,8},{28,12},{1,17},{... | collective-permute-start | bytes 522248 | tf_op jit(solution)/shard_map/ppermute | solution.py:626
  19.4 9.6 %collective-permute-start.3 = (bf16[272,640]{1,0:T(8,128)(2,1)S(1)}, bf16[272,640]{1,0:T(8,128)(2,1)S(1)}, u32[]{:S(2)}, u32[]{:S(2)}) collective-permute-start(bf16[272,640]{1,0:T(8,128)(2,1)S(1)} %pair_up.1), channel_id=1, source_target_pairs={{0,4},{4,0},{8,12},{12,8},{16,20},{20,16},{24,28},{28,24},{1,5},{5... | collective-permute-start | bytes 1044488 | tf_op jit(solution)/shard_map/ppermute | solution.py:623
  21.0 17.4 %collective-permute-start.19 = (bf16[16,128,128]{2,1,0:T(8,128)(2,1)S(1)}, bf16[16,128,128]{2,1,0:T(8,128)(2,1)S(1)}, u32[]{:S(2)}, u32[]{:S(2)}) collective-permute-start(bf16[16,128,128]{2,1,0:T(8,128)(2,1)S(1)} %copy-done), channel_id=1, source_target_pairs={{0,1},{1,0},{2,3},{3,2},{4,5},{5,4},{6,7},{7,6},{8,9},{9,8},{10,11... | collective-permute-start | bytes 1572872 | tf_op jit(solution)/shard_map/ppermute | solution.py:629
  29.0 6.8 %collective-permute-start.6 = (bf16[136,640]{1,0:T(8,128)(2,1)S(1)}, bf16[136,640]{1,0:T(8,128)(2,1)S(1)}, u32[]{:S(2)}, u32[]{:S(2)}) collective-permute-start(bf16[136,640]{1,0:T(8,128)(2,1)S(1)} %copy-done.2), channel_id=1, source_target_pairs={{0,8},{4,12},{8,0},{12,4},{16,24},{20,28},{24,16},{28,20},{1,9},{5... | collective-permute-start | bytes 522248 | tf_op jit(solution)/shard_map/ppermute | solution.py:626
  29.3 8.5 %collective-permute-start.10 = (bf16[136,640]{1,0:T(8,128)(2,1)S(1)}, bf16[136,640]{1,0:T(8,128)(2,1)S(1)}, u32[]{:S(2)}, u32[]{:S(2)}) collective-permute-start(bf16[136,640]{1,0:T(8,128)(2,1)S(1)} %collective-permute-done.5.refs_2_.refs_10_), channel_id=1, source_target_pairs={{0,4},{4,0},{8,12},{12,8},{16,20},{20,16},{24,28},{28,24},{1,5},{5... | collective-permute-start | bytes 522248 | tf_op jit(solution)/shard_map/ppermute | solution.py:623
  30.8 9.2 %collective-permute-start.7 = (bf16[136,640]{1,0:T(8,128)(2,1)S(1)}, bf16[136,640]{1,0:T(8,128)(2,1)S(1)}, u32[]{:S(2)}, u32[]{:S(2)}) collective-permute-start(bf16[136,640]{1,0:T(8,128)(2,1)S(1)} %collective-permute-done.4.refs_3_), channel_id=1, source_target_pairs={{0,4},{4,0},{8,12},{12,8},{16,20},{20,16},{24,28},{28,24},{1,5},{5... | collective-permute-start | bytes 522248 | tf_op jit(solution)/shard_map/ppermute | solution.py:623
  31.4 13.8 %collective-permute-start.8 = (bf16[136,640]{1,0:T(8,128)(2,1)S(1)}, bf16[136,640]{1,0:T(8,128)(2,1)S(1)}, u32[]{:S(2)}, u32[]{:S(2)}) collective-permute-start(bf16[136,640]{1,0:T(8,128)(2,1)S(1)} %collective-permute-done.5.refs_2_.refs_10_), channel_id=1, source_target_pairs={{0,8},{4,12},{8,0},{12,4},{16,24},{20,28},{24,16},{28,20},{1,9},{5... | collective-permute-start | bytes 522248 | tf_op jit(solution)/shard_map/ppermute | solution.py:626
  35.7 10.6 %collective-permute-start.9 = (bf16[136,640]{1,0:T(8,128)(2,1)S(1)}, bf16[136,640]{1,0:T(8,128)(2,1)S(1)}, u32[]{:S(2)}, u32[]{:S(2)}) collective-permute-start(bf16[136,640]{1,0:T(8,128)(2,1)S(1)} %collective-permute-done.6.refs_1_.refs_9_), channel_id=1, source_target_pairs={{0,4},{4,0},{8,12},{12,8},{16,20},{20,16},{24,28},{28,24},{1,5},{5... | collective-permute-start | bytes 522248 | tf_op jit(solution)/shard_map/ppermute | solution.py:623
  37.8 8.5 %collective-permute-start.11 = (bf16[136,640]{1,0:T(8,128)(2,1)S(1)}, bf16[136,640]{1,0:T(8,128)(2,1)S(1)}, u32[]{:S(2)}, u32[]{:S(2)}) collective-permute-start(bf16[136,640]{1,0:T(8,128)(2,1)S(1)} %collective-permute-done.10.refs_6_.refs_14_), channel_id=1, source_target_pairs={{0,8},{4,12},{8,0},{12,4},{16,24},{20,28},{24,16},{28,20},{1,9},{5... | collective-permute-start | bytes 522248 | tf_op jit(solution)/shard_map/ppermute | solution.py:626
  38.5 29.4 %collective-permute-start.20 = (bf16[2,16,128,128]{3,2,1,0:T(8,128)(2,1)S(1)}, bf16[2,16,128,128]{3,2,1,0:T(8,128)(2,1)S(1)}, u32[]{:S(2)}, u32[]{:S(2)}) collective-permute-start(bf16[2,16,128,128]{3,2,1,0:T(8,128)(2,1)S(1)} %pair_cores.1.here_ref), channel_id=1, source_target_pairs={{0,2},{1,3},{2,0},{3,1},{4,6},{5,7},{6,4},{7,5},{8,10},{9,11},{10,... | collective-permute-start | bytes 3145736 | tf_op jit(solution)/shard_map/ppermute | solution.py:629
  43.6 8.1 %collective-permute-start.13 = (bf16[136,512]{1,0:T(8,128)(2,1)S(1)}, bf16[136,512]{1,0:T(8,128)(2,1)S(1)}, u32[]{:S(2)}, u32[]{:S(2)}) collective-permute-start(bf16[136,512]{1,0:T(8,128)(2,1)S(1)} %get-tuple-element.65), channel_id=1, source_target_pairs={{0,4},{4,0},{8,12},{12,8},{16,20},{20,16},{24,28},{28,24},{1,5},{5... | collective-permute-start | bytes 417800 | tf_op jit(solution)/shard_map/ppermute | solution.py:623
  45.1 6.5 %collective-permute-start.14 = (bf16[136,512]{1,0:T(8,128)(2,1)S(1)}, bf16[136,512]{1,0:T(8,128)(2,1)S(1)}, u32[]{:S(2)}, u32[]{:S(2)}) collective-permute-start(bf16[136,512]{1,0:T(8,128)(2,1)S(1)} %get-tuple-element.68), channel_id=1, source_target_pairs={{0,8},{4,12},{8,0},{12,4},{16,24},{20,28},{24,16},{28,20},{1,9},{5... | collective-permute-start | bytes 417800 | tf_op jit(solution)/shard_map/ppermute | solution.py:626
  50.1 6.6 %collective-permute-start.12 = (bf16[136,512]{1,0:T(8,128)(2,1)S(1)}, bf16[136,512]{1,0:T(8,128)(2,1)S(1)}, u32[]{:S(2)}, u32[]{:S(2)}) collective-permute-start(bf16[136,512]{1,0:T(8,128)(2,1)S(1)} %get-tuple-element.62), channel_id=1, source_target_pairs={{0,4},{4,0},{8,12},{12,8},{16,20},{20,16},{24,28},{28,24},{1,5},{5... | collective-permute-start | bytes 417800 | tf_op jit(solution)/shard_map/ppermute | solution.py:623
  51.1 6.2 %collective-permute-start.15 = (bf16[136,512]{1,0:T(8,128)(2,1)S(1)}, bf16[136,512]{1,0:T(8,128)(2,1)S(1)}, u32[]{:S(2)}, u32[]{:S(2)}) collective-permute-start(bf16[136,512]{1,0:T(8,128)(2,1)S(1)} %get-tuple-element.71), channel_id=1, source_target_pairs={{0,8},{4,12},{8,0},{12,4},{16,24},{20,28},{24,16},{28,20},{1,9},{5... | collective-permute-start | bytes 417800 | tf_op jit(solution)/shard_map/ppermute | solution.py:626
  52.0 11.6 %collective-permute-start.21 = (bf16[264,512]{1,0:T(8,128)(2,1)S(1)}, bf16[264,512]{1,0:T(8,128)(2,1)S(1)}, u32[]{:S(2)}, u32[]{:S(2)}) collective-permute-start(bf16[264,512]{1,0:T(8,128)(2,1)S(1)} %get-tuple-element.83), channel_id=1, source_target_pairs={{0,4},{4,0},{8,12},{12,8},{16,20},{20,16},{24,28},{28,24},{1,5},{5... | collective-permute-start | bytes 811016 | tf_op jit(solution)/shard_map/ppermute | solution.py:623
  53.5 10.1 %collective-permute-start.22 = (bf16[264,512]{1,0:T(8,128)(2,1)S(1)}, bf16[264,512]{1,0:T(8,128)(2,1)S(1)}, u32[]{:S(2)}, u32[]{:S(2)}) collective-permute-start(bf16[264,512]{1,0:T(8,128)(2,1)S(1)} %get-tuple-element.84), channel_id=1, source_target_pairs={{0,8},{4,12},{8,0},{12,4},{16,24},{20,28},{24,16},{28,20},{1,9},{5... | collective-permute-start | bytes 811016 | tf_op jit(solution)/shard_map/ppermute | solution.py:626
  57.7 6.8 %collective-permute-start.16 = (bf16[264,512]{1,0:T(8,128)(2,1)S(1)}, bf16[264,512]{1,0:T(8,128)(2,1)S(1)}, u32[]{:S(2)}, u32[]{:S(2)}) collective-permute-start(bf16[264,512]{1,0:T(8,128)(2,1)S(1)} %get-tuple-element.72), channel_id=1, source_target_pairs={{0,4},{4,0},{8,12},{12,8},{16,20},{20,16},{24,28},{28,24},{1,5},{5... | collective-permute-start | bytes 811016 | tf_op jit(solution)/shard_map/ppermute | solution.py:623
  59.1 7.5 %collective-permute-start.17 = (bf16[264,512]{1,0:T(8,128)(2,1)S(1)}, bf16[264,512]{1,0:T(8,128)(2,1)S(1)}, u32[]{:S(2)}, u32[]{:S(2)}) collective-permute-start(bf16[264,512]{1,0:T(8,128)(2,1)S(1)} %get-tuple-element.73), channel_id=1, source_target_pairs={{0,8},{4,12},{8,0},{12,4},{16,24},{20,28},{24,16},{28,20},{1,9},{5... | collective-permute-start | bytes 811016 | tf_op jit(solution)/shard_map/ppermute | solution.py:626
  64.0 7.5 %collective-permute-start.23 = (bf16[136,512]{1,0:T(8,128)(2,1)S(1)}, bf16[136,512]{1,0:T(8,128)(2,1)S(1)}, u32[]{:S(2)}, u32[]{:S(2)}) collective-permute-start(bf16[136,512]{1,0:T(8,128)(2,1)S(1)} %get-tuple-element.87), channel_id=1, source_target_pairs={{0,16},{4,20},{8,24},{12,28},{16,0},{20,4},{24,8},{28,12},{1,17},{... | collective-permute-start | bytes 417800 | tf_op jit(solution)/shard_map/ppermute | solution.py:626
  67.0 7.5 %collective-permute-start.18 = (bf16[136,512]{1,0:T(8,128)(2,1)S(1)}, bf16[136,512]{1,0:T(8,128)(2,1)S(1)}, u32[]{:S(2)}, u32[]{:S(2)}) collective-permute-start(bf16[136,512]{1,0:T(8,128)(2,1)S(1)} %get-tuple-element.77), channel_id=1, source_target_pairs={{0,16},{4,20},{8,24},{12,28},{16,0},{20,4},{24,8},{28,12},{1,17},{... | collective-permute-start | bytes 417800 | tf_op jit(solution)/shard_map/ppermute | solution.py:626
  (11 other events, 113.4 us)
